TPU v7x, 32 devices: a whole 2x2x4 slice. The times are simulated.
32 devices in a mesh: dp: 8 (over y, x, core), mp: 4 (over z).
Axes of the slice: x: 2, y: 2, z: 4, core: 2. Of those that a mesh axis runs over, the one named last changes fastest.
Arguments:
- tokens: bfloat16 [24576, 768], P(('dp', 'mp')), may hold values from -6 to 6
- grad_out: bfloat16 [24576, 768], P(('dp', 'mp')), may hold values from -6 to 6
- pass_len: int32 [24, 4], P('dp'), may hold values from 100 to 200, as said below
- labels: int32 [96], P('dp'), may hold values from 0 to 95, each once
- w_query: bfloat16 [768, 768], P(None, 'mp'), may hold values from -0.21875 to 0.21875
- w_key: bfloat16 [768, 768], P(None, 'mp'), may hold values from -0.21875 to 0.21875
- w_value: bfloat16 [768, 768], P(None, 'mp'), may hold values from -0.21875 to 0.21875
- b_query: float32 [768], P('mp'), may hold values from -1 to 1
- b_value: float32 [768], P('mp'), may hold values from -1 to 1
- w_out: bfloat16 [768, 768], P('mp'), may hold values from -1.5 to 1.5
- b_out: float32 [768], replicated, may hold values from -1 to 1
- ln1_gain: float32 [768], replicated, may hold values from 0.5 to 1.5
- ln1_shift: float32 [768], replicated, may hold values from -1 to 1
- w_in: bfloat16 [768, 3072], P(None, 'mp'), may hold values from -0.21875 to 0.21875
- b_in: float32 [3072], P('mp'), may hold values from -1 to 1
- w_back: bfloat16 [3072, 768], P('mp'), may hold values from -0.15625 to 0.15625
- b_back: float32 [768], replicated, may hold values from -1 to 1
- ln2_gain: float32 [768], replicated, may hold values from 0.5 to 1.5
- ln2_shift: float32 [768], replicated, may hold values from -1 to 1
Outputs:
- mixed: bfloat16 [24576, 768], P(('dp', 'mp'))
- query_losses: float32 [96], P('dp')
- d_tokens: float32 [24576, 768], P(('dp', 'mp'))
- d_w_query: float32 [768, 768], P(None, 'mp')
- d_w_key: float32 [768, 768], P(None, 'mp')
- d_w_value: float32 [768, 768], P(None, 'mp')
- d_b_query: float32 [768], P('mp')
- d_b_value: float32 [768], P('mp')
- d_w_out: float32 [768, 768], P('mp')
- d_b_out: float32 [768], P('mp')
- d_ln1_gain: float32 [768], P('mp')
- d_ln1_shift: float32 [768], P('mp')
- d_w_in: float32 [768, 3072], P(None, 'mp')
- d_b_in: float32 [3072], P('mp')
- d_w_back: float32 [3072, 768], P('mp')
- d_b_back: float32 [768], P('mp')
- d_ln2_gain: float32 [768], P('mp')
- d_ln2_shift: float32 [768], P('mp')
Inputs may be any that keep to these rules, and one draw needn't show every extreme that they name: `pass_len`: each passage length lies in the stated range; the passages of a row follow its 4 queries of 32 tokens and the rest of the row is padding; row 0 holds a passage of exactly 200 tokens.
All inputs are finite; a program needn't handle non-finite values.
Results may differ from a plain program's by a relative error of at most 0.015.
The roundings to bfloat16 on the way count: a program that leaves them out, or rounds other values in their place, can miss the bound.
Values may be sent and summed in bfloat16 or wider, within the bound.
No kernel may reach another device: no remote copies, remote signals or barrier semaphores. Data moves between devices by JAX's collectives and lax.ppermute only.
A program may use at most 128 MiB of HBM per device.

v0:
```python
import math

import jax
import jax.numpy as jnp
from jax import lax
from jax.sharding import PartitionSpec as P

HEAD = 64
ROW_LEN = 1024
PAIRS = 4
QLEN = 32


epsilon = 1e-12
masked_score = -1e30
highest = lax.Precision.HIGHEST


def layer_norm(values, gain, shift):
    center = values - jnp.mean(values, axis=-1, keepdims=True)
    spread = jnp.mean(center * center, axis=-1, keepdims=True)
    return center * lax.rsqrt(spread + epsilon) * gain + shift


def gelu_exact(before):
    return jax.nn.gelu(before, approximate=False)


def row_segments(pass_len):
    query_span = PAIRS * QLEN
    passage_ends = query_span + jnp.cumsum(pass_len, axis=1)
    places = jnp.arange(ROW_LEN, dtype=jnp.int32)
    passed = jnp.sum((places[None, :, None] >= passage_ends[:, None, :]).astype(jnp.int32), axis=2)
    return jnp.where(places[None, :] < query_span, places[None, :] // QLEN, PAIRS + passed)


def cls_places(pass_len):
    passage_ends = PAIRS * QLEN + jnp.cumsum(pass_len, axis=1)
    query_starts = jnp.arange(PAIRS, dtype=jnp.int32) * QLEN
    query_starts = jnp.broadcast_to(query_starts[None, :], pass_len.shape)
    return jnp.concatenate([query_starts, passage_ends - pass_len], axis=1)


def masked_scores(query_row, key_row, segment_row):
    scores = jnp.einsum("qhd,khd->hqk", query_row, key_row, preferred_element_type=jnp.float32)
    same = segment_row[:, None] == segment_row[None, :]
    return jnp.where(same[None, :, :], scores, masked_score)


def attend_forward(parts):
    query_row, key_row, value_row, segment_row = parts
    scores = masked_scores(query_row, key_row, segment_row)
    top = jnp.max(scores, axis=-1, keepdims=True)
    raised = jnp.exp(scores - top)
    total = jnp.sum(raised, axis=-1, keepdims=True)
    weights = (raised / total).astype(jnp.bfloat16)
    context = jnp.einsum("hqk,khd->qhd", weights, value_row, preferred_element_type=jnp.float32)
    return (context.astype(jnp.bfloat16), (top + jnp.log(total))[:, :, 0])


def attend_backward(parts):
    query_row, key_row, value_row, segment_row, log_total, grad_row = parts
    scores = masked_scores(query_row, key_row, segment_row)
    weights = jnp.exp(scores - log_total[:, :, None])
    low_weights = weights.astype(jnp.bfloat16)
    grad_value = jnp.einsum(
        "hqk,qhd->khd", low_weights, grad_row, preferred_element_type=jnp.float32
    )
    grad_weights = jnp.einsum(
        "qhd,khd->hqk", grad_row, value_row, preferred_element_type=jnp.float32
    )
    inner = jnp.sum(weights * grad_weights, axis=-1, keepdims=True)
    grad_scores = (weights * (grad_weights - inner)).astype(jnp.bfloat16)
    grad_query = jnp.einsum(
        "hqk,khd->qhd", grad_scores, key_row, preferred_element_type=jnp.float32
    )
    grad_key = jnp.einsum(
        "hqk,qhd->khd", grad_scores, query_row, preferred_element_type=jnp.float32
    )
    return (
        grad_query.astype(jnp.bfloat16),
        grad_key.astype(jnp.bfloat16),
        grad_value.astype(jnp.bfloat16),
    )


def quarters(stats, model_ways):
    return stats.reshape(stats.shape[0], model_ways, stats.shape[1] // model_ways).transpose(
        1, 0, 2
    )


def shards(
    tokens,
    grad_out,
    pass_len,
    labels,
    w_query,
    w_key,
    w_value,
    b_query,
    b_value,
    w_out,
    b_out,
    ln1_gain,
    ln1_shift,
    w_in,
    b_in,
    w_back,
    b_back,
    ln2_gain,
    ln2_shift,
):
    model_ways = lax.axis_size("mp")
    data_ways = lax.axis_size("dp")
    own_rows = tokens.shape[0]
    width = tokens.shape[1]
    rows_here = pass_len.shape[0]
    group_rows = rows_here * ROW_LEN
    heads_here = w_query.shape[1] // HEAD
    scale = 1.0 / math.sqrt(HEAD)
    temper = 2.0 / math.sqrt(width)
    segment = row_segments(pass_len)
    shape_four = (rows_here, ROW_LEN, heads_here, HEAD)
    full_tokens = lax.all_gather(tokens, "mp", axis=0, tiled=True)
    queries = (
        (jnp.dot(full_tokens, w_query, preferred_element_type=jnp.float32) + b_query) * scale
    ).astype(jnp.bfloat16)
    keys = jnp.dot(full_tokens, w_key, preferred_element_type=jnp.float32).astype(jnp.bfloat16)
    values = (jnp.dot(full_tokens, w_value, preferred_element_type=jnp.float32) + b_value).astype(
        jnp.bfloat16
    )
    queries = queries.reshape(shape_four)
    keys = keys.reshape(shape_four)
    values = values.reshape(shape_four)
    context_rows, log_totals = lax.map(attend_forward, (queries, keys, values, segment))
    context = context_rows.reshape(group_rows, heads_here * HEAD)
    piece = context
    attn_own = lax.psum_scatter(
        jnp.dot(piece, w_out, preferred_element_type=jnp.float32),
        "mp",
        scatter_dimension=0,
        tiled=True,
    )
    first_sum = tokens.astype(jnp.float32) + attn_own + b_out
    hidden = layer_norm(first_sum, ln1_gain, ln1_shift)
    hidden_low = hidden.astype(jnp.bfloat16)
    full_hidden = lax.all_gather(hidden_low, "mp", axis=0, tiled=True)
    active = gelu_exact(
        jnp.dot(full_hidden, w_in, preferred_element_type=jnp.float32) + b_in
    ).astype(jnp.bfloat16)
    piece = active
    ffn_own = lax.psum_scatter(
        jnp.dot(piece, w_back, preferred_element_type=jnp.float32),
        "mp",
        scatter_dimension=0,
        tiled=True,
    )
    second_sum = hidden + ffn_own + b_back
    normed = layer_norm(second_sum, ln2_gain, ln2_shift)
    mixed = normed.astype(jnp.bfloat16)
    query_count = PAIRS * rows_here
    seg_group = 2 * query_count
    places = cls_places(pass_len) + (jnp.arange(rows_here, dtype=jnp.int32) * ROW_LEN)[:, None]
    table_places = jnp.concatenate([places[:, :PAIRS].reshape(-1), places[:, PAIRS:].reshape(-1)])
    table_places = table_places - lax.axis_index("mp") * own_rows
    picker = table_places[:, None] == jnp.arange(own_rows, dtype=jnp.int32)[None, :]
    table = jnp.dot(picker.astype(jnp.bfloat16), mixed, preferred_element_type=jnp.float32).astype(
        jnp.bfloat16
    )
    tables = lax.all_gather(table, ("dp", "mp"), axis=0, tiled=True)
    tables = jnp.sum(
        tables.reshape(data_ways, model_ways, seg_group, width).astype(jnp.float32), axis=1
    )
    data_index = lax.axis_index("dp")
    passage_cls = tables[:, query_count:].reshape(data_ways * query_count, width)
    all_count = data_ways * query_count
    query_cls = lax.dynamic_index_in_dim(tables, data_index, 0, keepdims=False)[:query_count]
    logits = jnp.dot(query_cls, passage_cls.T, precision=highest) * temper
    targets = labels[:, None] == jnp.arange(all_count, dtype=jnp.int32)[None, :]
    top = jnp.max(logits, axis=1, keepdims=True)
    raised = jnp.exp(logits - top)
    total = jnp.sum(raised, axis=1, keepdims=True)
    query_losses = (
        top[:, 0] + jnp.log(total[:, 0]) - jnp.sum(jnp.where(targets, logits, 0.0), axis=1)
    )
    grad_logits = (raised / total - targets.astype(jnp.float32)) * temper
    grad_query_cls = jnp.dot(grad_logits, passage_cls, precision=highest)
    grad_passage_cls = jnp.dot(grad_logits.T, query_cls, precision=highest)
    grad_table = jnp.zeros((data_ways, seg_group, width), jnp.float32)
    grad_table = grad_table.at[:, query_count:].set(
        grad_passage_cls.reshape(data_ways, query_count, width)
    )
    grad_table = lax.dynamic_update_slice(grad_table, grad_query_cls[None], (data_index, 0, 0))
    own_cls_grad = lax.psum_scatter(
        grad_table.reshape(data_ways * seg_group, width), "dp", scatter_dimension=0, tiled=True
    )
    grad_mixed = grad_out.astype(jnp.float32) + jnp.dot(
        picker.astype(jnp.float32).T, own_cls_grad, precision=highest
    )
    unused, norm_two_pull = jax.vjp(layer_norm, second_sum, ln2_gain, ln2_shift)
    grad_second, d_gain_two, d_shift_two = norm_two_pull(grad_mixed)
    stats_two = quarters(
        jnp.stack([d_gain_two, d_shift_two, jnp.sum(grad_second, axis=0)]), model_ways
    )
    full_grad_second = lax.all_gather(grad_second.astype(jnp.bfloat16), "mp", axis=0, tiled=True)
    back_hidden = lax.all_gather(hidden_low, "mp", axis=0, tiled=True)
    before = jnp.dot(back_hidden, w_in, preferred_element_type=jnp.float32) + b_in
    active_again, gelu_pull = jax.vjp(gelu_exact, before)
    active_again = active_again.astype(jnp.bfloat16)
    d_w_back = jnp.einsum(
        "tf,td->fd", active_again, full_grad_second, preferred_element_type=jnp.float32
    )
    grad_active = jnp.einsum(
        "td,fd->tf", full_grad_second, w_back, preferred_element_type=jnp.float32
    )
    (grad_before,) = gelu_pull(grad_active)
    grad_before = grad_before.astype(jnp.bfloat16)
    d_w_in = jnp.einsum("td,tf->df", back_hidden, grad_before, preferred_element_type=jnp.float32)
    d_b_in = jnp.sum(grad_before, axis=0, dtype=jnp.float32)
    hidden_terms = jnp.einsum("tf,df->td", grad_before, w_in, preferred_element_type=jnp.float32)
    hidden_own, stats_two_own = (
        lax.psum_scatter(hidden_terms, "mp", scatter_dimension=0, tiled=True),
        lax.psum_scatter(stats_two, "mp", scatter_dimension=0, tiled=True),
    )
    ffn_parts = (d_w_in, d_b_in, d_w_back, stats_two_own)
    grad_hidden = grad_second + hidden_own
    unused_one, norm_one_pull = jax.vjp(layer_norm, first_sum, ln1_gain, ln1_shift)
    grad_first, d_gain_one, d_shift_one = norm_one_pull(grad_hidden)
    stats_one = quarters(
        jnp.stack([d_gain_one, d_shift_one, jnp.sum(grad_first, axis=0)]), model_ways
    )
    full_grad_first = lax.all_gather(grad_first.astype(jnp.bfloat16), "mp", axis=0, tiled=True)
    d_w_out = jnp.einsum("tc,td->cd", context, full_grad_first, preferred_element_type=jnp.float32)
    grad_context = jnp.einsum(
        "td,cd->tc", full_grad_first, w_out, preferred_element_type=jnp.float32
    ).astype(jnp.bfloat16)
    grad_queries, grad_keys, grad_values = lax.map(
        attend_backward,
        (queries, keys, values, segment, log_totals, grad_context.reshape(shape_four)),
    )
    grad_queries = grad_queries.reshape(group_rows, heads_here * HEAD)
    grad_keys = grad_keys.reshape(group_rows, heads_here * HEAD)
    grad_values = grad_values.reshape(group_rows, heads_here * HEAD)
    d_w_query = (
        jnp.einsum("td,tc->dc", full_tokens, grad_queries, preferred_element_type=jnp.float32)
        * scale
    )
    d_w_key = jnp.einsum("td,tc->dc", full_tokens, grad_keys, preferred_element_type=jnp.float32)
    d_w_value = jnp.einsum(
        "td,tc->dc", full_tokens, grad_values, preferred_element_type=jnp.float32
    )
    d_b_query = jnp.sum(grad_queries, axis=0, dtype=jnp.float32) * scale
    d_b_value = jnp.sum(grad_values, axis=0, dtype=jnp.float32)
    token_terms = (
        jnp.einsum("tc,dc->td", grad_queries, w_query, preferred_element_type=jnp.float32) * scale
    )
    token_terms = token_terms + jnp.einsum(
        "tc,dc->td", grad_keys, w_key, preferred_element_type=jnp.float32
    )
    token_terms = token_terms + jnp.einsum(
        "tc,dc->td", grad_values, w_value, preferred_element_type=jnp.float32
    )
    token_own, stats_one_own = (
        lax.psum_scatter(
            token_terms.astype(jnp.bfloat16), "mp", scatter_dimension=0, tiled=True
        ).astype(jnp.float32),
        lax.psum_scatter(
            stats_one.astype(jnp.bfloat16), "mp", scatter_dimension=0, tiled=True
        ).astype(jnp.float32),
    )
    d_tokens = grad_first + token_own
    attn_parts = (d_w_query, d_w_key, d_w_value, d_b_query, d_b_value, d_w_out, stats_one_own)
    summed = lax.psum(attn_parts + ffn_parts, "dp")
    attn_parts = summed[:7]
    ffn_parts = summed[7:]
    stats_one_sum = attn_parts[6][0]
    stats_two_sum = ffn_parts[3][0]
    return (
        mixed,
        query_losses,
        d_tokens,
        attn_parts[0],
        attn_parts[1],
        attn_parts[2],
        attn_parts[3],
        attn_parts[4],
        attn_parts[5],
        stats_one_sum[2],
        stats_one_sum[0],
        stats_one_sum[1],
        ffn_parts[0],
        ffn_parts[1],
        ffn_parts[2],
        stats_two_sum[2],
        stats_two_sum[0],
        stats_two_sum[1],
    )


def solution(mesh):
    return jax.shard_map(
        shards,
        mesh=mesh,
        in_specs=(
            P(("dp", "mp"), None),
            P(("dp", "mp"), None),
            P("dp", None),
            P("dp"),
            P(None, "mp"),
            P(None, "mp"),
            P(None, "mp"),
            P("mp"),
            P("mp"),
            P("mp", None),
            P(),
            P(),
            P(),
            P(None, "mp"),
            P("mp"),
            P("mp", None),
            P(),
            P(),
            P(),
        ),
        out_specs=(
            P(("dp", "mp"), None),
            P("dp"),
            P(("dp", "mp"), None),
            P(None, "mp"),
            P(None, "mp"),
            P(None, "mp"),
            P("mp"),
            P("mp"),
            P("mp", None),
            P("mp"),
            P("mp"),
            P("mp"),
            P(None, "mp"),
            P("mp"),
            P("mp", None),
            P("mp"),
            P("mp"),
            P("mp"),
        ),
        check_vma=False,
    )
```

profile of v0, /device:TPU:1, one launch (start us, length us, event | category | flops | bytes accessed | tf_op | source)
XLA Modules:
  0.0 1479.8 jit_solution(16429647247187790098)
XLA Ops:
  10.2 91.0 %all-gather.6.cloned.1.call-done = bf16[3072,768]{1,0:T(8,128)(2,1)} async-done(((bf16[768,768]{1,0:T(8,128)(2,1)}), bf16[3072,768]{1,0:T(8,128)(2,1)}) %all-gather.6.cloned.1.call-update) | async-done | bytes 4718608 | tf_op jit(solution)/shard_map/all_gather | solution.py:125
  132.1 71.4 %while.27 = (s32[]{:T(128)}, bf16[3,1024,3,64]{1,3,2,0:T(8,128)(2,1)}, f32[3,3,1024]{2,1,0:T(4,128)}, bf16[3,1024,3,64]{1,3,2,0:T(8,128)(2,1)}, s32[3,1024]{1,0:...) while((s32[]{:T(128)}, ...), condition=%wide.region_5.6_spmd, body=%wide.region_2.5_spmd.sunk | while | flops 834860032 | bytes 43632740 | solution.py:136
  146.5 8.9 fusion.167
  170.3 8.9 fusion.167
  194.1 8.9 fusion.167
  213.7 159.2 %reduce-scatter.7.cloned.1.call-done = f32[768,768]{1,0:T(8,128)} async-done(((f32[3072,768]{1,0:T(8,128)}), f32[768,768]{1,0:T(8,128)}) %reduce-scatter.7.cloned.1.call-update) | async-done | bytes 2359312 | tf_op jit(solution)/shard_map/reduce_scatter | solution.py:139
  378.4 90.8 %all-gather.8.cloned.1.call-done = bf16[3072,768]{1,0:T(8,128)(2,1)} async-done(((bf16[768,768]{1,0:T(8,128)(2,1)}), bf16[3072,768]{1,0:T(8,128)(2,1)}) %all-gather.8.cloned.1.call-update) | async-done | bytes 4718608 | tf_op jit(solution)/shard_map/all_gather | solution.py:148
  469.2 26.2 %multiply_convert_fusion.1 = (bf16[3072,768]{1,0:T(8,128)(2,1)S(1)}, f32[3072,768]{1,0:T(8,128)}, f32[3072,768]{1,0:T(8,128)}) fusion(f32[768]{0:T(1024)} %param.39, bf16[3072,768]{1,0:T(8,128)(2,1)} %all-gather.8.cloned.1.call-done, bf16[768,768]{1,0:T(8,128)(2,1)S(1)} %copy-done), kind=kOutput, calls=%fused_computation.66 | convolution fusion | flops 3779592192 | bytes 29494272 | tf_op jit(solution)/shard_map/dot_general | solution.py:150
  509.2 154.1 %reduce-scatter.9.cloned.1.call-done = f32[768,768]{1,0:T(8,128)} async-done(((f32[3072,768]{1,0:T(8,128)}), f32[768,768]{1,0:T(8,128)}) %reduce-scatter.9.cloned.1.call-update) | async-done | bytes 2359312 | tf_op jit(solution)/shard_map/reduce_scatter | solution.py:153
  669.4 55.9 %all-gather.10.cloned.1.call-done = bf16[768,768]{1,0:T(8,128)(2,1)} async-done(((bf16[24,768]{1,0:T(8,128)(2,1)}), bf16[768,768]{1,0:T(8,128)(2,1)}) %all-gather.10.cloned.1.call-update) | async-done | bytes 1179664 | tf_op jit(solution)/shard_map/all_gather | solution.py:171
  741.7 32.1 %reduce-scatter.11.cloned.1.call-done = f32[24,768]{1,0:T(8,128)} async-done(((f32[192,768]{1,0:T(8,128)}), f32[24,768]{1,0:T(8,128)}) %reduce-scatter.11.cloned.1.call-update) | async-done | bytes 73744 | tf_op jit(solution)/shard_map/reduce_scatter | solution.py:195
  783.0 90.1 %all-gather.12.cloned.1.call-done = bf16[3072,768]{1,0:T(8,128)(2,1)} async-done(((bf16[768,768]{1,0:T(8,128)(2,1)}), bf16[3072,768]{1,0:T(8,128)(2,1)}) %all-gather.12.cloned.1.call-update) | async-done | bytes 4718608 | tf_op jit(solution)/shard_map/all_gather | solution.py:206
  873.1 13.5 convert_reduce_fusion
  895.3 159.3 %reduce-scatter.13.cloned.1.call-done = f32[768,768]{1,0:T(8,128)} async-done(((f32[3072,768]{1,0:T(8,128)}), f32[768,768]{1,0:T(8,128)}) %reduce-scatter.13.cloned.1.call-update) | async-done | bytes 2359312 | tf_op jit(solution)/shard_map/reduce_scatter | solution.py:223
  1062.7 90.7 %all-gather.14.cloned.1.call-done = bf16[3072,768]{1,0:T(8,128)(2,1)} async-done(((bf16[768,768]{1,0:T(8,128)(2,1)}), bf16[3072,768]{1,0:T(8,128)(2,1)}) %all-gather.14.cloned.1.call-update) | async-done | bytes 4718608 | tf_op jit(solution)/shard_map/all_gather | solution.py:233
  1164.2 80.8 %while.28 = (s32[]{:T(128)}, bf16[3,1024,3,64]{1,3,2,0:T(8,128)(2,1)}, bf16[3,1024,3,64]{1,3,2,0:T(8,128)(2,1)}, bf16[3,1024,3,64]{1,3,2,0:T(8,128)(2,1)}, bf16[...) while((s32[]{:T(128)}, ...), condition=%wide.region_24.25_spmd, body=%wide.region_22.24_spmd.sunk | while | flops 2052649984 | bytes 107328664 | solution.py:238
  1171.6 7.8 multiply_reduce_fusion.8
  1225.3 7.8 multiply_reduce_fusion.8
  1259.2 9.2 fusion.107
  1268.5 9.2 fusion.106
  1290.9 14.7 all-reduce.2
  1310.5 12.0 all-reduce.1
  1325.8 22.8 %all-reduce.3 = (f32[192]{0:T(256)}, f32[192]{0:T(256)}, f32[1,3,192]{2,1,0:T(4,128)S(1)}, f32[768]{0:T(1024)}, f32[1,3,192]{2,0,1:T(1,128)S(1)}) all-reduce(f32[192]{0:T(256)S(1)} %mul.260, f32[192]{0:T(256)S(1)} %reduce_sum.231, f32[1,3,192]{2,1,0:T(4,128)S(1)} %dynamic-slice_convert_fusion, ...), channel_id=1, replica_groups=mesh['dp'=8,'mp'=4] {'dp'}, use_global_device_ids=true, to_apply=%region_30.31 | all-reduce | flops 2304 | bytes 18432 | tf_op jit(solution)/shard_map/psum | solution.py:274
  1352.7 110.6 %all-reduce.7.cloned.1.call-done = (f32[768,192]{0,1:T(8,128)}, f32[768,192]{0,1:T(8,128)}, f32[768,192]{0,1:T(8,128)}, f32[192,768]{1,0:T(8,128)}, f32[768,768]{1,0:T(8,128)}, /*index=5*/f32[768,768]{1,0:T(8,128)}) async-done(((f32[768,192]{0,1:T(8,128)}, f32[768,192]{0,1:T(8,128)}, f32[768,192]{0,1:T(8,128)}, f32[192,768]{1,0:T(8,128)}, f32[768,768]{1,0:T(8,128)}, /*index=5*/f32[768,768]{1,0:T(8,128)}), ...) | async-done | bytes 7077904 | tf_op jit(solution)/shard_map/psum | solution.py:274
  (313 shorter events, 280.7 us)
Async XLA Ops:
  7.2 462.1 %copy-start = (bf16[768,768]{1,0:T(8,128)(2,1)S(1)}, bf16[768,768]{1,0:T(8,128)(2,1)}, u32[]{:S(2)}) copy-start(bf16[768,768]{1,0:T(8,128)(2,1)} %param.38) | copy-start | bytes 3538948
  7.2 94.0 %all-gather.6.cloned.1.call-start = ((), (), s32[]{:S(2)}) async-start(), calls=%async_computation.5 | async-start | bytes 5898240 | tf_op jit(solution)/shard_map/all_gather | solution.py:125
  7.9 364.9 %reduce-scatter.7.cloned.1.call-start = ((), (), s32[]{:S(2)}) async-start(), calls=%async_computation.6 | async-start | bytes 11796480 | tf_op jit(solution)/shard_map/reduce_scatter | solution.py:139
  213.4 255.8 %all-gather.8.cloned.1.call-start = ((), (), s32[]{:S(2)}) async-start(), calls=%async_computation.7 | async-start | bytes 5898240 | tf_op jit(solution)/shard_map/all_gather | solution.py:148
  378.4 285.0 %reduce-scatter.9.cloned.1.call-start = ((), (), s32[]{:S(2)}) async-start(), calls=%async_computation.8 | async-start | bytes 11796480 | tf_op jit(solution)/shard_map/reduce_scatter | solution.py:153
  469.2 28.4 %copy-start.59 = (bf16[768,768]{1,0:T(8,128)(2,1)S(1)}, bf16[768,768]{1,0:T(8,128)(2,1)}, u32[]{:S(2)}) copy-start(bf16[768,768]{1,0:T(8,128)(2,1)} %param.40) | copy-start | bytes 3538948
  503.9 221.4 %all-gather.10.cloned.1.call-start = ((), (), s32[]{:S(2)}) async-start(), calls=%async_computation.9 | async-start | bytes 1216512 | tf_op jit(solution)/shard_map/all_gather | solution.py:171
  669.4 104.5 %reduce-scatter.11.cloned.1.call-start = ((), (), s32[]{:S(2)}) async-start(), calls=%async_computation.10 | async-start | bytes 663552 | tf_op jit(solution)/shard_map/reduce_scatter | solution.py:195
  741.3 131.8 %all-gather.12.cloned.1.call-start = ((), (), s32[]{:S(2)}) async-start(), calls=%async_computation.11 | async-start | bytes 5898240 | tf_op jit(solution)/shard_map/all_gather | solution.py:206
  782.9 271.7 %reduce-scatter.13.cloned.1.call-start = ((), (), s32[]{:S(2)}) async-start(), calls=%async_computation.12 | async-start | bytes 11796480 | tf_op jit(solution)/shard_map/reduce_scatter | solution.py:223
  895.2 159.4 %copy-start.32 = (f32[768]{0:T(1024)S(1)}, f32[768]{0:T(1024)}, u32[]{:S(2)}) copy-start(f32[768]{0:T(1024)} %copy-done.31) | copy-start | bytes 9220
  895.2 159.4 %copy-start.34 = (f32[768]{0:T(1024)S(1)}, f32[768]{0:T(1024)}, u32[]{:S(2)}) copy-start(f32[768]{0:T(1024)} %copy-done.33) | copy-start | bytes 9220
  895.2 159.4 %copy-start.38 = (f32[768]{0:T(1024)S(1)}, f32[768]{0:T(1024)}, u32[]{:S(2)}) copy-start(f32[768]{0:T(1024)} %param.36) | copy-start | bytes 9220
  895.2 159.4 %copy-start.44 = (f32[768]{0:T(1024)S(1)}, f32[768]{0:T(1024)}, u32[]{:S(2)}) copy-start(f32[768]{0:T(1024)} %copy-done.43) | copy-start | bytes 9220
  895.3 163.0 %copy-start.46 = (f32[768]{0:T(1024)S(1)}, f32[768]{0:T(1024)}, u32[]{:S(2)}) copy-start(f32[768]{0:T(1024)} %copy-done.45) | copy-start | bytes 9220
  895.3 258.1 %all-gather.14.cloned.1.call-start = ((), (), s32[]{:S(2)}) async-start(), calls=%async_computation.13 | async-start | bytes 5898240 | tf_op jit(solution)/shard_map/all_gather | solution.py:233
  1060.6 92.8 %copy-start.26 = (bf16[192,768]{1,0:T(8,128)(2,1)S(1)}, bf16[192,768]{1,0:T(8,128)(2,1)}, u32[]{:S(2)}) copy-start(bf16[192,768]{1,0:T(8,128)(2,1)} %param.34) | copy-start | bytes 884740
  1062.5 287.2 %reduce-scatter.15.cloned.1.call-start = ((), (), s32[]{:S(2)}) async-start(), calls=%async_computation.14 | async-start | bytes 5898240 | tf_op jit(solution)/shard_map/reduce_scatter | solution.py:265
  1258.9 204.4 %all-reduce.7.cloned.1.call-start = ((), (), s32[]{:S(2)}) async-start(), calls=%async_computation.15 | async-start | bytes 14155776 | tf_op jit(solution)/shard_map/psum | solution.py:274
  1259.2 18.5 %slice-start.2 = ((s8[4718592]{0:T(1024)(128)(4,1)}), s8[4194304]{0:T(1024)(128)(4,1)S(1)}, s32[]{:S(2)}) async-start(s8[4718592]{0:T(1024)(128)(4,1)} %bitcast.225), calls=%async_computation.18 | async-start | bytes 8388608
  1259.2 20.4 %slice-start = ((s8[4718592]{0:T(1024)(128)(4,1)}), s8[4194304]{0:T(1024)(128)(4,1)S(1)}, s32[]{:S(2)}) async-start(s8[4718592]{0:T(1024)(128)(4,1)} %bitcast.211), calls=%async_computation.16 | async-start | bytes 8388608
  1285.5 38.4 %copy-start.16 = (bf16[3,1024,3,64]{1,3,2,0:T(8,128)(2,1)S(1)}, bf16[3,1024,3,64]{1,3,2,0:T(8,128)(2,1)}, u32[]{:S(2)}) copy-start(bf16[3,1024,3,64]{1,3,2,0:T(8,128)(2,1)} %get-tuple-element.126) | copy-start | bytes 3538948
  1285.5 64.2 %copy-start.9 = (f32[768,768]{1,0:T(8,128)S(1)}, f32[768,768]{1,0:T(8,128)}, u32[]{:S(2)}) copy-start(f32[768,768]{1,0:T(8,128)} %copy-done.8) | copy-start | bytes 7077892
  1285.5 64.2 %copy-start.50 = (f32[768]{0:T(1024)S(1)}, f32[768]{0:T(1024)}, u32[]{:S(2)}) copy-start(f32[768]{0:T(1024)} %copy-done.49) | copy-start | bytes 9220
  (57 other events, 167.7 us)
Sparse Core Ops, SparseCore 0:
  9.6 91.5 all-gather.5
  213.6 159.2 reduce-scatter.6
  378.5 90.7 all-gather.7
  504.0 159.2 reduce-scatter.8
  669.5 55.7 all-gather.9
  741.4 32.3 reduce-scatter.10
  783.1 89.9 all-gather.11
  895.4 159.2 reduce-scatter.12
  1062.6 90.7 all-gather.13
  1259.0 84.7 reduce-scatter.14
  1349.0 114.2 all-reduce.6
where the time goes:
time: 1490 us; the launch traced here: 1480 us
  waiting for transfers between devices  1030 us (69%)
  matrix products  221 us (15%)
  other arithmetic  81.2 us (5%)
  local copies, waits for them, and re-layouts  76.4 us (5%)
  blocking collectives  49.5 us (3%)
  between operations  15.1 us (1%)
    reduce_scatter x1, waiting for transfers between devices, shards(): lax.psum_scatter(hidden_terms, 'mp', scatter_dimension=0, tiled=True)  159 us
    reduce_scatter x1, waiting for transfers between devices, shards(): lax.psum_scatter(jnp.dot(piece, w_out, preferred_element_type=jnp.float32...  159 us
    reduce_scatter x1, waiting for transfers between devices, shards(): lax.psum_scatter(jnp.dot(piece, w_back, preferred_element_type=jnp.float3...  154 us
    psum x1, waiting for transfers between devices, shards(): summed = lax.psum(attn_parts + ffn_parts, 'dp')  111 us
    all_gather x1, waiting for transfers between devices, shards(): full_tokens = lax.all_gather(tokens, 'mp', axis=0, tiled=True)  91 us
    all_gather x1, waiting for transfers between devices, shards(): full_hidden = lax.all_gather(hidden_low, 'mp', axis=0, tiled=True)  90.8 us
    all_gather x1, waiting for transfers between devices, shards(): lax.all_gather(grad_first.astype(jnp.bfloat16), 'mp', axis=0, tiled=True)  90.7 us
    all_gather x1, waiting for transfers between devices, shards(): lax.all_gather(grad_second.astype(jnp.bfloat16), 'mp', axis=0, tiled=True)  90.1 us
  transfers between devices with their start and end apart: 11, of which 10 were waited for; matrix products, arithmetic and copies ran while one was open for 3% of the time, Pallas kernels for 0%

commit v1 on v0

v1 whole, which is shorter than its diff:
```python
import functools
import math

import jax
import jax.numpy as jnp
from jax import lax
from jax.experimental import pallas as pl
from jax.experimental.pallas import tpu as pltpu
from jax.sharding import PartitionSpec as P

HEAD = 64
ROW_LEN = 1024
PAIRS = 4
QLEN = 32
TILE = 128
ALIGN = 32
BLOCKS = (2, 3, 4, 5, 7, 10)

epsilon = 1e-12
masked_score = -1e30
highest = lax.Precision.HIGHEST
f32 = jnp.float32
bf16 = jnp.bfloat16
NT = (((1,), (1,)), ((), ()))
TN = (((0,), (0,)), ((), ()))
NN = (((1,), (0,)), ((), ()))


def mm(a, b, dims=NN):
    return lax.dot_general(a, b, dims, preferred_element_type=f32)


def segment_bounds(pass_len, start, count):
    rows = pass_len.shape[0]
    lens = [pass_len[:, j] for j in range(PAIRS)]
    cuts = [jnp.full((rows,), j * QLEN, jnp.int32) for j in range(PAIRS + 1)]
    for j in range(PAIRS):
        cuts.append(cuts[-1] + lens[j])
    cuts = jnp.stack(cuts, axis=1) + (jnp.arange(rows, dtype=jnp.int32) * ROW_LEN)[:, None]
    cuts = cuts.reshape(-1)
    place = start + jnp.arange(count, dtype=jnp.int32)
    below = cuts[None, :] <= place[:, None]
    low = jnp.max(jnp.where(below, cuts[None, :], start), axis=1)
    high = jnp.min(jnp.where(below, rows * ROW_LEN, cuts[None, :]), axis=1)
    outside = place >= rows * ROW_LEN
    low = jnp.where(outside, rows * ROW_LEN, low)
    high = jnp.where(outside, start + count, high)
    return jnp.clip(low - start, 0, count), jnp.clip(high - start, 0, count)


def cls_places(pass_len):
    lens = [pass_len[:, j] for j in range(PAIRS)]
    starts = [jnp.full_like(lens[0], j * QLEN) for j in range(PAIRS)]
    at = jnp.full_like(lens[0], PAIRS * QLEN)
    for j in range(PAIRS):
        starts.append(at)
        at = at + lens[j]
    return jnp.stack(starts, axis=1)


def by_span(blocks, count, act):
    least = 0
    for size in BLOCKS:
        if size * TILE > count:
            break

        @pl.when((blocks > least) & (blocks <= size))
        def _(size=size):
            act(size * TILE)

        least = size


def split_pair(block):
    lane = lax.broadcasted_iota(jnp.int32, block.shape, 1)
    even = lane < HEAD
    zero = jnp.zeros_like(block)
    return jnp.concatenate([jnp.where(even, block, zero), jnp.where(even, zero, block)], axis=0)


def join_pair(both):
    rows = both.shape[0] // 2
    lane = lax.broadcasted_iota(jnp.int32, (rows, both.shape[1]), 1)
    return jnp.where(lane < HEAD, both[:rows], both[rows:])


def write_bias(bias_ref, lo_ref, hi_ref, row, first, span):
    place = lax.broadcasted_iota(jnp.int32, (TILE, span), 1) + first
    low = lo_ref[pl.ds(row, TILE), :]
    high = hi_ref[pl.ds(row, TILE), :]
    bias_ref[:, :span] = jnp.where((place >= low) & (place < high), 0.0, masked_score)


def pair_weights(q2, k, bias):
    span = k.shape[0]
    scores = mm(q2, k, NT)
    scores = (scores.reshape(2, TILE, span) + bias[None]).reshape(2 * TILE, span)
    top = jnp.max(scores, axis=1, keepdims=True)
    raised = jnp.exp(scores - top)
    total = jnp.sum(raised, axis=1, keepdims=True)
    return raised * (1.0 / total)


def forward_kernel(halo, tiles_ref, lo_ref, hi_ref, q_ref, k_ref, v_ref, out_ref, bias_ref):
    count = k_ref.shape[0]
    pairs = q_ref.shape[1] // TILE
    tiles = q_ref.shape[0] // TILE

    def tile_step(tile, carry):
        here = tile + halo // TILE
        blocks = tiles_ref[1, here]

        def act(span):
            first = jnp.minimum(tiles_ref[0, here], count - span)
            first = pl.multiple_of(first, ALIGN)
            row = pl.multiple_of(tile * TILE, TILE)
            write_bias(bias_ref, lo_ref, hi_ref, pl.multiple_of(row + halo, TILE), first, span)

            def pair_step(pair, inner):
                lanes = pl.ds(pl.multiple_of(pair * TILE, TILE), TILE)
                q2 = split_pair(q_ref[pl.ds(row, TILE), lanes])
                k = k_ref[pl.ds(first, span), lanes]
                v = v_ref[pl.ds(first, span), lanes]
                weights = pair_weights(q2, k, bias_ref[:, :span]).astype(bf16)
                out_ref[pl.ds(row, TILE), lanes] = join_pair(mm(weights, v)).astype(bf16)
                return inner

            lax.fori_loop(0, pairs, pair_step, 0, unroll=2)

        by_span(blocks, count, act)
        return carry

    lax.fori_loop(0, tiles, tile_step, 0)


def attend_forward(bounds, queries, keys, values, halo):
    tiles, low, high = bounds
    vmem = pl.BlockSpec(memory_space=pltpu.VMEM)
    return pl.pallas_call(
        functools.partial(forward_kernel, halo),
        out_shape=jax.ShapeDtypeStruct(queries.shape, bf16),
        in_specs=[pl.BlockSpec(memory_space=pltpu.SMEM)] + [vmem] * 5,
        out_specs=vmem,
        scratch_shapes=[pltpu.VMEM((TILE, keys.shape[0]), f32)],
        compiler_params=pltpu.CompilerParams(vmem_limit_bytes=32 * 2**20),
        name="attend_forward",
    )(tiles, low, high, queries, keys, values)


def backward_kernel(
    halo, tiles_ref, lo_ref, hi_ref, q_ref, k_ref, v_ref, g_ref,
    dq_ref, dk_ref, dv_ref, bias_ref, dk_sum, dv_sum,
):
    count = k_ref.shape[0]
    own = dq_ref.shape[0]
    pairs = q_ref.shape[1] // TILE
    dk_sum[...] = jnp.zeros_like(dk_sum)
    dv_sum[...] = jnp.zeros_like(dv_sum)

    def tile_step(tile, carry):
        blocks = tiles_ref[2, tile]
        mine = (tile >= halo // TILE) & (tile < (halo + own) // TILE)

        def act(span):
            first = jnp.minimum(tiles_ref[0, tile], count - span)
            first = pl.multiple_of(first, ALIGN)
            row = pl.multiple_of(tile * TILE, TILE)
            write_bias(bias_ref, lo_ref, hi_ref, row, first, span)

            def pair_step(pair, inner):
                lanes = pl.ds(pl.multiple_of(pair * TILE, TILE), TILE)
                q2 = split_pair(q_ref[pl.ds(row, TILE), lanes])
                g2 = split_pair(g_ref[pl.ds(row, TILE), lanes])
                k = k_ref[pl.ds(first, span), lanes]
                v = v_ref[pl.ds(first, span), lanes]
                weights = pair_weights(q2, k, bias_ref[:, :span])
                slopes = mm(g2, v, NT)
                inner_sum = jnp.sum(weights * slopes, axis=1, keepdims=True)
                scores = (weights * (slopes - inner_sum)).astype(bf16)
                dv_sum[pl.ds(first, span), lanes] += mm(weights.astype(bf16), g2, TN)
                dk_sum[pl.ds(first, span), lanes] += mm(scores, q2, TN)

                @pl.when(mine)
                def _():
                    grad = join_pair(mm(scores, k)).astype(bf16)
                    to = pl.multiple_of(row - halo, TILE)
                    dq_ref[pl.ds(to, TILE), lanes] = grad * jnp.asarray(1.0 / math.sqrt(HEAD), bf16)

                return inner

            lax.fori_loop(0, pairs, pair_step, 0)

        by_span(blocks, count, act)
        return carry

    lax.fori_loop(0, count // TILE, tile_step, 0)
    dk_ref[...] = dk_sum[pl.ds(halo, own), :].astype(bf16)
    dv_ref[...] = dv_sum[pl.ds(halo, own), :].astype(bf16)


def attend_backward(bounds, queries, keys, values, grads, halo):
    tiles, low, high = bounds
    count, width = keys.shape
    vmem = pl.BlockSpec(memory_space=pltpu.VMEM)
    out = jax.ShapeDtypeStruct((count - 2 * halo, width), bf16)
    return pl.pallas_call(
        functools.partial(backward_kernel, halo),
        out_shape=(out, out, out),
        in_specs=[pl.BlockSpec(memory_space=pltpu.SMEM)] + [vmem] * 6,
        out_specs=(vmem, vmem, vmem),
        scratch_shapes=[
            pltpu.VMEM((TILE, count), f32),
            pltpu.VMEM((count, width), f32),
            pltpu.VMEM((count, width), f32),
        ],
        compiler_params=pltpu.CompilerParams(vmem_limit_bytes=44 * 2**20),
        name="attend_backward",
    )(tiles, low, high, queries, keys, values, grads)


def norm_parts(values):
    center = values - jnp.mean(values, axis=-1, keepdims=True)
    spread = jnp.mean(center * center, axis=-1, keepdims=True)
    return center, lax.rsqrt(spread + epsilon)


def norm_pull(grad, unit, inverse, gain):
    scaled = grad * gain
    mean = jnp.mean(scaled, axis=-1, keepdims=True)
    along = jnp.mean(scaled * unit, axis=-1, keepdims=True)
    return inverse * (scaled - mean - unit * along)


def gelu_both(before):
    half = 0.5 * (1.0 + lax.erf(before * math.sqrt(0.5)))
    bell = jnp.exp(-0.5 * before * before) * (1.0 / math.sqrt(2.0 * math.pi))
    return before * half, half + before * bell


def turn(ways, step):
    return [(i, (i - step) % ways) for i in range(ways)]


def halo_rows(values, halo):
    ways = lax.axis_size("mp")
    before = lax.ppermute(values[-halo:], "mp", [(i, i + 1) for i in range(ways - 1)])
    after = lax.ppermute(values[:halo], "mp", [(i + 1, i) for i in range(ways - 1)])
    return jnp.concatenate([before, values, after], axis=0)


def ring_stack(values):
    ways = lax.axis_size("mp")
    held = [values] + [lax.ppermute(values, "mp", turn(ways, step)) for step in range(1, ways)]
    return jnp.roll(jnp.stack(held), lax.axis_index("mp"), axis=0)


def group_tables(table):
    ways = lax.axis_size("mp")
    data_ways = lax.axis_size("dp")
    total = table
    for step in range(1, ways):
        total = total + lax.ppermute(table, "mp", turn(ways, step))
    held = total[None]
    data_index = lax.axis_index("dp")
    level = 1
    while level < data_ways:
        other = lax.ppermute(held, "dp", [(i, i ^ level) for i in range(data_ways)])
        first = (data_index & level) == 0
        held = jnp.where(
            first, jnp.concatenate([held, other]), jnp.concatenate([other, held])
        )
        level *= 2
    return held


def gather_rows(shard):
    data_ways = lax.axis_size("dp")
    ways = lax.axis_size("mp")
    rows = shard.shape[0] // data_ways
    own = lax.dynamic_slice_in_dim(shard, lax.axis_index("dp") * rows, rows, 0)
    full = lax.all_gather(own, ("dp", "mp"), axis=0, tiled=True)
    return full.reshape(data_ways, ways, rows, shard.shape[1])


def reduce_rows(grads):
    data_ways, ways, rows, width = grads.shape
    own = lax.psum_scatter(
        grads.reshape(data_ways * ways * rows, width), ("dp", "mp"), scatter_dimension=0, tiled=True
    )
    return lax.all_gather(own, "dp", axis=0, tiled=True)


def shards(
    tokens, grad_out, pass_len, labels, w_query, w_key, w_value, b_query, b_value, w_out, b_out,
    ln1_gain, ln1_shift, w_in, b_in, w_back, b_back, ln2_gain, ln2_shift,
):
    ways = lax.axis_size("mp")
    data_ways = lax.axis_size("dp")
    mp_index = lax.axis_index("mp")
    data_index = lax.axis_index("dp")
    own_rows, width = tokens.shape
    rows_here = pass_len.shape[0]
    inner = w_query.shape[1]
    units = w_in.shape[1]
    halo = ROW_LEN // 4
    count = own_rows + 2 * halo
    scale = 1.0 / math.sqrt(HEAD)
    temper = 2.0 / math.sqrt(width)

    attn_shard = jnp.concatenate([w_query.T, w_key.T, w_value.T, w_out], axis=0)
    attn_all = gather_rows(attn_shard)
    in_all = gather_rows(w_in.T).reshape(ways * units, width)
    back_all = gather_rows(w_back).reshape(ways * units, width)
    attn_all = attn_all.transpose(1, 0, 2, 3).reshape(ways, 4, inner, width)
    attn_all = attn_all.transpose(1, 0, 2, 3).reshape(4, ways * inner, width)
    biases = ring_stack(jnp.concatenate([b_query, b_value, b_in]))
    bias_query = biases[:, :inner].reshape(-1)
    bias_value = biases[:, inner : 2 * inner].reshape(-1)
    bias_in = biases[:, 2 * inner :].reshape(ways, data_ways, units // data_ways)
    bias_in = bias_in.transpose(1, 0, 2).reshape(-1)

    low, high = segment_bounds(pass_len, mp_index * own_rows - halo, count)
    tile_low = low[::TILE] // ALIGN * ALIGN
    tile_high = high[TILE - 1 :: TILE]
    blocks = (tile_high - tile_low + TILE - 1) // TILE
    tile = jnp.arange(count // TILE, dtype=jnp.int32)
    before_own = tile < halo // TILE
    after_own = tile >= (halo + own_rows) // TILE
    reach = (~before_own | (tile_high > halo)) & (~after_own | (low[::TILE] < halo + own_rows))
    tiles = jnp.stack([tile_low, blocks, jnp.where(reach, blocks, 0)])
    bounds = (tiles, low[:, None], high[:, None])

    window = halo_rows(tokens, halo)
    queries = ((mm(window, attn_all[0], NT) + bias_query) * scale).astype(bf16)
    keys = mm(window, attn_all[1], NT).astype(bf16)
    values = (mm(window, attn_all[2], NT) + bias_value).astype(bf16)
    context = attend_forward(bounds, queries[halo : halo + own_rows], keys, values, halo)
    first_sum = tokens.astype(f32) + mm(context, attn_all[3]) + b_out
    center_one, inverse_one = norm_parts(first_sum)
    unit_one = center_one * inverse_one
    hidden = unit_one * ln1_gain + ln1_shift
    hidden_low = hidden.astype(bf16)

    active, slope = gelu_both(mm(hidden_low, in_all, NT) + bias_in)
    active = active.astype(bf16)
    slope = slope.astype(bf16)
    second_sum = hidden + mm(active, back_all) + b_back
    center_two, inverse_two = norm_parts(second_sum)
    unit_two = center_two * inverse_two
    mixed = (unit_two * ln2_gain + ln2_shift).astype(bf16)

    query_count = PAIRS * rows_here
    places = cls_places(pass_len) + (jnp.arange(rows_here, dtype=jnp.int32) * ROW_LEN)[:, None]
    table_places = jnp.concatenate([places[:, :PAIRS].reshape(-1), places[:, PAIRS:].reshape(-1)])
    table_places = table_places - mp_index * own_rows
    picker = table_places[:, None] == jnp.arange(own_rows, dtype=jnp.int32)[None, :]
    table = mm(picker.astype(bf16), mixed).astype(bf16)
    digits = jnp.concatenate([labels // 32, labels % 32]).astype(bf16)
    digits = jnp.where(mp_index == 0, digits, 0)
    extra = jnp.zeros((8, width), bf16).at[0, : 2 * query_count].set(digits)
    tables = group_tables(jnp.concatenate([table, extra]))
    all_count = data_ways * query_count
    query_cls = tables[:, :query_count].reshape(all_count, width)
    passage_cls = tables[:, query_count : 2 * query_count].reshape(all_count, width)
    digits = tables[:, 2 * query_count, : 2 * query_count].astype(jnp.int32)
    all_labels = (digits[:, :query_count] * 32 + digits[:, query_count:]).reshape(-1)

    logits = mm(query_cls, passage_cls, NT) * temper
    targets = all_labels[:, None] == jnp.arange(all_count, dtype=jnp.int32)[None, :]
    top = jnp.max(logits, axis=1, keepdims=True)
    raised = jnp.exp(logits - top)
    total = jnp.sum(raised, axis=1, keepdims=True)
    losses = top[:, 0] + jnp.log(total[:, 0]) - jnp.sum(jnp.where(targets, logits, 0.0), axis=1)
    query_losses = lax.dynamic_slice_in_dim(losses, data_index * query_count, query_count)
    grad_logits = (raised / total - targets.astype(f32)) * temper
    rows_of = lax.dynamic_slice_in_dim(grad_logits, data_index * query_count, query_count, 0)
    columns_of = lax.dynamic_slice_in_dim(grad_logits, data_index * query_count, query_count, 1)
    grad_cls = jnp.concatenate(
        [
            jnp.dot(rows_of, passage_cls.astype(f32), precision=highest),
            jnp.dot(columns_of.T, query_cls.astype(f32), precision=highest),
        ]
    )
    grad_mixed = grad_out.astype(f32) + jnp.dot(
        picker.astype(f32).T, grad_cls, precision=highest
    )

    grad_second = norm_pull(grad_mixed, unit_two, inverse_two, ln2_gain)
    stats = [
        jnp.sum(grad_mixed * unit_two, axis=0),
        jnp.sum(grad_mixed, axis=0),
        jnp.sum(grad_second, axis=0),
    ]
    second_low = grad_second.astype(bf16)
    grad_before = (mm(second_low, back_all, NT) * slope.astype(f32)).astype(bf16)
    grad_hidden = grad_second + mm(grad_before, in_all)
    grad_first = norm_pull(grad_hidden, unit_one, inverse_one, ln1_gain)
    stats += [
        jnp.sum(grad_hidden * unit_one, axis=0),
        jnp.sum(grad_hidden, axis=0),
        jnp.sum(grad_first, axis=0),
    ]
    first_low = grad_first.astype(bf16)
    first_window = halo_rows(first_low, halo)
    d_back = mm(active, second_low, TN).astype(bf16)
    d_in = mm(grad_before, hidden_low, TN).astype(bf16)
    unit_rows = units // data_ways
    back_sum = reduce_rows(d_back.reshape(data_ways, ways, unit_rows, width))
    in_sum = reduce_rows(d_in.reshape(data_ways, ways, unit_rows, width))
    d_b_in = jnp.sum(grad_before, axis=0, dtype=f32)
    d_b_in = d_b_in.reshape(data_ways, ways, unit_rows).transpose(1, 0, 2).reshape(ways, units)

    grad_context = mm(first_window, attn_all[3], NT).astype(bf16)
    grad_queries, grad_keys, grad_values = attend_backward(
        bounds, queries, keys, values, grad_context, halo
    )
    d_attn = jnp.stack(
        [
            mm(grad_queries, tokens, TN),
            mm(grad_keys, tokens, TN),
            mm(grad_values, tokens, TN),
            mm(context, first_low, TN),
        ]
    ).astype(bf16)
    d_attn = d_attn.reshape(4, ways, inner, width).transpose(1, 0, 2, 3)
    d_attn = d_attn.reshape(ways, data_ways, 4 * inner // data_ways, width).transpose(1, 0, 2, 3)
    attn_sum = reduce_rows(d_attn).astype(f32).reshape(4, inner, width)
    d_b_query = jnp.sum(grad_queries, axis=0, dtype=f32)
    d_b_value = jnp.sum(grad_values, axis=0, dtype=f32)
    d_tokens = (
        grad_first
        + mm(grad_queries, attn_all[0])
        + mm(grad_keys, attn_all[1])
        + mm(grad_values, attn_all[2])
    )

    vectors = [v.reshape(ways, -1) for v in [*stats, d_b_query, d_b_value]] + [d_b_in]
    vectors = lax.psum(jnp.concatenate(vectors, axis=1), ("dp", "mp"))
    vectors = lax.dynamic_index_in_dim(vectors, mp_index, 0, keepdims=False)
    part = width // ways
    pieces = [vectors[i * part : (i + 1) * part] for i in range(8)]
    return (
        mixed,
        query_losses,
        d_tokens,
        attn_sum[0].T,
        attn_sum[1].T,
        attn_sum[2].T,
        pieces[6],
        pieces[7],
        attn_sum[3],
        pieces[5],
        pieces[3],
        pieces[4],
        in_sum.astype(f32).T,
        vectors[8 * part :],
        back_sum.astype(f32),
        pieces[2],
        pieces[0],
        pieces[1],
    )


def solution(mesh):
    return jax.shard_map(
        shards,
        mesh=mesh,
        in_specs=(
            P(("dp", "mp"), None), P(("dp", "mp"), None), P("dp", None), P("dp"),
            P(None, "mp"), P(None, "mp"), P(None, "mp"), P("mp"), P("mp"), P("mp", None), P(),
            P(), P(), P(None, "mp"), P("mp"), P("mp", None), P(), P(), P(),
        ),
        out_specs=(
            P(("dp", "mp"), None), P("dp"), P(("dp", "mp"), None),
            P(None, "mp"), P(None, "mp"), P(None, "mp"), P("mp"), P("mp"), P("mp", None),
            P("mp"), P("mp"), P("mp"), P(None, "mp"), P("mp"), P("mp", None), P("mp"), P("mp"), P("mp"),
        ),
        check_vma=False,
    )
```

time: 1490 us -> 709 us (0.48)
  waiting for transfers between devices: 1030 us -> 388 us
  matrix products: 221 us -> 93.6 us
  Pallas kernels: 0 us -> 68.9 us
  other arithmetic: 81.2 us -> 19.7 us
  local copies, waits for them, and re-layouts: 76.4 us -> 48.2 us
  starting transfers between devices: 1.49 us -> 23.3 us
    all_gather x5 -> x6, waiting for transfers between devices: 418 us -> 135 us  [the longest x3 123 us: gather_rows(): full = lax.all_gather(own, ('dp', 'mp'), axis=0, tiled=True)]
    reduce_scatter x5 -> x3, waiting for transfers between devices: 505 us -> 233 us  [reduce_rows(): lax.psum_scatter(grads.reshape(data_ways * ways * rows, width), ('dp', 'm...]
    dot_general x44 -> x23, matrix products: 221 us -> 93.6 us  [the longest x20 87.4 us: mm(): return lax.dot_general(a, b, dims, preferred_element_type=f32)]
    psum x1 -> x0, waiting for transfers between devices: 111 us -> none  [shards(): summed = lax.psum(attn_parts + ffn_parts, 'dp')]
    pallas_call x0 -> x2, Pallas kernels: none -> 68.9 us  [the longest x1 49.4 us: attend_backward(): pl.pallas_call(functools.partial(backward_kernel, halo), out_shape=(out,...]
    reduce_sum x14 -> x4, other arithmetic: 35.2 us -> 2.71 us  [the longest x2 2.27 us: norm_parts(): spread = jnp.mean(center * center, axis=-1, keepdims=True)]
    unnamed x2 -> x0, blocking collectives: 26.7 us -> none
    ppermute x0 -> x13, starting transfers between devices: none -> 22.8 us  [the longest x2 8.25 us: halo_rows(): lax.ppermute(values[-halo:], 'mp', [(i, i + 1) for i in range(ways - 1)])]
  transfers between devices with their start and end apart: 11 -> 22, of which waited for: 10 -> 16; matrix products, arithmetic and copies ran while one was open for 3% -> 15% of each run, Pallas kernels for 0% -> 10%
where the time goes in v1:
time: 709 us; the launch traced here: 698 us
  waiting for transfers between devices  388 us (55%)
  matrix products  93.6 us (13%)
  Pallas kernels  68.9 us (10%)
  local copies, waits for them, and re-layouts  48.2 us (7%)
  blocking collectives  41.2 us (6%)
  starting transfers between devices  23.3 us (3%)
  other arithmetic  19.7 us (3%)
  between operations  15.2 us (2%)
    reduce_scatter x3, waiting for transfers between devices, reduce_rows(): lax.psum_scatter(grads.reshape(data_ways * ways * rows, width), ('dp', 'm...  233 us
    all_gather x3, waiting for transfers between devices, gather_rows(): full = lax.all_gather(own, ('dp', 'mp'), axis=0, tiled=True)  123 us
    dot_general x20, matrix products, mm(): return lax.dot_general(a, b, dims, preferred_element_type=f32)  87.4 us
    pallas_call x1, Pallas kernels, attend_backward(): pl.pallas_call(functools.partial(backward_kernel, halo), out_shape=(out,...  49.4 us
    psum x1, blocking collectives, shards(): vectors = lax.psum(jnp.concatenate(vectors, axis=1), ('dp', 'mp'))  41.2 us
    unnamed x110, local copies, waits for them, and re-layouts  22.9 us
    pallas_call x1, Pallas kernels, attend_forward(): pl.pallas_call(functools.partial(forward_kernel, halo), out_shape=jax.Sha...  19.6 us
  transfers between devices with their start and end apart: 22, of which 16 were waited for; matrix products, arithmetic and copies ran while one was open for 15% of the time, Pallas kernels for 10%

profile of v1, /device:TPU:1, one launch (start us, length us, event | category | flops | bytes accessed | tf_op | source)
XLA Modules:
  0.0 698.0 jit_solution(11528547088795433769)
XLA Ops:
  12.1 4.2 collective-permute-start.2
  17.6 4.1 collective-permute-start
  27.9 5.1 collective-permute-done
  36.3 42.1 %all-gather.7.cloned.1.call-done = bf16[3072,768]{1,0:T(8,128)(2,1)} async-done(((bf16[96,768]{1,0:T(8,128)(2,1)}), bf16[3072,768]{1,0:T(8,128)(2,1)}) %all-gather.7.cloned.1.call-update) | async-done | bytes 4718608 | tf_op jit(solution)/shard_map/all_gather | solution.py:281
  81.5 4.8 multiply_convert_fusion.2.q_ref
  86.4 3.9 convolution_convert_fusion.3.k_ref
  93.7 19.6 %attend_forward.1 = bf16[768,768]{1,0:T(8,128)(2,1)S(1)} custom-call(s32[3,10]{1,0:T(4,128)S(1)} %pad_add_fusion.tiles_ref, s32[1280,1]{1,0:T(8,128)S(1)} %get-tuple-element.189.lo_ref, s32[1280,1]{1,0:T(8,128)S(1)} %get-tuple-element.188.hi_ref, bf16[768,768]{1,0:T(8,128)(2,1)S(1)} %slice.221.q_ref, bf16[1280,768]{1,0:T(8,128)(2,1)S(1)} %convolution_convert_fusion.3.k_ref, ...), custom_call_target="tpu_custom_call" | custom-call | tf_op jit(solution)/shard_map/attend_forward/pallas_call | solution.py:139
  118.0 26.2 %all-gather.9.cloned.1.call-done = bf16[3072,768]{1,0:T(8,128)(2,1)} async-done(((bf16[96,768]{1,0:T(8,128)(2,1)}), bf16[3072,768]{1,0:T(8,128)(2,1)}) %all-gather.9.cloned.1.call-update) | async-done | bytes 4718608 | tf_op jit(solution)/shard_map/all_gather | solution.py:281
  144.2 10.9 %multiply_convert_fusion.1 = (bf16[768,3072]{1,0:T(8,128)(2,1)}, f32[768,3072]{1,0:T(8,128)}) fusion(f32[3072]{0:T(1024)S(1)} %add.268, bf16[3072,768]{1,0:T(8,128)(2,1)} %all-gather.9.cloned.1.call-done, f32[768,768]{0,1:T(8,128)} %get-tuple-element.177, f32[768]{0:T(1024)S(1)} %copy-done.48, f32[768]{0:T(1024)S(1)} %copy-done.42, ...), kind=kOutput, calls=%fused_computation.8 | convolution fusion | flops 3640983552 | bytes 21258240 | tf_op jit(solution)/shard_map/dot_general | solution.py:30
  155.1 54.8 %all-gather.11.cloned.1.call-done = bf16[3072,768]{1,0:T(8,128)(2,1)} async-done(((bf16[96,768]{1,0:T(8,128)(2,1)}), bf16[3072,768]{1,0:T(8,128)(2,1)}) %all-gather.11.cloned.1.call-update) | async-done | bytes 4718608 | tf_op jit(solution)/shard_map/all_gather | solution.py:281
  210.0 9.0 %fusion.56 = (f32[768]{0:T(1024)S(1)}, f32[768,768]{0,1:T(8,128)S(1)}) fusion(f32[768]{0:T(1024)S(1)} %copy-done.47, bf16[768,3072]{1,0:T(8,128)(2,1)} %get-tuple-element.178, bf16[3072,768]{1,0:T(8,128)(2,1)} %all-gather.11.cloned.1.call-done, f32[768]{0:T(1024)S(1)} %copy-done.48, f32[768]{0:T(1024)S(1)} %copy-done.42, f32[768]{0:T(1024)S(1)} %add_rsqrt_fusion.1, ...), kind=kOutput, calls=%fused_computation.163 | convolution fusion | flops 3628006656 | bytes 14174208 | tf_op jit(solution)/shard_map/dot_general | solution.py:30
  250.0 4.8 multiply_reduce_fusion.1
  255.8 10.9 %convert_reduce_fusion = (f32[3072]{0:T(1024)}, bf16[768,3072]{1,0:T(8,128)(2,1)S(1)}) fusion(f32[768,3072]{1,0:T(8,128)} %get-tuple-element.179, f32[3072]{0:T(1024)S(1)} %add.268, bf16[3072,768]{1,0:T(8,128)(2,1)} %all-gather.11.cloned.1.call-done, f32[768,768]{0,1:T(8,128)S(1)} %get-tuple-element.141), kind=kOutput, calls=%fused_computation.6 | convolution fusion | flops 3659854848 | bytes 21258240 | tf_op jit(solution)/shard_map/dot_general | solution.py:30
  268.8 7.8 %convolution_convert_fusion.1 = bf16[3072,768]{1,0:T(8,128)(2,1)} fusion(bf16[768,3072]{1,0:T(8,128)(2,1)S(1)} %get-tuple-element.187, f32[768,768]{0,1:T(8,128)} %get-tuple-element.177, f32[768]{0:T(1024)S(1)} %copy-done.48, f32[768]{0:T(1024)S(1)} %copy-done.42, f32[768]{0:T(1024)S(1)} %add_rsqrt_fusion.1, f32[768]{0:T(1024)S(1)} %broadcast_multiply_fusion.5), kind=kOutput, calls=%fused_computation.11 | convolution fusion | flops 3629187072 | bytes 11808768 | tf_op jit(solution)/shard_map/dot_general | solution.py:30
  276.9 9.2 %convolution_convert_fusion = bf16[3072,768]{1,0:T(8,128)(2,1)} fusion(bf16[768,3072]{1,0:T(8,128)(2,1)} %get-tuple-element.178, f32[768,768]{0,1:T(8,128)} %copy-done.25), kind=kOutput, calls=%fused_computation.10 | convolution fusion | flops 3626827776 | bytes 11796480 | tf_op jit(solution)/shard_map/dot_general | solution.py:30
  286.2 11.1 %multiply_reduce_fusion = (f32[768]{0:T(1024)}, f32[768]{0:T(1024)S(1)}, f32[768]{0:T(1024)S(1)}, f32[768]{0:T(1024)}, f32[768,768]{0,1:T(8,128)S(1)}) fusion(f32[768,768]{0,1:T(8,128)} %get-tuple-element.177, f32[768]{0:T(1024)S(1)} %add_rsqrt_fusion.1, f32[768]{0:T(1024)S(1)} %broadcast_multiply_fusion.5, f32[768]{0:T(1024)S(1)} %copy-done.42, ...), kind=kOutput, calls=%fused_computation.20 | convolution fusion | flops 3629773824 | bytes 16536576 | tf_op jit(solution)/shard_map/dot_general | solution.py:30
  302.6 4.1 collective-permute-start.11
  307.9 3.8 collective-permute-done.12
  315.8 49.4 %attend_backward.1 = (bf16[768,768]{1,0:T(8,128)(2,1)S(1)}, bf16[768,768]{1,0:T(8,128)(2,1)S(1)}, bf16[768,768]{1,0:T(8,128)(2,1)S(1)}) custom-call(s32[3,10]{1,0:T(4,128)S(1)} %pad_add_fusion.tiles_ref, s32[1280,1]{1,0:T(8,128)S(1)} %get-tuple-element.189.lo_ref, s32[1280,1]{1,0:T(8,128)S(1)} %get-tuple-element.188.hi_ref, bf16[1280,768]{1,0:T(8,128)(2,1)S(1)} %copy-done.4, ...), custom_call_target="tpu_custom_call" | custom-call | tf_op jit(solution)/shard_map/attend_backward/pallas_call | solution.py:206
  372.1 11.1 %reduce-scatter.6.cloned.1.call-done = bf16[96,768]{1,0:T(8,128)(2,1)} async-done(((bf16[3072,768]{1,0:T(8,128)(2,1)}), bf16[96,768]{1,0:T(8,128)(2,1)}) %reduce-scatter.6.cloned.1.call-update) | async-done | bytes 147472 | tf_op jit(solution)/shard_map/reduce_scatter | solution.py:287
  383.3 112.3 %reduce-scatter.8.cloned.1.call-done = bf16[96,768]{1,0:T(8,128)(2,1)} async-done(((bf16[3072,768]{1,0:T(8,128)(2,1)}), bf16[96,768]{1,0:T(8,128)(2,1)}) %reduce-scatter.8.cloned.1.call-update) | async-done | bytes 147472 | tf_op jit(solution)/shard_map/reduce_scatter | solution.py:287
  497.3 109.7 %reduce-scatter.4.cloned.1.call-done = bf16[96,768]{1,0:T(8,128)(2,1)} async-done(((bf16[3072,768]{1,0:T(8,128)(2,1)}), bf16[96,768]{1,0:T(8,128)(2,1)}) %reduce-scatter.4.cloned.1.call-update) | async-done | bytes 147472 | tf_op jit(solution)/shard_map/reduce_scatter | solution.py:287
  625.9 41.2 %psum.7 = f32[4,2304]{1,0:T(4,128)S(1)} all-reduce(f32[4,2304]{1,0:T(4,128)S(1)} %concatenate.91), channel_id=1, replica_groups=mesh['dp'=8,'mp'=4] {'dp','mp'}, use_global_device_ids=true, to_apply=%region_23.24 | all-reduce | flops 9216 | bytes 73728 | tf_op jit(solution)/shard_map/psum | solution.py:438
  674.7 12.0 %all-gather.13.cloned.1.call-done = bf16[768,768]{1,0:T(8,128)(2,1)} async-done(((bf16[96,768]{1,0:T(8,128)(2,1)}), bf16[768,768]{1,0:T(8,128)(2,1)}) %all-gather.13.cloned.1.call-update) | async-done | bytes 1179664 | tf_op jit(solution)/shard_map/all_gather | solution.py:290
  (266 shorter events, 110.8 us)
Async XLA Ops:
  7.3 71.2 %all-gather.7.cloned.1.call-start = ((), (), s32[]{:S(2)}) async-start(), calls=%async_computation.3 | async-start | bytes 4866048 | tf_op jit(solution)/shard_map/all_gather | solution.py:281
  9.3 134.9 %all-gather.9.cloned.1.call-start = ((), (), s32[]{:S(2)}) async-start(), calls=%async_computation.4 | async-start | bytes 4866048 | tf_op jit(solution)/shard_map/all_gather | solution.py:281
  10.3 199.7 %all-gather.11.cloned.1.call-start = ((), (), s32[]{:S(2)}) async-start(), calls=%async_computation.5 | async-start | bytes 4866048 | tf_op jit(solution)/shard_map/all_gather | solution.py:281
  11.9 371.3 %reduce-scatter.6.cloned.1.call-start = ((), (), s32[]{:S(2)}) async-start(), calls=%async_computation.8 | async-start | bytes 4866048 | tf_op jit(solution)/shard_map/reduce_scatter | solution.py:287
  12.1 15.2 %collective-permute-start.2 = (f32[1152]{0:T(1024)S(1)}, f32[1152]{0:T(1024)S(1)}, u32[]{:S(2)}, u32[]{:S(2)}) collective-permute-start(f32[1152]{0:T(1024)S(1)} %concatenate.74), channel_id=1, source_target_pairs={{0,3},{1,0},{2,1},{3,2},{4,7},{5,4},{6,5},{7,6},{8,11},{9,8},{10,9... | collective-permute-start | bytes 13832 | tf_op jit(solution)/shard_map/ppermute | solution.py:253
  16.3 11.1 %collective-permute-start.3 = (f32[1152]{0:T(1024)S(1)}, f32[1152]{0:T(1024)S(1)}, u32[]{:S(2)}, u32[]{:S(2)}) collective-permute-start(f32[1152]{0:T(1024)S(1)} %concatenate.74), channel_id=1, source_target_pairs={{0,2},{1,3},{2,0},{3,1},{4,6},{5,7},{6,4},{7,5},{8,10},{9,11},{10,... | collective-permute-start | bytes 13832 | tf_op jit(solution)/shard_map/ppermute | solution.py:253
  16.3 11.1 %collective-permute-start.4 = (f32[1152]{0:T(1024)S(1)}, f32[1152]{0:T(1024)S(1)}, u32[]{:S(2)}, u32[]{:S(2)}) collective-permute-start(f32[1152]{0:T(1024)S(1)} %concatenate.74), channel_id=1, source_target_pairs={{0,1},{1,2},{2,3},{3,0},{4,5},{5,6},{6,7},{7,4},{8,9},{9,10},{10,1... | collective-permute-start | bytes 13832 | tf_op jit(solution)/shard_map/ppermute | solution.py:253
  17.6 15.4 %collective-permute-start = (bf16[256,768]{1,0:T(8,128)(2,1)}, bf16[256,768]{1,0:T(8,128)(2,1)S(1)}, u32[]{:S(2)}, u32[]{:S(2)}) collective-permute-start(bf16[256,768]{1,0:T(8,128)(2,1)} %get-tuple-element.157), channel_id=1, source_target_pairs={{0,1},{1,2},{2,3},{4,5},{5,6},{6,7},{8,9},{9,10},{10,11},{12,13},{... | collective-permute-start | bytes 1179656 | tf_op jit(solution)/shard_map/ppermute | solution.py:246
  21.8 13.8 %collective-permute-start.1 = (bf16[256,768]{1,0:T(8,128)(2,1)}, bf16[256,768]{1,0:T(8,128)(2,1)S(1)}, u32[]{:S(2)}, u32[]{:S(2)}) collective-permute-start(bf16[256,768]{1,0:T(8,128)(2,1)} %get-tuple-element.156), channel_id=1, source_target_pairs={{1,0},{2,1},{3,2},{5,4},{6,5},{7,6},{9,8},{10,9},{11,10},{13,12},{... | collective-permute-start | bytes 1179656 | tf_op jit(solution)/shard_map/ppermute | solution.py:247
  222.2 4.8 collective-permute-start.7
  223.9 6.1 collective-permute-start.6
  224.4 5.6 collective-permute-start.5
  230.1 1.5 collective-permute-start.8
  231.6 4.2 collective-permute-start.9
  236.9 5.4 collective-permute-start.10
  276.7 218.9 %reduce-scatter.8.cloned.1.call-start = ((), (), s32[]{:S(2)}) async-start(), calls=%async_computation.10 | async-start | bytes 4866048 | tf_op jit(solution)/shard_map/reduce_scatter | solution.py:287
  286.1 320.8 %reduce-scatter.4.cloned.1.call-start = ((), (), s32[]{:S(2)}) async-start(), calls=%async_computation.6 | async-start | bytes 4866048 | tf_op jit(solution)/shard_map/reduce_scatter | solution.py:287
  301.3 10.4 %collective-permute-start.12 = (bf16[256,768]{0,1:T(8,128)(2,1)S(1)}, bf16[256,768]{0,1:T(8,128)(2,1)S(1)}, u32[]{:S(2)}, u32[]{:S(2)}) collective-permute-start(bf16[256,768]{0,1:T(8,128)(2,1)S(1)} %get-tuple-element.155), channel_id=1, source_target_pairs={{1,0},{2,1},{3,2},{5,4},{6,5},{7,6},{9,8},{10,9},{11,10},{13,12},{... | collective-permute-start | bytes 1179656 | tf_op jit(solution)/shard_map/ppermute | solution.py:247
  302.6 10.1 %collective-permute-start.11 = (bf16[256,768]{0,1:T(8,128)(2,1)S(1)}, bf16[256,768]{0,1:T(8,128)(2,1)S(1)}, u32[]{:S(2)}, u32[]{:S(2)}) collective-permute-start(bf16[256,768]{0,1:T(8,128)(2,1)S(1)} %get-tuple-element.154), channel_id=1, source_target_pairs={{0,1},{1,2},{2,3},{4,5},{5,6},{6,7},{8,9},{9,10},{10,11},{12,13},{... | collective-permute-start | bytes 1179656 | tf_op jit(solution)/shard_map/ppermute | solution.py:246
  372.0 243.3 %copy-start.12 = (bf16[768,768]{1,0:T(8,128)(2,1)S(1)}, bf16[768,768]{1,0:T(8,128)(2,1)}, u32[]{:S(2)}) copy-start(bf16[768,768]{1,0:T(8,128)(2,1)} %copy-done.11) | copy-start | bytes 3538948
  372.0 243.3 %copy-start.29 = (bf16[1,4,192,768]{3,2,0,1:T(8,128)(2,1)S(1)}, bf16[1,4,192,768]{3,2,0,1:T(8,128)(2,1)}, u32[]{:S(2)}) copy-start(bf16[1,4,192,768]{3,2,0,1:T(8,128)(2,1)} %copy-done.28) | copy-start | bytes 3538948
  372.0 296.4 %all-gather.15.cloned.1.call-start = ((), (), s32[]{:S(2)}) async-start(), calls=%async_computation.9 | async-start | bytes 1327104 | tf_op jit(solution)/shard_map/all_gather | solution.py:290
  383.2 288.6 %all-gather.17.cloned.1.call-start = ((), (), s32[]{:S(2)}) async-start(), calls=%async_computation.11 | async-start | bytes 1327104 | tf_op jit(solution)/shard_map/all_gather | solution.py:290
  495.6 191.1 %all-gather.13.cloned.1.call-start = ((), (), s32[]{:S(2)}) async-start(), calls=%async_computation.7 | async-start | bytes 1327104 | tf_op jit(solution)/shard_map/all_gather | solution.py:290
  (49 other events, 579.8 us)
Sparse Core Ops, SparseCore 0:
  11.5 66.9 all-gather.6
  81.9 62.2 all-gather.8
  147.6 62.3 all-gather.10
  276.8 106.3 reduce-scatter.5
  389.4 106.0 reduce-scatter.7
  500.9 106.0 reduce-scatter.3
  609.0 25.2 all-gather.14
  636.3 24.2 all-gather.16
  662.6 24.0 all-gather.12

commit v2 on v1

--- a/solution.py
+++ b/solution.py
@@ -125,7 +125,7 @@
                 out_ref[pl.ds(row, TILE), lanes] = join_pair(mm(weights, v)).astype(bf16)
                 return inner
 
-            lax.fori_loop(0, pairs, pair_step, 0, unroll=2)
+            lax.fori_loop(0, pairs, pair_step, 0, unroll=pairs)
 
         by_span(blocks, count, act)
         return carry
@@ -133,18 +133,34 @@
     lax.fori_loop(0, tiles, tile_step, 0)
 
 
-def attend_forward(bounds, queries, keys, values, halo):
+def lasting(micros):
+    return pl.CostEstimate(flops=int(micros * 1e9), bytes_accessed=int(micros * 3.5e6), transcendentals=0)
+
+
+def lane_group(array, group, groups):
+    return pl.BlockSpec((array.shape[0], array.shape[1] // groups), lambda i: (0, group))
+
+
+def whole(array):
+    return pl.BlockSpec(array.shape, lambda i: (0, 0))
+
+
+def attend_forward(bounds, queries, keys, values, halo, group, groups):
     tiles, low, high = bounds
-    vmem = pl.BlockSpec(memory_space=pltpu.VMEM)
+    rows, width = queries.shape
+    arrays = (queries, keys, values)
     return pl.pallas_call(
         functools.partial(forward_kernel, halo),
-        out_shape=jax.ShapeDtypeStruct(queries.shape, bf16),
-        in_specs=[pl.BlockSpec(memory_space=pltpu.SMEM)] + [vmem] * 5,
-        out_specs=vmem,
+        grid=(1,),
+        out_shape=jax.ShapeDtypeStruct((rows, width // groups), bf16),
+        in_specs=[pl.BlockSpec(memory_space=pltpu.SMEM), whole(low), whole(high)]
+        + [lane_group(a, group, groups) for a in arrays],
+        out_specs=pl.BlockSpec((rows, width // groups), lambda i: (0, 0)),
         scratch_shapes=[pltpu.VMEM((TILE, keys.shape[0]), f32)],
         compiler_params=pltpu.CompilerParams(vmem_limit_bytes=32 * 2**20),
+        cost_estimate=lasting(18 / groups),
         name="attend_forward",
-    )(tiles, low, high, queries, keys, values)
+    )(tiles, low, high, *arrays)
 
 
 def backward_kernel(
@@ -188,7 +204,7 @@
 
                 return inner
 
-            lax.fori_loop(0, pairs, pair_step, 0)
+            lax.fori_loop(0, pairs, pair_step, 0, unroll=pairs)
 
         by_span(blocks, count, act)
         return carry
@@ -198,24 +214,217 @@
     dv_ref[...] = dv_sum[pl.ds(halo, own), :].astype(bf16)
 
 
-def attend_backward(bounds, queries, keys, values, grads, halo):
+def attend_backward(bounds, queries, keys, values, grads, halo, group, groups):
     tiles, low, high = bounds
     count, width = keys.shape
-    vmem = pl.BlockSpec(memory_space=pltpu.VMEM)
-    out = jax.ShapeDtypeStruct((count - 2 * halo, width), bf16)
+    lanes = width // groups
+    arrays = (queries, keys, values, grads)
+    out = jax.ShapeDtypeStruct((count - 2 * halo, lanes), bf16)
     return pl.pallas_call(
         functools.partial(backward_kernel, halo),
+        grid=(1,),
         out_shape=(out, out, out),
-        in_specs=[pl.BlockSpec(memory_space=pltpu.SMEM)] + [vmem] * 6,
-        out_specs=(vmem, vmem, vmem),
+        in_specs=[pl.BlockSpec(memory_space=pltpu.SMEM), whole(low), whole(high)]
+        + [lane_group(a, group, groups) for a in arrays],
+        out_specs=(pl.BlockSpec(out.shape, lambda i: (0, 0)),) * 3,
         scratch_shapes=[
             pltpu.VMEM((TILE, count), f32),
-            pltpu.VMEM((count, width), f32),
-            pltpu.VMEM((count, width), f32),
+            pltpu.VMEM((count, lanes), f32),
+            pltpu.VMEM((count, lanes), f32),
         ],
-        compiler_params=pltpu.CompilerParams(vmem_limit_bytes=44 * 2**20),
+        compiler_params=pltpu.CompilerParams(vmem_limit_bytes=32 * 2**20),
+        cost_estimate=lasting(42 / groups),
         name="attend_backward",
-    )(tiles, low, high, queries, keys, values, grads)
+    )(tiles, low, high, *arrays)
+
+
+SMEM = pl.BlockSpec(memory_space=pltpu.SMEM)
+VMEM = pl.BlockSpec(memory_space=pltpu.VMEM)
+PLANE = 8
+
+
+def local(kernel, place, arrays, outs, scratch, micros, name):
+    return pl.pallas_call(
+        kernel,
+        out_shape=tuple(jax.ShapeDtypeStruct(shape, dtype) for shape, dtype in outs),
+        in_specs=[SMEM] + [VMEM] * len(arrays),
+        out_specs=(VMEM,) * len(outs),
+        scratch_shapes=[pltpu.VMEM(shape, dtype) for shape, dtype in scratch],
+        compiler_params=pltpu.CompilerParams(vmem_limit_bytes=48 * 2**20),
+        cost_estimate=lasting(micros),
+        name=name,
+    )(place, *arrays)
+
+
+def own_heads_kernel(place_ref, q_ref, k_ref, v_ref, out_ref, rows_ref):
+    place = place_ref[0]
+    eighths = q_ref.shape[0] // PLANE
+    slabs = q_ref.shape[0] // 8
+    for i, ref in enumerate((q_ref, k_ref, v_ref)):
+        rows_ref[pl.ds(i * slabs, slabs)] = ref[...].astype(f32).reshape(slabs, 8, -1)
+    heads = 3 * eighths // 8
+    for j in range(PLANE):
+        held = [rows_ref[h * PLANE + (place ^ j)] for h in range(heads)]
+        out_ref[j] = jnp.concatenate(held, axis=0).astype(bf16)
+
+
+def own_units_kernel(place_ref, o_ref, i_ref, b_ref, out_ref, in_ref, back_ref, rows_ref, units_ref):
+    place = place_ref[0]
+    rows = in_ref.shape[1]
+    heads = out_ref.shape[1] // 8
+    rows_ref[...] = o_ref[...].astype(f32).reshape(rows_ref.shape)
+    units_ref[...] = i_ref[...].astype(f32).T.reshape(units_ref.shape)
+    for j in range(PLANE):
+        held = [rows_ref[h * PLANE + (place ^ j)] for h in range(heads)]
+        out_ref[j] = jnp.concatenate(held, axis=0).astype(bf16)
+        in_ref[j] = units_ref[place ^ j].astype(bf16)
+        back_ref[j] = b_ref[pl.ds(pl.multiple_of((place ^ j) * rows, rows), rows), :]
+
+
+def stage_eighths(own_ref, near_ref, far_ref, member, first, stage_ref):
+    rows = stage_ref.shape[1]
+    for j in range(PLANE):
+        if member == 0:
+            stage_ref[j] = own_ref[j].astype(f32)
+        else:
+            ref = near_ref if j < 4 else far_ref
+            stage_ref[j] = ref[j % 4, member - 1, pl.ds(first, rows), :].astype(f32)
+
+
+def head_block(stage_ref, head):
+    return jnp.concatenate([stage_ref[j, pl.ds(head * 8, 8), :] for j in range(PLANE)], axis=0)
+
+
+def project_kernel(
+    place_ref, left_ref, tokens_ref, right_ref, own_ref, near_ref, far_ref, bq_ref, bv_ref,
+    q_ref, k_ref, v_ref, w_ref, x_ref, stage_ref,
+):
+    ways = near_ref.shape[1] + 1
+    heads = own_ref.shape[1] // 24
+    halo = left_ref.shape[0]
+    own = tokens_ref.shape[0]
+    width = tokens_ref.shape[1]
+    inner = heads * HEAD
+    x_ref[:halo] = left_ref[...]
+    x_ref[pl.ds(halo, own)] = tokens_ref[...]
+    x_ref[pl.ds(halo + own, halo)] = right_ref[...]
+    for member in range(ways):
+        stage_eighths(own_ref, near_ref, far_ref, member, 0, stage_ref)
+        for kind in range(3):
+            blocks = [head_block(stage_ref, kind * heads + h) for h in range(heads)]
+            at = kind * width + member * inner
+            w_ref[pl.ds(at, inner)] = jnp.concatenate(blocks, axis=0).astype(bf16)
+
+    def step(i, carry):
+        rows = pl.ds(pl.multiple_of(i * 256, 256), 256)
+        x = x_ref[rows, :]
+        q = mm(x, w_ref[:width], NT) + bq_ref[...]
+        q_ref[rows, :] = (q * (1.0 / math.sqrt(HEAD))).astype(bf16)
+        k_ref[rows, :] = mm(x, w_ref[pl.ds(width, width)], NT).astype(bf16)
+        v_ref[rows, :] = (mm(x, w_ref[pl.ds(2 * width, width)], NT) + bv_ref[...]).astype(bf16)
+        return carry
+
+    lax.fori_loop(0, x_ref.shape[0] // 256, step, 0)
+
+
+def join_units_kernel(place_ref, own_ref, near_ref, far_ref, out_ref):
+    rows = own_ref.shape[1]
+    ways = near_ref.shape[1] + 1
+    for j in range(PLANE):
+        ref = near_ref if j < 4 else far_ref
+        out_ref[pl.ds(j * ways * rows, rows), :] = own_ref[j]
+        for member in range(1, ways):
+            at = (j * ways + member) * rows
+            out_ref[pl.ds(at, rows), :] = ref[j % 4, member - 1, :rows, :]
+
+
+def join_in_out_kernel(place_ref, own_ref, own_out_ref, near_ref, far_ref, in_ref, out_ref, stage_ref):
+    join_units_kernel(place_ref, own_ref, near_ref, far_ref, in_ref)
+    rows = own_ref.shape[1]
+    heads = own_out_ref.shape[1] // 8
+    for member in range(near_ref.shape[1] + 1):
+        stage_eighths(own_out_ref, near_ref, far_ref, member, rows, stage_ref)
+        for h in range(heads):
+            block = head_block(stage_ref, h)
+            out_ref[pl.ds((member * heads + h) * HEAD, HEAD), :] = block.astype(bf16)
+
+
+def piece_grads_kernel(groups, place_ref, *refs):
+    grad_refs, context_refs = refs[: 3 * groups], refs[3 * groups : 3 * groups + 2]
+    tokens_ref, first_ref, vectors_ref, keep_ref, send_ref, sum_ref = refs[3 * groups + 2 :]
+    place = place_ref[0]
+    ways = vectors_ref.shape[0]
+    width = tokens_ref.shape[1]
+    inner = width // ways
+    heads = inner // HEAD
+
+    def put(kind, first_head, block):
+        for i in range(block.shape[0] // HEAD):
+            member, h = divmod(first_head + i, heads)
+            for j in range(PLANE):
+                part = block[i * HEAD + j * 8 : i * HEAD + j * 8 + 8]
+                sum_ref[j * ways + member, pl.ds((kind * heads + h) * 8, 8), :] = part
+
+    lanes = width // groups
+    for kind in range(3):
+        for g in range(groups):
+            put(kind, g * lanes // HEAD, mm(grad_refs[kind * groups + g][...], tokens_ref[...], TN))
+    for g, ref in enumerate(context_refs):
+        put(3, g * width // 2 // HEAD, mm(ref[...], first_ref[...], TN))
+    lane = lax.broadcasted_iota(jnp.int32, (width, width), 0)
+    to = lax.broadcasted_iota(jnp.int32, (width, width), 1)
+    member = sum((lane >= i * inner).astype(jnp.int32) for i in range(1, ways))
+    within = lane - member * inner
+    spot = (within & ~(HEAD - 8)) | ((((within >> 3) & 7) ^ place) << 3)
+    row = lax.broadcasted_iota(jnp.int32, (8, width), 0)
+    column = lax.broadcasted_iota(jnp.int32, (8, width), 1)
+    of = sum((column >= i * inner).astype(jnp.int32) for i in range(1, ways))
+    ones = jnp.ones((8, tokens_ref.shape[0]), bf16)
+    lines = jnp.zeros((8, width), f32)
+    for kind, first in ((0, width - 2 * inner), (2, width - inner)):
+        sums = [mm(ones, grad_refs[kind * groups + g][...]) for g in range(groups)]
+        sums = jnp.where(of == row, jnp.concatenate(sums, axis=1), 0.0)
+        chosen = jnp.where(spot + first == to, 1.0, 0.0).astype(bf16)
+        lines = lines + mm(sums.astype(bf16), chosen)
+    below = 4 * heads * 8
+    for i in range(ways):
+        block = vectors_ref[i] + jnp.where(row == 2, lines[i : i + 1], 0.0)
+        for j in range(PLANE):
+            sum_ref[j * ways + i, pl.ds(below, 8), :] = block
+    half = keep_ref.shape[0]
+    for i in range(half):
+        keep_ref[i] = sum_ref[i].astype(bf16)
+        send_ref[i] = sum_ref[half + i].astype(bf16)
+
+
+def finish_heads_kernel(place_ref, near_ref, far_ref, q_ref, k_ref, v_ref, o_ref, rows_ref):
+    place = place_ref[0]
+    heads = o_ref.shape[0] // HEAD
+    rows_ref[:4] = near_ref[...].astype(f32)
+    rows_ref[4:] = far_ref[...].astype(f32)
+    for kind, ref in enumerate((q_ref, k_ref, v_ref, o_ref)):
+        held = []
+        for h in range(heads):
+            for p in range(PLANE):
+                held.append(rows_ref[place ^ p, pl.ds((kind * heads + h) * 8, 8), :])
+        block = jnp.concatenate(held, axis=0)
+        ref[...] = block
+
+
+def finish_units_kernel(
+    place_ref, back_near_ref, back_far_ref, in_near_ref, in_far_ref, back_ref, in_ref, rows_ref, turned_ref
+):
+    place = place_ref[0]
+    rows = back_near_ref.shape[1]
+    rows_ref[:4] = back_near_ref[...].astype(f32)
+    rows_ref[4:] = back_far_ref[...].astype(f32)
+    for p in range(PLANE):
+        back_ref[pl.ds(p * rows, rows), :] = rows_ref[place ^ p]
+    rows_ref[:4] = in_near_ref[...].astype(f32)
+    rows_ref[4:] = in_far_ref[...].astype(f32)
+    for p in range(PLANE):
+        turned_ref[pl.ds(p * rows, rows), :] = rows_ref[place ^ p]
+    in_ref[...] = turned_ref[...].T
 
 
 def norm_parts(values):
@@ -245,13 +454,7 @@
     ways = lax.axis_size("mp")
     before = lax.ppermute(values[-halo:], "mp", [(i, i + 1) for i in range(ways - 1)])
     after = lax.ppermute(values[:halo], "mp", [(i + 1, i) for i in range(ways - 1)])
-    return jnp.concatenate([before, values, after], axis=0)
-
-
-def ring_stack(values):
-    ways = lax.axis_size("mp")
-    held = [values] + [lax.ppermute(values, "mp", turn(ways, step)) for step in range(1, ways)]
-    return jnp.roll(jnp.stack(held), lax.axis_index("mp"), axis=0)
+    return before, after
 
 
 def group_tables(table):
@@ -273,21 +476,50 @@
     return held
 
 
-def gather_rows(shard):
+CORE, NEAR_X, NEAR_Y = 1, 2, 4
+
+
+def swap(values, bit):
+    ways = lax.axis_size("dp")
+    return lax.ppermute(values, "dp", [(i, i ^ bit) for i in range(ways)])
+
+
+def along(piece):
+    ways = lax.axis_size("mp")
+    return [lax.ppermute(piece, "mp", turn(ways, step)) for step in range(1, ways)]
+
+
+def spread_at_once(values):
+    others = [swap(values, bit) for bit in (NEAR_X, NEAR_Y, NEAR_X | NEAR_Y)]
+    near = jnp.stack([values, *others])
+    return near, swap(near, CORE)
+
+
+def spread_x_first(values):
+    both = jnp.stack([values, swap(values, NEAR_X)])
+    return jnp.stack([both, swap(both, NEAR_Y)]).reshape(4, *values.shape)
+
+
+def spread_y_first(values):
+    both = jnp.stack([values, swap(values, NEAR_Y)])
+    return jnp.stack([both, swap(both, NEAR_X)], axis=1).reshape(4, *values.shape)
+
+
+def add(first, second):
+    return (first.astype(f32) + second.astype(f32)).astype(bf16)
+
+
+def sum_along(parts):
+    ways = lax.axis_size("mp")
     data_ways = lax.axis_size("dp")
-    ways = lax.axis_size("mp")
-    rows = shard.shape[0] // data_ways
-    own = lax.dynamic_slice_in_dim(shard, lax.axis_index("dp") * rows, rows, 0)
-    full = lax.all_gather(own, ("dp", "mp"), axis=0, tiled=True)
-    return full.reshape(data_ways, ways, rows, shard.shape[1])
-
-
-def reduce_rows(grads):
-    data_ways, ways, rows, width = grads.shape
-    own = lax.psum_scatter(
-        grads.reshape(data_ways * ways * rows, width), ("dp", "mp"), scatter_dimension=0, tiled=True
-    )
-    return lax.all_gather(own, "dp", axis=0, tiled=True)
+    total = parts[0].astype(f32)
+    for step in range(1, ways):
+        total = total + lax.ppermute(parts[step], "mp", turn(ways, -step)).astype(f32)
+    level = PLANE
+    while level < data_ways:
+        total = total + swap(total, level)
+        level *= 2
+    return total
 
 
 def shards(
@@ -307,16 +539,56 @@
     scale = 1.0 / math.sqrt(HEAD)
     temper = 2.0 / math.sqrt(width)
 
-    attn_shard = jnp.concatenate([w_query.T, w_key.T, w_value.T, w_out], axis=0)
-    attn_all = gather_rows(attn_shard)
-    in_all = gather_rows(w_in.T).reshape(ways * units, width)
-    back_all = gather_rows(w_back).reshape(ways * units, width)
-    attn_all = attn_all.transpose(1, 0, 2, 3).reshape(ways, 4, inner, width)
-    attn_all = attn_all.transpose(1, 0, 2, 3).reshape(4, ways * inner, width)
-    biases = ring_stack(jnp.concatenate([b_query, b_value, b_in]))
-    bias_query = biases[:, :inner].reshape(-1)
-    bias_value = biases[:, inner : 2 * inner].reshape(-1)
-    bias_in = biases[:, 2 * inner :].reshape(ways, data_ways, units // data_ways)
+    piece_rows = units // PLANE
+    heads = inner // HEAD
+    part = inner // PLANE
+    place = ((data_index & CORE) << 2 | (data_index % PLANE) >> 1).reshape(1)
+    (qkv_own,) = local(
+        own_heads_kernel, place, (w_query.T, w_key.T, w_value.T), [((PLANE, 3 * part, width), bf16)],
+        [((3 * heads * PLANE, 8, width), f32)], 4, "own_heads",
+    )
+    biases = jnp.concatenate([b_in, b_query, b_value])
+    digits, rest = [], biases
+    for _ in range(3):
+        digits.append(lax.reduce_precision(rest, 8, 7))
+        rest = rest - digits[-1]
+    digits = jnp.stack(digits)
+    lines = jnp.concatenate(
+        [digits[:, :units], jnp.pad(digits[:, units:], ((0, 0), (0, width - 2 * inner)))]
+    )
+    lines = jnp.pad(lines, ((0, 2), (0, 0))).astype(bf16)
+    qkv_along = along(jnp.concatenate([qkv_own[0], lines]))
+    tokens_before, tokens_after = halo_rows(tokens, halo)
+    w_out, w_in, w_back, place = lax.optimization_barrier((w_out, w_in, w_back, place, qkv_own))[:4]
+    out_own, in_own, back_own = local(
+        own_units_kernel, place, (w_out, w_in, w_back),
+        [((PLANE, part, width), bf16), ((PLANE, piece_rows, width), bf16), ((PLANE, piece_rows, width), bf16)],
+        [((heads * PLANE, 8, width), f32), ((PLANE, piece_rows, width), f32)], 5, "own_units",
+    )
+    in_piece = jnp.concatenate([in_own[0], out_own[0]])
+    back_piece = back_own[0]
+    qkv_along, in_piece, back_piece = lax.optimization_barrier((qkv_along, in_piece, back_piece))
+    bias_rest = jnp.stack([piece[3 * part :] for piece in qkv_along]).astype(f32)
+    bias_in_rest = bias_rest[:, 0] + bias_rest[:, 1] + bias_rest[:, 2]
+    bias_head_rest = bias_rest[:, 3] + bias_rest[:, 4] + bias_rest[:, 5]
+    bias_in_all = jnp.concatenate([b_in[None], bias_in_rest])
+    bias_heads = jnp.concatenate(
+        [jnp.concatenate([b_query, b_value])[None], bias_head_rest[:, : 2 * inner]]
+    )
+    qkv_near, qkv_far = spread_at_once(jnp.stack([piece[: 3 * part] for piece in qkv_along]))
+    in_along = jnp.stack(along(in_piece))
+    back_along = jnp.stack(along(back_piece))
+
+    def in_order(parts):
+        split = parts.reshape(*parts.shape[:-2], 2, 2, 2, parts.shape[-1])
+        for axis, bit in ((-4, CORE), (-3, NEAR_Y), (-2, NEAR_X)):
+            split = jnp.where((data_index & bit) != 0, jnp.flip(split, axis), split)
+        return split.reshape(parts.shape)
+
+    bias_heads = in_order(bias_heads.reshape(ways, 2 * heads, PLANE, 8)).reshape(ways, 2, inner)
+    bias_query = bias_heads[:, 0].reshape(1, width)
+    bias_value = bias_heads[:, 1].reshape(1, width)
+    bias_in = in_order(bias_in_all.reshape(ways, PLANE, piece_rows))
     bias_in = bias_in.transpose(1, 0, 2).reshape(-1)
 
     low, high = segment_bounds(pass_len, mp_index * own_rows - halo, count)
@@ -330,20 +602,35 @@
     tiles = jnp.stack([tile_low, blocks, jnp.where(reach, blocks, 0)])
     bounds = (tiles, low[:, None], high[:, None])
 
-    window = halo_rows(tokens, halo)
-    queries = ((mm(window, attn_all[0], NT) + bias_query) * scale).astype(bf16)
-    keys = mm(window, attn_all[1], NT).astype(bf16)
-    values = (mm(window, attn_all[2], NT) + bias_value).astype(bf16)
-    context = attend_forward(bounds, queries[halo : halo + own_rows], keys, values, halo)
-    first_sum = tokens.astype(f32) + mm(context, attn_all[3]) + b_out
+    qkv = (tokens_before, tokens, tokens_after, qkv_own, qkv_near, qkv_far, bias_query, bias_value)
+    queries, keys, values, qkv_all = local(
+        project_kernel, place, qkv, [((count, width), bf16)] * 3 + [((3 * width, width), bf16)],
+        [((count, width), bf16), ((PLANE, 3 * part, width), f32)], 10, "project",
+    )
+    in_near = spread_x_first(in_along)
+    back_near = spread_y_first(back_along)
+    in_far = swap(in_near, CORE)
+    back_far = swap(back_near, CORE)
+    own_queries = queries[halo : halo + own_rows]
+    context = [attend_forward(bounds, own_queries, keys, values, halo, i, 2) for i in range(2)]
+    in_all, out_all = local(
+        join_in_out_kernel, place, (in_own, out_own, in_near, in_far),
+        [((ways * units, width), bf16), ((width, width), bf16)],
+        [((PLANE, part, width), f32)], 5, "join_in_out",
+    )
+    (back_all,) = local(
+        join_units_kernel, place, (back_own, back_near, back_far),
+        [((ways * units, width), bf16)], [], 4, "join_back",
+    )
+    attended = mm(context[0], out_all[: width // 2]) + mm(context[1], out_all[width // 2 :])
+    first_sum = tokens.astype(f32) + attended + b_out
     center_one, inverse_one = norm_parts(first_sum)
     unit_one = center_one * inverse_one
     hidden = unit_one * ln1_gain + ln1_shift
     hidden_low = hidden.astype(bf16)
 
     active, slope = gelu_both(mm(hidden_low, in_all, NT) + bias_in)
-    active = active.astype(bf16)
-    slope = slope.astype(bf16)
+    active, slope = lax.optimization_barrier((active.astype(bf16), slope.astype(bf16)))
     second_sum = hidden + mm(active, back_all) + b_back
     center_two, inverse_two = norm_parts(second_sum)
     unit_two = center_two * inverse_two
@@ -392,8 +679,24 @@
         jnp.sum(grad_second, axis=0),
     ]
     second_low = grad_second.astype(bf16)
-    grad_before = (mm(second_low, back_all, NT) * slope.astype(f32)).astype(bf16)
-    grad_hidden = grad_second + mm(grad_before, in_all)
+
+    def to_core(left, right):
+        return mm(left[:, left.shape[1] // 2 :], right, TN).astype(bf16)
+
+    def chip_sum(left, right, arrived):
+        own = mm(left[:, : left.shape[1] // 2], right, TN)
+        return add(own, arrived).reshape(2, 2, ways, piece_rows, width)
+
+    back_sent = to_core(active, second_low)
+    back_arrived = swap(back_sent, CORE)
+    pulled, back_sent = lax.optimization_barrier((second_low, back_sent))
+    grad_before = (mm(pulled, back_all, NT) * slope.astype(f32)).astype(bf16)
+    back_sum = chip_sum(active, second_low, back_arrived)
+    back_half = swap(back_sum[1], NEAR_Y)
+    in_sent = to_core(grad_before, hidden_low)
+    in_arrived = swap(in_sent, CORE)
+    pulled, in_sent = lax.optimization_barrier((grad_before, in_sent))
+    grad_hidden = grad_second + mm(pulled, in_all)
     grad_first = norm_pull(grad_hidden, unit_one, inverse_one, ln1_gain)
     stats += [
         jnp.sum(grad_hidden * unit_one, axis=0),
@@ -401,63 +704,93 @@
         jnp.sum(grad_first, axis=0),
     ]
     first_low = grad_first.astype(bf16)
-    first_window = halo_rows(first_low, halo)
-    d_back = mm(active, second_low, TN).astype(bf16)
-    d_in = mm(grad_before, hidden_low, TN).astype(bf16)
-    unit_rows = units // data_ways
-    back_sum = reduce_rows(d_back.reshape(data_ways, ways, unit_rows, width))
-    in_sum = reduce_rows(d_in.reshape(data_ways, ways, unit_rows, width))
-    d_b_in = jnp.sum(grad_before, axis=0, dtype=f32)
-    d_b_in = d_b_in.reshape(data_ways, ways, unit_rows).transpose(1, 0, 2).reshape(ways, units)
-
-    grad_context = mm(first_window, attn_all[3], NT).astype(bf16)
-    grad_queries, grad_keys, grad_values = attend_backward(
-        bounds, queries, keys, values, grad_context, halo
-    )
-    d_attn = jnp.stack(
-        [
-            mm(grad_queries, tokens, TN),
-            mm(grad_keys, tokens, TN),
-            mm(grad_values, tokens, TN),
-            mm(context, first_low, TN),
-        ]
-    ).astype(bf16)
-    d_attn = d_attn.reshape(4, ways, inner, width).transpose(1, 0, 2, 3)
-    d_attn = d_attn.reshape(ways, data_ways, 4 * inner // data_ways, width).transpose(1, 0, 2, 3)
-    attn_sum = reduce_rows(d_attn).astype(f32).reshape(4, inner, width)
-    d_b_query = jnp.sum(grad_queries, axis=0, dtype=f32)
-    d_b_value = jnp.sum(grad_values, axis=0, dtype=f32)
+    first_before, first_after = halo_rows(first_low, halo)
+    in_sum = chip_sum(grad_before, hidden_low, in_arrived)
+    in_half = swap(in_sum[:, 1], NEAR_X)
+    d_b_in = jnp.sum(grad_before, axis=0, dtype=f32).reshape(PLANE, ways, piece_rows)
+
+    d_b_in = in_order(d_b_in.transpose(1, 0, 2)).reshape(ways, 1, units)
+    turned = jnp.roll(jnp.stack(stats).reshape(6, ways, inner), -mp_index, axis=1).transpose(1, 0, 2)
+    turned = jnp.pad(turned.reshape(ways, -1), ((0, 0), (0, 2 * inner))).reshape(ways, 2, width)
+    vectors = jnp.concatenate([d_b_in, turned, jnp.zeros((ways, 5, width), f32)], axis=1)
+
+    first_window = jnp.concatenate([first_before, first_low, first_after])
+    grad_context = mm(first_window, out_all, NT).astype(bf16)
+    groups = 3
+    parts = []
+
+    def attend(grads, group):
+        return attend_backward(bounds, queries, keys, values, grads, halo, group, groups)
+
+    grad_context, back_half, vectors = lax.optimization_barrier((grad_context, back_half, vectors))
+    parts.append(attend(grad_context, 0))
+    back_sum = add(back_sum[0], back_half)
+    back_half = swap(back_sum[1], NEAR_X)
+    grad_context, in_half, _ = lax.optimization_barrier((grad_context, in_half, parts[0]))
+    parts.append(attend(grad_context, 1))
+    in_sum = add(in_sum[:, 0], in_half)
+    in_half = swap(in_sum[1], NEAR_Y)
+    grad_context, back_half, in_half, _ = lax.optimization_barrier(
+        (grad_context, back_half, in_half, parts[1])
+    )
+    parts.append(attend(grad_context, 2))
+    early_sum = jnp.concatenate([add(back_sum[0], back_half), add(in_sum[0], in_half)], axis=1)
+    early_own = sum_along([early_sum[i] for i in range(ways)]).astype(bf16)
+
+    grad_parts = [g[i] for i in range(3) for g in parts]
+    late_keep, late_sent = local(
+        functools.partial(piece_grads_kernel, groups), place,
+        (*grad_parts, *context, tokens, first_low, vectors),
+        [((4 * ways, 4 * part + 8, width), bf16)] * 2,
+        [((8 * ways, 4 * part + 8, width), f32)], 10, "piece_grads",
+    )
+    late_sum = add(late_keep, swap(late_sent, CORE)).reshape(4, ways, 4 * part + 8, width)
+    arrived = [swap(late_sum[j], bit) for j, bit in ((1, NEAR_X), (2, NEAR_Y), (3, NEAR_X | NEAR_Y))]
+    late_sum = sum((a.astype(f32) for a in arrived), late_sum[0].astype(f32)).astype(bf16)
+    late_total = sum_along([late_sum[i] for i in range(ways)])
+    late_near, late_far = spread_at_once(late_total[: 4 * part].astype(bf16))
+    line = late_total[4 * part :]
+    back_near = spread_x_first(early_own[:piece_rows])
+    in_near = spread_y_first(early_own[piece_rows:])
+    early_far = swap(jnp.stack([back_near, in_near]), CORE)
+    grad_queries, grad_keys, grad_values = (jnp.concatenate(p, axis=1) for p in zip(*parts))
     d_tokens = (
         grad_first
-        + mm(grad_queries, attn_all[0])
-        + mm(grad_keys, attn_all[1])
-        + mm(grad_values, attn_all[2])
-    )
-
-    vectors = [v.reshape(ways, -1) for v in [*stats, d_b_query, d_b_value]] + [d_b_in]
-    vectors = lax.psum(jnp.concatenate(vectors, axis=1), ("dp", "mp"))
-    vectors = lax.dynamic_index_in_dim(vectors, mp_index, 0, keepdims=False)
-    part = width // ways
-    pieces = [vectors[i * part : (i + 1) * part] for i in range(8)]
+        + mm(grad_queries, qkv_all[:width])
+        + mm(grad_keys, qkv_all[width : 2 * width])
+        + mm(grad_values, qkv_all[2 * width :])
+    )
+
+    d_query, d_key, d_value, d_out = local(
+        finish_heads_kernel, place, (late_near, late_far),
+        [((inner, width), f32)] * 4,
+        [((PLANE, 4 * part, width), f32)], 5, "finish_heads",
+    )
+    d_back, d_in = local(
+        finish_units_kernel, place, (back_near, early_far[0], in_near, early_far[1]),
+        [((units, width), f32), ((width, units), f32)],
+        [((PLANE, piece_rows, width), f32), ((units, width), f32)], 6, "finish_units",
+    )
+    norms = [line[1 + i // ways, i % ways * inner : (i % ways + 1) * inner] for i in range(8)]
     return (
         mixed,
         query_losses,
         d_tokens,
-        attn_sum[0].T,
-        attn_sum[1].T,
-        attn_sum[2].T,
-        pieces[6],
-        pieces[7],
-        attn_sum[3],
-        pieces[5],
-        pieces[3],
-        pieces[4],
-        in_sum.astype(f32).T,
-        vectors[8 * part :],
-        back_sum.astype(f32),
-        pieces[2],
-        pieces[0],
-        pieces[1],
+        d_query.T,
+        d_key.T,
+        d_value.T,
+        norms[6],
+        norms[7],
+        d_out,
+        norms[5],
+        norms[3],
+        norms[4],
+        d_in,
+        line[0],
+        d_back,
+        norms[2],
+        norms[0],
+        norms[1],
     )
 
 

time: 709 us -> 449 us (0.63)
  waiting for transfers between devices: 388 us -> 135 us
  starting transfers between devices: 23.3 us -> 86.6 us
  blocking collectives: 41.2 us -> 0 us
  matrix products: 93.6 us -> 55 us
  Pallas kernels: 68.9 us -> 90.8 us
  between operations: 15.2 us -> 2.59 us
  other arithmetic: 19.7 us -> 31.5 us
    reduce_scatter x3 -> x0, waiting for transfers between devices: 233 us -> none  [reduce_rows(): lax.psum_scatter(grads.reshape(data_ways * ways * rows, width), ('dp', 'm...]
    all_gather x6 -> x0, waiting for transfers between devices: 135 us -> none  [the longest x3 123 us: gather_rows(): full = lax.all_gather(own, ('dp', 'mp'), axis=0, tiled=True)]
    ppermute x3 -> x44, waiting for transfers between devices: 0.01 us -> 123 us  [the longest x29 75.5 us: swap(): return lax.ppermute(values, 'dp', [(i, i ^ bit) for i in range(ways)])]
    ppermute x3 -> x44, starting transfers between devices: 4.6 us -> 56.4 us  [the longest x29 32.9 us: swap(): return lax.ppermute(values, 'dp', [(i, i ^ bit) for i in range(ways)])]
    psum x1 -> x0, blocking collectives: 41.2 us -> none  [shards(): vectors = lax.psum(jnp.concatenate(vectors, axis=1), ('dp', 'mp'))]
    dot_general x20 -> x16, matrix products: 87.4 us -> 50.4 us  [mm(): return lax.dot_general(a, b, dims, preferred_element_type=f32)]
    pallas_call x2 -> x13, Pallas kernels: 68.9 us -> 90.8 us  [the longest x3 43.4 us: attend_backward(): pl.pallas_call(functools.partial(backward_kernel, halo), grid=(1,), out_s...]
    another operation x1 -> x15, other arithmetic: 0.64 us -> 15.9 us  [the longest x4 4.29 us: spread_x_first(): return jnp.stack([both, swap(both, NEAR_Y)]).reshape(4, *values.shape)]
  transfers between devices with their start and end apart: 22 -> 54, of which waited for: 16 -> 22; matrix products, arithmetic and copies ran while one was open for 15% -> 17% of each run, Pallas kernels for 10% -> 14%
where the time goes in v2:
time: 449 us; the launch traced here: 443 us
  waiting for transfers between devices  135 us (30%)
  Pallas kernels  90.8 us (20%)
  starting transfers between devices  86.6 us (19%)
  matrix products  55 us (12%)
  local copies, waits for them, and re-layouts  41.7 us (9%)
  other arithmetic  31.5 us (7%)
    ppermute x29, waiting for transfers between devices, swap(): return lax.ppermute(values, 'dp', [(i, i ^ bit) for i in range(ways)])  75.5 us
    dot_general x16, matrix products, mm(): return lax.dot_general(a, b, dims, preferred_element_type=f32)  50.4 us
    pallas_call x3, Pallas kernels, attend_backward(): pl.pallas_call(functools.partial(backward_kernel, halo), grid=(1,), out_s...  43.4 us
    ppermute x6, waiting for transfers between devices, sum_along(): lax.ppermute(parts[step], 'mp', turn(ways, -step)).astype(f32)  36.6 us
    ppermute x29, starting transfers between devices, swap(): return lax.ppermute(values, 'dp', [(i, i ^ bit) for i in range(ways)])  32.9 us
    pallas_call x8, Pallas kernels, local(): pl.pallas_call(kernel, out_shape=tuple((jax.ShapeDtypeStruct(shape, dtype...  31 us
    ppermute x2, starting transfers between devices, halo_rows(): lax.ppermute(values[-halo:], 'mp', [(i, i + 1) for i in range(ways - 1)])  18.8 us
    unnamed x149, local copies, waits for them, and re-layouts  17.3 us
  transfers between devices with their start and end apart: 54, of which 22 were waited for; matrix products, arithmetic and copies ran while one was open for 17% of the time, Pallas kernels for 14%

profile of v2, /device:TPU:1, one launch (start us, length us, event | category | flops | bytes accessed | tf_op | source)
XLA Modules:
  0.0 443.0 jit_solution(12665609826579178214)
XLA Ops:
  42.7 6.9 %collective-permute-done.10 = bf16[120,768]{1,0:T(8,128)(2,1)} collective-permute-done((bf16[120,768]{1,0:T(8,128)(2,1)}, bf16[120,768]{1,0:T(8,128)(2,1)}, u32[]{:S(2)}, u32[]{:S(2)}) %collective-permute-start.10) | collective-permute-done | bytes 184352 | tf_op jit(solution)/shard_map/ppermute | solution.py:489
  66.5 4.5 %collective-permute-done.7 = bf16[3,72,768]{2,1,0:T(8,128)(2,1)S(1)} collective-permute-done((bf16[3,72,768]{2,1,0:T(8,128)(2,1)S(1)}, bf16[3,72,768]{2,1,0:T(8,128)(2,1)S(1)}, u32[]{:S(2)}, u32[]{:S(2)}) %collective-permute-start.7) | collective-permute-done | bytes 331808 | tf_op jit(solution)/shard_map/ppermute | solution.py:484
  71.0 13.8 %collective-permute-start = (bf16[256,768]{1,0:T(8,128)(2,1)}, bf16[256,768]{1,0:T(8,128)(2,1)}, u32[]{:S(2)}, u32[]{:S(2)}) collective-permute-start(bf16[256,768]{1,0:T(8,128)(2,1)} %get-tuple-element.162), channel_id=1, source_target_pairs={{0,1},{1,2},{2,3},{4,5},{5,6},{6,7},{8,9},{9,10},{10,11},{12,13},{... | collective-permute-start | bytes 1179656 | tf_op jit(solution)/shard_map/ppermute | solution.py:455
  104.1 14.0 %collective-permute-done.19 = bf16[2,3,96,768]{3,2,1,0:T(8,128)(2,1)} collective-permute-done((bf16[2,3,96,768]{3,2,1,0:T(8,128)(2,1)}, bf16[2,3,96,768]{3,2,1,0:T(8,128)(2,1)}, u32[]{:S(2)}, u32[]{:S(2)}) %collective-permute-start.19) | collective-permute-done | bytes 884768 | tf_op jit(solution)/shard_map/ppermute | solution.py:484
  123.6 10.5 %project.1 = (bf16[1280,768]{1,0:T(8,128)(2,1)}, bf16[1280,768]{1,0:T(8,128)(2,1)}, bf16[1280,768]{1,0:T(8,128)(2,1)}, bf16[2304,768]{1,0:T(8,128)(2,1)}) custom-call(s32[1]{0:T(128)} %bitcast.3.place_ref, bf16[256,768]{1,0:T(8,128)(2,1)} %collective-permute-done.left_ref, bf16[768,768]{1,0:T(8,128)(2,1)S(1)} %copy-done, ...), custom_call_target="tpu_custom_call" | custom-call | flops 10000000000 | bytes 35000000 | tf_op jit(solution)/shard_map/project/pallas_call | solution.py:247
  138.6 8.0 %attend_forward.3.refs_10_ = bf16[768,384]{1,0:T(8,128)(2,1)S(1)} custom-call(s32[3,10]{1,0:T(4,128)S(1)} %pad_add_fusion.tiles_ref, s32[1280,1]{1,0:T(8,128)S(1)} %copy-done.2, s32[1280,1]{1,0:T(8,128)S(1)} %get-tuple-element.217.hi_ref, bf16[768,768]{1,0:T(8,128)(2,1)S(1)} %slice.311.q_ref, bf16[1280,768]{1,0:T(8,128)(2,1)S(1)} %copy-done.20, ...), custom_call_target="tpu_custom_call" | custom-call | flops 8999999488 | bytes 31500000 | tf_op jit(solution)/shard_map/attend_forward/pallas_call | solution.py:152
  146.7 8.3 %attend_forward.2.refs_9_ = bf16[768,384]{1,0:T(8,128)(2,1)S(1)} custom-call(s32[3,10]{1,0:T(4,128)S(1)} %pad_add_fusion.tiles_ref, s32[1280,1]{1,0:T(8,128)S(1)} %copy-done.2, s32[1280,1]{1,0:T(8,128)S(1)} %get-tuple-element.217.hi_ref, bf16[768,768]{1,0:T(8,128)(2,1)S(1)} %slice.311.q_ref, bf16[1280,768]{1,0:T(8,128)(2,1)S(1)} %copy-done.20, ...), custom_call_target="tpu_custom_call" | custom-call | flops 8999999488 | bytes 31500000 | tf_op jit(solution)/shard_map/attend_forward/pallas_call | solution.py:152
  164.8 9.4 %fusion.4 = (bf16[768,3072]{1,0:T(8,128)(2,1)}, bf16[768,3072]{1,0:T(8,128)(2,1)S(1)}) fusion(f32[3072]{0:T(1024)S(1)} %add.313, bf16[768,768]{1,0:T(8,128)(2,1)S(1)} %fusion.17, bf16[3072,768]{1,0:T(8,128)(2,1)S(1)} %bitcast.237), kind=kOutput, calls=%fused_computation.5 | convolution fusion | flops 3652190208 | bytes 15347712 | tf_op jit(solution)/shard_map/dot_general | solution.py:30
  196.5 4.5 %collective-permute-done.26 = bf16[4,32,768]{2,1,0:T(8,128)(2,1)S(1)} collective-permute-done((bf16[4,32,768]{2,1,0:T(8,128)(2,1)S(1)}, bf16[4,32,768]{2,1,0:T(8,128)(2,1)S(1)}, u32[]{:S(2)}, u32[]{:S(2)}) %collective-permute-start.26) | collective-permute-done | bytes 196640 | tf_op jit(solution)/shard_map/ppermute | solution.py:470
  223.4 6.7 %multiply_reduce_fusion = (f32[768]{0:T(1024)S(1)}, f32[768]{0:T(1024)S(1)}, f32[768]{0:T(1024)S(1)}, f32[768]{0:T(1024)S(1)}, f32[768,768]{1,0:T(8,128)S(1)}) fusion(f32[768,768]{1,0:T(8,128)S(1)} %copy-done.25, f32[768]{0:T(1024)S(1)} %add_rsqrt_fusion.1, f32[768]{0:T(1024)S(1)} %broadcast_multiply_fusion.5, f32[768]{0:T(1024)S(1)} %copy-done.48, ...), kind=kOutput, calls=%fused_computation.24 | convolution fusion | flops 3629773824 | bytes 16536576 | tf_op jit(solution)/shard_map/dot_general | solution.py:30
  234.3 4.9 %collective-permute-start.27 = (bf16[256,768]{1,0:T(8,128)(2,1)}, bf16[256,768]{1,0:T(8,128)(2,1)}, u32[]{:S(2)}, u32[]{:S(2)}) collective-permute-start(bf16[256,768]{1,0:T(8,128)(2,1)} %get-tuple-element.159), channel_id=1, source_target_pairs={{0,1},{1,2},{2,3},{4,5},{5,6},{6,7},{8,9},{9,10},{10,11},{12,13},{... | collective-permute-start | bytes 1179656 | tf_op jit(solution)/shard_map/ppermute | solution.py:455
  240.3 4.8 %add_convert_fusion.2 = bf16[1536,768]{1,0:T(8,128)(2,1)S(1)} fusion(bf16[1536,768]{1,0:T(8,128)(2,1)} %collective-permute-done.29, bf16[768,768]{1,0:T(8,128)(2,1)} %copy-done.39, bf16[768,3072]{1,0:T(8,128)(2,1)} %copy-done.59), kind=kOutput, calls=%fused_computation.12 | convolution fusion | flops 1815478272 | bytes 8257536 | tf_op jit(solution)/shard_map/dot_general | solution.py:30
  255.5 16.9 %collective-permute-done.30 = bf16[2,4,96,768]{3,2,1,0:T(8,128)(2,1)S(1)} collective-permute-done((bf16[2,4,96,768]{3,2,1,0:T(8,128)(2,1)S(1)}, bf16[2,4,96,768]{3,2,1,0:T(8,128)(2,1)S(1)}, u32[]{:S(2)}, u32[]{:S(2)}) %collective-permute-start.30) | collective-permute-done | bytes 1179680 | tf_op jit(solution)/shard_map/ppermute | solution.py:484
  272.4 14.5 %attend_backward.3 = (bf16[768,256]{1,0:T(8,128)(2,1)S(1)}, bf16[768,256]{1,0:T(8,128)(2,1)S(1)}, bf16[768,256]{1,0:T(8,128)(2,1)S(1)}) custom-call(s32[3,10]{1,0:T(4,128)S(1)} %pad_add_fusion.tiles_ref, s32[1280,1]{1,0:T(8,128)S(1)} %copy-done.3, s32[1280,1]{1,0:T(8,128)S(1)} %get-tuple-element.217.hi_ref, bf16[1280,768]{1,0:T(8,128)(2,1)S(1)} %copy-done.1, ...), custom_call_target="tpu_custom_call" | custom-call | flops 14000000000 | bytes 49000000 | tf_op jit(solution)/shard_map/attend_backward/pallas_call | solution.py:223
  291.7 14.3 %attend_backward.4 = (bf16[768,256]{1,0:T(8,128)(2,1)S(1)}, bf16[768,256]{1,0:T(8,128)(2,1)S(1)}, bf16[768,256]{1,0:T(8,128)(2,1)S(1)}) custom-call(s32[3,10]{1,0:T(4,128)S(1)} %pad_add_fusion.tiles_ref, s32[1280,1]{1,0:T(8,128)S(1)} %copy-done.3, s32[1280,1]{1,0:T(8,128)S(1)} %get-tuple-element.217.hi_ref, bf16[1280,768]{1,0:T(8,128)(2,1)S(1)} %copy-done.1, ...), custom_call_target="tpu_custom_call" | custom-call | flops 14000000000 | bytes 49000000 | tf_op jit(solution)/shard_map/attend_backward/pallas_call | solution.py:223
  306.1 14.6 %attend_backward.5 = (bf16[768,256]{1,0:T(8,128)(2,1)S(1)}, bf16[768,256]{1,0:T(8,128)(2,1)S(1)}, bf16[768,256]{1,0:T(8,128)(2,1)S(1)}) custom-call(s32[3,10]{1,0:T(4,128)S(1)} %pad_add_fusion.tiles_ref, s32[1280,1]{1,0:T(8,128)S(1)} %copy-done.3, s32[1280,1]{1,0:T(8,128)S(1)} %get-tuple-element.217.hi_ref, bf16[1280,768]{1,0:T(8,128)(2,1)S(1)} %copy-done.1, ...), custom_call_target="tpu_custom_call" | custom-call | flops 14000000000 | bytes 49000000 | tf_op jit(solution)/shard_map/attend_backward/pallas_call | solution.py:223
  320.7 8.5 %piece_grads.1 = (bf16[16,104,768]{2,1,0:T(8,128)(2,1)}, bf16[16,104,768]{2,1,0:T(8,128)(2,1)}) custom-call(s32[1]{0:T(128)} %bitcast.3.place_ref, bf16[768,256]{1,0:T(8,128)(2,1)S(1)} %get-tuple-element.99.refs_0_, bf16[768,256]{1,0:T(8,128)(2,1)S(1)} %get-tuple-element.103.refs_1_, bf16[768,256]{1,0:T(8,128)(2,1)S(1)} %get-tuple-element.109.refs_2_, ...), custom_call_target="tpu_custom_call" | custom-call | flops 10000000000 | bytes 35000000 | tf_op jit(solution)/shard_map/piece_grads/pallas_call | solution.py:247
  333.1 6.4 %collective-permute-start.47 = (bf16[192,768]{1,0:T(8,128)(2,1)S(1)}, bf16[192,768]{1,0:T(8,128)(2,1)S(1)}, u32[]{:S(2)}, u32[]{:S(2)}) collective-permute-start(bf16[192,768]{1,0:T(8,128)(2,1)S(1)} %get-tuple-element.158), channel_id=1, source_target_pairs={{0,2},{1,3},{2,0},{3,1},{4,6},{5,7},{6,4},{7,5},{8,10},{9,11},{10,... | collective-permute-start | bytes 884744 | tf_op jit(solution)/shard_map/ppermute | solution.py:517
  343.2 22.6 %collective-permute-done.47 = bf16[192,768]{1,0:T(8,128)(2,1)S(1)} collective-permute-done((bf16[192,768]{1,0:T(8,128)(2,1)S(1)}, bf16[192,768]{1,0:T(8,128)(2,1)S(1)}, u32[]{:S(2)}, u32[]{:S(2)}) %collective-permute-start.47) | collective-permute-done | bytes 294944 | tf_op jit(solution)/shard_map/ppermute | solution.py:517
  373.2 4.8 %collective-permute-done.50 = bf16[2,96,768]{2,1,0:T(8,128)(2,1)S(1)} collective-permute-done((bf16[2,96,768]{2,1,0:T(8,128)(2,1)S(1)}, bf16[2,96,768]{2,1,0:T(8,128)(2,1)S(1)}, u32[]{:S(2)}, u32[]{:S(2)}) %collective-permute-start.50) | collective-permute-done | bytes 294944 | tf_op jit(solution)/shard_map/ppermute | solution.py:484
  388.1 9.0 %collective-permute-done.38 = bf16[4,104,768]{2,1,0:T(8,128)(2,1)S(1)} collective-permute-done((bf16[4,104,768]{2,1,0:T(8,128)(2,1)S(1)}, bf16[4,104,768]{2,1,0:T(8,128)(2,1)S(1)}, u32[]{:S(2)}, u32[]{:S(2)}) %collective-permute-start.38) | collective-permute-done | bytes 639008 | tf_op jit(solution)/shard_map/ppermute | solution.py:484
  397.1 15.4 %collective-permute-done.37 = bf16[4,104,768]{2,1,0:T(8,128)(2,1)S(1)} collective-permute-done((bf16[4,104,768]{2,1,0:T(8,128)(2,1)S(1)}, bf16[4,104,768]{2,1,0:T(8,128)(2,1)S(1)}, u32[]{:S(2)}, u32[]{:S(2)}) %collective-permute-start.37) | collective-permute-done | bytes 639008 | tf_op jit(solution)/shard_map/ppermute | solution.py:484
  414.5 4.7 %collective-permute-done.41 = bf16[104,768]{1,0:T(8,128)(2,1)S(1)} collective-permute-done((bf16[104,768]{1,0:T(8,128)(2,1)S(1)}, bf16[104,768]{1,0:T(8,128)(2,1)S(1)}, u32[]{:S(2)}, u32[]{:S(2)}) %collective-permute-start.41) | collective-permute-done | bytes 159776 | tf_op jit(solution)/shard_map/ppermute | solution.py:517
  419.2 7.0 %collective-permute-done.40 = bf16[104,768]{1,0:T(8,128)(2,1)S(1)} collective-permute-done((bf16[104,768]{1,0:T(8,128)(2,1)S(1)}, bf16[104,768]{1,0:T(8,128)(2,1)S(1)}, u32[]{:S(2)}, u32[]{:S(2)}) %collective-permute-start.40) | collective-permute-done | bytes 159776 | tf_op jit(solution)/shard_map/ppermute | solution.py:517
  (430 shorter events, 205.3 us)
Async XLA Ops:
  35.3 21.3 %collective-permute-start.17 = (bf16[96,768]{1,0:T(8,128)(2,1)}, bf16[96,768]{1,0:T(8,128)(2,1)}, u32[]{:S(2)}, u32[]{:S(2)}) collective-permute-start(bf16[96,768]{1,0:T(8,128)(2,1)} %get-tuple-element.94), channel_id=1, source_target_pairs={{0,1},{1,2},{2,3},{3,0},{4,5},{5,6},{6,7},{7,4},{8,9},{9,10},{10,1... | collective-permute-start | bytes 442376 | tf_op jit(solution)/shard_map/ppermute | solution.py:489
  35.6 25.4 %collective-permute-start.16 = (bf16[96,768]{1,0:T(8,128)(2,1)}, bf16[96,768]{1,0:T(8,128)(2,1)}, u32[]{:S(2)}, u32[]{:S(2)}) collective-permute-start(bf16[96,768]{1,0:T(8,128)(2,1)} %get-tuple-element.94), channel_id=1, source_target_pairs={{0,2},{1,3},{2,0},{3,1},{4,6},{5,7},{6,4},{7,5},{8,10},{9,11},{10,... | collective-permute-start | bytes 442376 | tf_op jit(solution)/shard_map/ppermute | solution.py:489
  41.2 21.1 %collective-permute-start.15 = (bf16[96,768]{1,0:T(8,128)(2,1)}, bf16[96,768]{1,0:T(8,128)(2,1)}, u32[]{:S(2)}, u32[]{:S(2)}) collective-permute-start(bf16[96,768]{1,0:T(8,128)(2,1)} %get-tuple-element.94), channel_id=1, source_target_pairs={{0,3},{1,0},{2,1},{3,2},{4,7},{5,4},{6,5},{7,6},{8,11},{9,8},{10,9... | collective-permute-start | bytes 442376 | tf_op jit(solution)/shard_map/ppermute | solution.py:489
  51.7 39.7 %collective-permute-start.12 = (bf16[3,120,768]{2,1,0:T(8,128)(2,1)}, bf16[3,120,768]{2,1,0:T(8,128)(2,1)}, u32[]{:S(2)}, u32[]{:S(2)}) collective-permute-start(bf16[3,120,768]{2,1,0:T(8,128)(2,1)} %get-tuple-element.171), channel_id=1, source_target_pairs={{0,8},{4,12},{8,0},{12,4},{16,24},{20,28},{24,16},{28,20},{1,9},{5... | collective-permute-start | bytes 1658888 | tf_op jit(solution)/shard_map/ppermute | solution.py:484
  56.6 28.2 %collective-permute-start.6 = (bf16[3,72,768]{2,1,0:T(8,128)(2,1)S(1)}, bf16[3,72,768]{2,1,0:T(8,128)(2,1)S(1)}, u32[]{:S(2)}, u32[]{:S(2)}) collective-permute-start(bf16[3,72,768]{2,1,0:T(8,128)(2,1)S(1)} %get-tuple-element.177), channel_id=1, source_target_pairs={{0,16},{4,20},{8,24},{12,28},{16,0},{20,4},{24,8},{28,12},{1,17},{... | collective-permute-start | bytes 995336 | tf_op jit(solution)/shard_map/ppermute | solution.py:484
  61.1 25.3 %collective-permute-start.5 = (bf16[3,72,768]{2,1,0:T(8,128)(2,1)S(1)}, bf16[3,72,768]{2,1,0:T(8,128)(2,1)S(1)}, u32[]{:S(2)}, u32[]{:S(2)}) collective-permute-start(bf16[3,72,768]{2,1,0:T(8,128)(2,1)S(1)} %get-tuple-element.177), channel_id=1, source_target_pairs={{0,8},{4,12},{8,0},{12,4},{16,24},{20,28},{24,16},{28,20},{1,9},{5... | collective-permute-start | bytes 995336 | tf_op jit(solution)/shard_map/ppermute | solution.py:484
  64.3 30.1 %collective-permute-start.18 = (bf16[3,96,768]{2,1,0:T(8,128)(2,1)}, bf16[3,96,768]{2,1,0:T(8,128)(2,1)}, u32[]{:S(2)}, u32[]{:S(2)}) collective-permute-start(bf16[3,96,768]{2,1,0:T(8,128)(2,1)} %get-tuple-element.173), channel_id=1, source_target_pairs={{0,16},{4,20},{8,24},{12,28},{16,0},{20,4},{24,8},{28,12},{1,17},{... | collective-permute-start | bytes 1327112 | tf_op jit(solution)/shard_map/ppermute | solution.py:484
  71.0 52.6 %collective-permute-start = (bf16[256,768]{1,0:T(8,128)(2,1)}, bf16[256,768]{1,0:T(8,128)(2,1)}, u32[]{:S(2)}, u32[]{:S(2)}) collective-permute-start(bf16[256,768]{1,0:T(8,128)(2,1)} %get-tuple-element.162), channel_id=1, source_target_pairs={{0,1},{1,2},{2,3},{4,5},{5,6},{6,7},{8,9},{9,10},{10,11},{12,13},{... | collective-permute-start | bytes 1179656 | tf_op jit(solution)/shard_map/ppermute | solution.py:455
  84.9 38.7 %collective-permute-start.1 = (bf16[256,768]{1,0:T(8,128)(2,1)}, bf16[256,768]{1,0:T(8,128)(2,1)}, u32[]{:S(2)}, u32[]{:S(2)}) collective-permute-start(bf16[256,768]{1,0:T(8,128)(2,1)} %get-tuple-element.161), channel_id=1, source_target_pairs={{1,0},{2,1},{3,2},{5,4},{6,5},{7,6},{9,8},{10,9},{11,10},{13,12},{... | collective-permute-start | bytes 1179656 | tf_op jit(solution)/shard_map/ppermute | solution.py:456
  88.6 35.0 %collective-permute-start.8 = (bf16[4,3,72,768]{3,2,1,0:T(8,128)(2,1)S(1)}, bf16[4,3,72,768]{3,2,1,0:T(8,128)(2,1)}, u32[]{:S(2)}, u32[]{:S(2)}) collective-permute-start(bf16[4,3,72,768]{3,2,1,0:T(8,128)(2,1)S(1)} %pad_maximum_fusion.2.near_ref), channel_id=1, source_target_pairs={{0,4},{4,0},{8,12},{12,8},{16,20},{20,16},{24,28},{28,24},{1,5},{5... | collective-permute-start | bytes 3981320 | tf_op jit(solution)/shard_map/ppermute | solution.py:484
  94.2 26.8 %collective-permute-start.13 = (bf16[2,3,120,768]{3,2,1,0:T(8,128)(2,1)}, bf16[2,3,120,768]{3,2,1,0:T(8,128)(2,1)}, u32[]{:S(2)}, u32[]{:S(2)}) collective-permute-start(bf16[2,3,120,768]{3,2,1,0:T(8,128)(2,1)} %get-tuple-element.164), channel_id=1, source_target_pairs={{0,16},{4,20},{8,24},{12,28},{16,0},{20,4},{24,8},{28,12},{1,17},{... | collective-permute-start | bytes 3317768 | tf_op jit(solution)/shard_map/ppermute | solution.py:484
  96.8 21.2 %collective-permute-start.19 = (bf16[2,3,96,768]{3,2,1,0:T(8,128)(2,1)}, bf16[2,3,96,768]{3,2,1,0:T(8,128)(2,1)}, u32[]{:S(2)}, u32[]{:S(2)}) collective-permute-start(bf16[2,3,96,768]{3,2,1,0:T(8,128)(2,1)} %get-tuple-element.166), channel_id=1, source_target_pairs={{0,8},{4,12},{8,0},{12,4},{16,24},{20,28},{24,16},{28,20},{1,9},{5... | collective-permute-start | bytes 2654216 | tf_op jit(solution)/shard_map/ppermute | solution.py:484
  119.8 35.2 %collective-permute-start.20 = (bf16[4,3,96,768]{3,2,1,0:T(8,128)(2,1)S(1)}, bf16[4,3,96,768]{3,2,1,0:T(8,128)(2,1)S(1)}, u32[]{:S(2)}, u32[]{:S(2)}) collective-permute-start(bf16[4,3,96,768]{3,2,1,0:T(8,128)(2,1)S(1)} %bitcast.188), channel_id=1, source_target_pairs={{0,4},{4,0},{8,12},{12,8},{16,20},{20,16},{24,28},{28,24},{1,5},{5... | collective-permute-start | bytes 5308424 | tf_op jit(solution)/shard_map/ppermute | solution.py:484
  122.5 35.1 %collective-permute-start.14 = (bf16[4,3,120,768]{3,2,1,0:T(8,128)(2,1)S(1)}, bf16[4,3,120,768]{3,2,1,0:T(8,128)(2,1)}, u32[]{:S(2)}, u32[]{:S(2)}) collective-permute-start(bf16[4,3,120,768]{3,2,1,0:T(8,128)(2,1)S(1)} %bitcast.186), channel_id=1, source_target_pairs={{0,4},{4,0},{8,12},{12,8},{16,20},{20,16},{24,28},{28,24},{1,5},{5... | collective-permute-start | bytes 6635528 | tf_op jit(solution)/shard_map/ppermute | solution.py:484
  212.6 27.7 %collective-permute-start.29 = (bf16[1536,768]{1,0:T(8,128)(2,1)}, bf16[1536,768]{1,0:T(8,128)(2,1)}, u32[]{:S(2)}, u32[]{:S(2)}) collective-permute-start(bf16[1536,768]{1,0:T(8,128)(2,1)} %convolution_convert_fusion.1), channel_id=1, source_target_pairs={{0,4},{4,0},{8,12},{12,8},{16,20},{20,16},{24,28},{28,24},{1,5},{5... | collective-permute-start | bytes 7077896 | tf_op jit(solution)/shard_map/ppermute | solution.py:484
  222.2 27.9 %collective-permute-start.31 = (bf16[1536,768]{1,0:T(8,128)(2,1)}, bf16[1536,768]{1,0:T(8,128)(2,1)}, u32[]{:S(2)}, u32[]{:S(2)}) collective-permute-start(bf16[1536,768]{1,0:T(8,128)(2,1)} %convolution_convert_fusion), channel_id=1, source_target_pairs={{0,4},{4,0},{8,12},{12,8},{16,20},{20,16},{24,28},{28,24},{1,5},{5... | collective-permute-start | bytes 7077896 | tf_op jit(solution)/shard_map/ppermute | solution.py:484
  245.3 27.0 %collective-permute-start.30 = (bf16[2,4,96,768]{3,2,1,0:T(8,128)(2,1)S(1)}, bf16[2,4,96,768]{3,2,1,0:T(8,128)(2,1)S(1)}, u32[]{:S(2)}, u32[]{:S(2)}) collective-permute-start(bf16[2,4,96,768]{3,2,1,0:T(8,128)(2,1)S(1)} %bitcast.196), channel_id=1, source_target_pairs={{0,16},{4,20},{8,24},{12,28},{16,0},{20,4},{24,8},{28,12},{1,17},{... | collective-permute-start | bytes 3538952 | tf_op jit(solution)/shard_map/ppermute | solution.py:484
  254.2 32.7 %collective-permute-start.32 = (bf16[2,4,96,768]{3,2,1,0:T(8,128)(2,1)S(1)}, bf16[2,4,96,768]{3,2,1,0:T(8,128)(2,1)S(1)}, u32[]{:S(2)}, u32[]{:S(2)}) collective-permute-start(bf16[2,4,96,768]{3,2,1,0:T(8,128)(2,1)S(1)} %slice_bitcast_fusion.1), channel_id=1, source_target_pairs={{0,8},{4,12},{8,0},{12,4},{16,24},{20,28},{24,16},{28,20},{1,9},{5... | collective-permute-start | bytes 3538952 | tf_op jit(solution)/shard_map/ppermute | solution.py:484
  329.2 51.6 %collective-permute-start.35 = (bf16[16,104,768]{2,1,0:T(8,128)(2,1)}, bf16[16,104,768]{2,1,0:T(8,128)(2,1)S(1)}, u32[]{:S(2)}, u32[]{:S(2)}) collective-permute-start(bf16[16,104,768]{2,1,0:T(8,128)(2,1)} %get-tuple-element.115), channel_id=1, source_target_pairs={{0,4},{4,0},{8,12},{12,8},{16,20},{20,16},{24,28},{28,24},{1,5},{5... | collective-permute-start | bytes 7667720 | tf_op jit(solution)/shard_map/ppermute | solution.py:484
  333.1 32.6 %collective-permute-start.47 = (bf16[192,768]{1,0:T(8,128)(2,1)S(1)}, bf16[192,768]{1,0:T(8,128)(2,1)S(1)}, u32[]{:S(2)}, u32[]{:S(2)}) collective-permute-start(bf16[192,768]{1,0:T(8,128)(2,1)S(1)} %get-tuple-element.158), channel_id=1, source_target_pairs={{0,2},{1,3},{2,0},{3,1},{4,6},{5,7},{6,4},{7,5},{8,10},{9,11},{10,... | collective-permute-start | bytes 884744 | tf_op jit(solution)/shard_map/ppermute | solution.py:517
  339.5 26.3 %collective-permute-start.46 = (bf16[192,768]{1,0:T(8,128)(2,1)S(1)}, bf16[192,768]{1,0:T(8,128)(2,1)S(1)}, u32[]{:S(2)}, u32[]{:S(2)}) collective-permute-start(bf16[192,768]{1,0:T(8,128)(2,1)S(1)} %get-tuple-element.156), channel_id=1, source_target_pairs={{0,1},{1,2},{2,3},{3,0},{4,5},{5,6},{6,7},{7,4},{8,9},{9,10},{10,1... | collective-permute-start | bytes 884744 | tf_op jit(solution)/shard_map/ppermute | solution.py:517
  378.3 36.1 %collective-permute-start.53 = (bf16[2,4,96,768]{3,2,1,0:T(8,128)(2,1)S(1)}, bf16[2,4,96,768]{3,2,1,0:T(8,128)(2,1)S(1)}, u32[]{:S(2)}, u32[]{:S(2)}) collective-permute-start(bf16[2,4,96,768]{3,2,1,0:T(8,128)(2,1)S(1)} %pad_maximum_fusion.3), channel_id=1, source_target_pairs={{0,4},{4,0},{8,12},{12,8},{16,20},{20,16},{24,28},{28,24},{1,5},{5... | collective-permute-start | bytes 3538952 | tf_op jit(solution)/shard_map/ppermute | solution.py:484
  383.1 29.4 %collective-permute-start.37 = (bf16[4,104,768]{2,1,0:T(8,128)(2,1)S(1)}, bf16[4,104,768]{2,1,0:T(8,128)(2,1)S(1)}, u32[]{:S(2)}, u32[]{:S(2)}) collective-permute-start(bf16[4,104,768]{2,1,0:T(8,128)(2,1)S(1)} %get-tuple-element.151), channel_id=1, source_target_pairs={{0,16},{4,20},{8,24},{12,28},{16,0},{20,4},{24,8},{28,12},{1,17},{... | collective-permute-start | bytes 1916936 | tf_op jit(solution)/shard_map/ppermute | solution.py:484
  383.8 28.7 %collective-permute-start.36 = (bf16[4,104,768]{2,1,0:T(8,128)(2,1)S(1)}, bf16[4,104,768]{2,1,0:T(8,128)(2,1)S(1)}, u32[]{:S(2)}, u32[]{:S(2)}) collective-permute-start(bf16[4,104,768]{2,1,0:T(8,128)(2,1)S(1)} %get-tuple-element.149), channel_id=1, source_target_pairs={{0,8},{4,12},{8,0},{12,4},{16,24},{20,28},{24,16},{28,20},{1,9},{5... | collective-permute-start | bytes 1916936 | tf_op jit(solution)/shard_map/ppermute | solution.py:484
  (103 other events, 744.1 us)

commit v3 on v2

--- a/solution.py
+++ b/solution.py
@@ -281,14 +281,37 @@
         back_ref[j] = b_ref[pl.ds(pl.multiple_of((place ^ j) * rows, rows), rows), :]
 
 
-def stage_eighths(own_ref, near_ref, far_ref, member, first, stage_ref):
-    rows = stage_ref.shape[1]
+def by_eighth(refs):
+    first, second = [], []
     for j in range(PLANE):
-        if member == 0:
+        far, y, x = j // 4, j // 2 % 2, j % 2
+        first.append(refs[4].at[y, x] if far else refs[y].at[x])
+        second.append(refs[4].at[2 + x, y] if far else refs[2 + x].at[y])
+    return first, second
+
+
+def eighth_rows(halves, j, member, start, count):
+    first, second = halves[0][j], halves[1][j]
+    middle = first.shape[1]
+    pieces = []
+    if start < middle:
+        pieces.append(first[member, pl.ds(start, min(count, middle - start)), :])
+    if start + count > middle:
+        at = max(start, middle)
+        pieces.append(second[member, pl.ds(at - middle, start + count - at), :])
+    return pieces
+
+
+def stage_eighths(own_ref, halves, member, start, stage_ref):
+    for j in range(PLANE):
+        if own_ref is not None and member == 0:
             stage_ref[j] = own_ref[j].astype(f32)
-        else:
-            ref = near_ref if j < 4 else far_ref
-            stage_ref[j] = ref[j % 4, member - 1, pl.ds(first, rows), :].astype(f32)
+            continue
+        at = 0
+        of = member if own_ref is None else member - 1
+        for piece in eighth_rows(halves, j, of, start, stage_ref.shape[1]):
+            stage_ref[j, pl.ds(at, piece.shape[0]), :] = piece.astype(f32)
+            at += piece.shape[0]
 
 
 def head_block(stage_ref, head):
@@ -296,10 +319,11 @@
 
 
 def project_kernel(
-    place_ref, left_ref, tokens_ref, right_ref, own_ref, near_ref, far_ref, bq_ref, bv_ref,
-    q_ref, k_ref, v_ref, w_ref, x_ref, stage_ref,
+    place_ref, left_ref, tokens_ref, right_ref, own_ref, *refs
 ):
-    ways = near_ref.shape[1] + 1
+    halves, refs = by_eighth(refs[:5]), refs[5:]
+    bq_ref, bv_ref, q_ref, k_ref, v_ref, w_ref, x_ref, stage_ref = refs
+    ways = halves[0][0].shape[0] + 1
     heads = own_ref.shape[1] // 24
     halo = left_ref.shape[0]
     own = tokens_ref.shape[0]
@@ -309,7 +333,7 @@
     x_ref[pl.ds(halo, own)] = tokens_ref[...]
     x_ref[pl.ds(halo + own, halo)] = right_ref[...]
     for member in range(ways):
-        stage_eighths(own_ref, near_ref, far_ref, member, 0, stage_ref)
+        stage_eighths(own_ref, halves, member, 0, stage_ref)
         for kind in range(3):
             blocks = [head_block(stage_ref, kind * heads + h) for h in range(heads)]
             at = kind * width + member * inner
@@ -327,50 +351,72 @@
     lax.fori_loop(0, x_ref.shape[0] // 256, step, 0)
 
 
-def join_units_kernel(place_ref, own_ref, near_ref, far_ref, out_ref):
+def join_units(own_ref, halves, out_ref):
     rows = own_ref.shape[1]
-    ways = near_ref.shape[1] + 1
+    ways = halves[0][0].shape[0] + 1
     for j in range(PLANE):
-        ref = near_ref if j < 4 else far_ref
         out_ref[pl.ds(j * ways * rows, rows), :] = own_ref[j]
         for member in range(1, ways):
             at = (j * ways + member) * rows
-            out_ref[pl.ds(at, rows), :] = ref[j % 4, member - 1, :rows, :]
-
-
-def join_in_out_kernel(place_ref, own_ref, own_out_ref, near_ref, far_ref, in_ref, out_ref, stage_ref):
-    join_units_kernel(place_ref, own_ref, near_ref, far_ref, in_ref)
-    rows = own_ref.shape[1]
+            for piece in eighth_rows(halves, j, member - 1, 0, rows):
+                out_ref[pl.ds(at, piece.shape[0]), :] = piece
+                at += piece.shape[0]
+
+
+def join_units_kernel(place_ref, own_ref, *refs):
+    join_units(own_ref, by_eighth(refs[:5]), refs[5])
+
+
+def join_in_out_kernel(place_ref, own_ref, own_out_ref, *refs):
+    halves = by_eighth(refs[:5])
+    in_ref, out_ref, stage_ref = refs[5:]
+    join_units(own_ref, halves, in_ref)
     heads = own_out_ref.shape[1] // 8
-    for member in range(near_ref.shape[1] + 1):
-        stage_eighths(own_out_ref, near_ref, far_ref, member, rows, stage_ref)
+    for member in range(halves[0][0].shape[0] + 1):
+        stage_eighths(own_out_ref, halves, member, own_ref.shape[1], stage_ref)
         for h in range(heads):
             block = head_block(stage_ref, h)
             out_ref[pl.ds((member * heads + h) * HEAD, HEAD), :] = block.astype(bf16)
 
 
+def put_heads(ways, heads, sum_ref, kind, first_head, block):
+    for i in range(block.shape[0] // HEAD):
+        member, h = divmod(first_head + i, heads)
+        for j in range(PLANE):
+            part = block[i * HEAD + j * 8 : i * HEAD + j * 8 + 8]
+            sum_ref[j * ways + member, pl.ds((kind * heads + h) * 8, 8), :] = part
+
+
+def part_pieces(sum_ref, keep_ref, send_ref):
+    half = keep_ref.shape[0]
+    for i in range(half):
+        keep_ref[i] = sum_ref[i].astype(bf16)
+        send_ref[i] = sum_ref[half + i].astype(bf16)
+
+
+def out_grads_kernel(ways, place_ref, left_ref, right_ref, first_ref, keep_ref, send_ref, sum_ref):
+    width = first_ref.shape[1]
+    heads = width // ways // HEAD
+    sum_ref[:, heads * 8 :, :] = jnp.zeros((PLANE * ways, 8, width), f32)
+    for g, ref in enumerate((left_ref, right_ref)):
+        block = mm(ref[...], first_ref[...], TN)
+        put_heads(ways, heads, sum_ref, 0, g * width // 2 // HEAD, block)
+    part_pieces(sum_ref, keep_ref, send_ref)
+
+
 def piece_grads_kernel(groups, place_ref, *refs):
-    grad_refs, context_refs = refs[: 3 * groups], refs[3 * groups : 3 * groups + 2]
-    tokens_ref, first_ref, vectors_ref, keep_ref, send_ref, sum_ref = refs[3 * groups + 2 :]
+    grad_refs = refs[: 3 * groups]
+    tokens_ref, vectors_ref, keep_ref, send_ref, sum_ref = refs[3 * groups :]
     place = place_ref[0]
     ways = vectors_ref.shape[0]
     width = tokens_ref.shape[1]
     inner = width // ways
     heads = inner // HEAD
-
-    def put(kind, first_head, block):
-        for i in range(block.shape[0] // HEAD):
-            member, h = divmod(first_head + i, heads)
-            for j in range(PLANE):
-                part = block[i * HEAD + j * 8 : i * HEAD + j * 8 + 8]
-                sum_ref[j * ways + member, pl.ds((kind * heads + h) * 8, 8), :] = part
-
     lanes = width // groups
     for kind in range(3):
         for g in range(groups):
-            put(kind, g * lanes // HEAD, mm(grad_refs[kind * groups + g][...], tokens_ref[...], TN))
-    for g, ref in enumerate(context_refs):
-        put(3, g * width // 2 // HEAD, mm(ref[...], first_ref[...], TN))
+            block = mm(grad_refs[kind * groups + g][...], tokens_ref[...], TN)
+            put_heads(ways, heads, sum_ref, kind, g * lanes // HEAD, block)
     lane = lax.broadcasted_iota(jnp.int32, (width, width), 0)
     to = lax.broadcasted_iota(jnp.int32, (width, width), 1)
     member = sum((lane >= i * inner).astype(jnp.int32) for i in range(1, ways))
@@ -386,45 +432,39 @@
         sums = jnp.where(of == row, jnp.concatenate(sums, axis=1), 0.0)
         chosen = jnp.where(spot + first == to, 1.0, 0.0).astype(bf16)
         lines = lines + mm(sums.astype(bf16), chosen)
-    below = 4 * heads * 8
+    below = 3 * heads * 8
     for i in range(ways):
         block = vectors_ref[i] + jnp.where(row == 2, lines[i : i + 1], 0.0)
         for j in range(PLANE):
             sum_ref[j * ways + i, pl.ds(below, 8), :] = block
-    half = keep_ref.shape[0]
-    for i in range(half):
-        keep_ref[i] = sum_ref[i].astype(bf16)
-        send_ref[i] = sum_ref[half + i].astype(bf16)
-
-
-def finish_heads_kernel(place_ref, near_ref, far_ref, q_ref, k_ref, v_ref, o_ref, rows_ref):
+    part_pieces(sum_ref, keep_ref, send_ref)
+
+
+def gather_heads(place, rows_ref, first, out_ref):
+    held = []
+    for h in range(out_ref.shape[0] // HEAD):
+        for p in range(PLANE):
+            held.append(rows_ref[place ^ p, pl.ds(first + h * 8, 8), :])
+    out_ref[...] = jnp.concatenate(held, axis=0)
+
+
+def finish_heads_kernel(place_ref, *refs):
+    q_ref, k_ref, v_ref, rows_ref = refs[5:]
+    stage_eighths(None, by_eighth(refs[:5]), 0, 0, rows_ref)
+    for kind, ref in enumerate((q_ref, k_ref, v_ref)):
+        gather_heads(place_ref[0], rows_ref, kind * ref.shape[0] // PLANE, ref)
+
+
+def finish_units_kernel(place_ref, *refs):
+    back_ref, in_ref, out_ref, rows_ref, turned_ref = refs[5:]
     place = place_ref[0]
-    heads = o_ref.shape[0] // HEAD
-    rows_ref[:4] = near_ref[...].astype(f32)
-    rows_ref[4:] = far_ref[...].astype(f32)
-    for kind, ref in enumerate((q_ref, k_ref, v_ref, o_ref)):
-        held = []
-        for h in range(heads):
-            for p in range(PLANE):
-                held.append(rows_ref[place ^ p, pl.ds((kind * heads + h) * 8, 8), :])
-        block = jnp.concatenate(held, axis=0)
-        ref[...] = block
-
-
-def finish_units_kernel(
-    place_ref, back_near_ref, back_far_ref, in_near_ref, in_far_ref, back_ref, in_ref, rows_ref, turned_ref
-):
-    place = place_ref[0]
-    rows = back_near_ref.shape[1]
-    rows_ref[:4] = back_near_ref[...].astype(f32)
-    rows_ref[4:] = back_far_ref[...].astype(f32)
+    rows = back_ref.shape[0] // PLANE
+    stage_eighths(None, by_eighth(refs[:5]), 0, 0, rows_ref)
     for p in range(PLANE):
-        back_ref[pl.ds(p * rows, rows), :] = rows_ref[place ^ p]
-    rows_ref[:4] = in_near_ref[...].astype(f32)
-    rows_ref[4:] = in_far_ref[...].astype(f32)
-    for p in range(PLANE):
-        turned_ref[pl.ds(p * rows, rows), :] = rows_ref[place ^ p]
+        back_ref[pl.ds(p * rows, rows), :] = rows_ref[place ^ p, :rows, :]
+        turned_ref[pl.ds(p * rows, rows), :] = rows_ref[place ^ p, pl.ds(rows, rows), :]
     in_ref[...] = turned_ref[...].T
+    gather_heads(place, rows_ref, 2 * rows, out_ref)
 
 
 def norm_parts(values):
@@ -446,8 +486,9 @@
     return before * half, half + before * bell
 
 
-def turn(ways, step):
-    return [(i, (i - step) % ways) for i in range(ways)]
+def partner(values, step):
+    ways = lax.axis_size("mp")
+    return lax.ppermute(values, "mp", [(i, i ^ step) for i in range(ways)])
 
 
 def halo_rows(values, halo):
@@ -462,7 +503,7 @@
     data_ways = lax.axis_size("dp")
     total = table
     for step in range(1, ways):
-        total = total + lax.ppermute(table, "mp", turn(ways, step))
+        total = total + partner(table, step)
     held = total[None]
     data_index = lax.axis_index("dp")
     level = 1
@@ -485,41 +526,66 @@
 
 
 def along(piece):
-    ways = lax.axis_size("mp")
-    return [lax.ppermute(piece, "mp", turn(ways, step)) for step in range(1, ways)]
-
-
-def spread_at_once(values):
-    others = [swap(values, bit) for bit in (NEAR_X, NEAR_Y, NEAR_X | NEAR_Y)]
-    near = jnp.stack([values, *others])
-    return near, swap(near, CORE)
-
-
-def spread_x_first(values):
-    both = jnp.stack([values, swap(values, NEAR_X)])
-    return jnp.stack([both, swap(both, NEAR_Y)]).reshape(4, *values.shape)
-
-
-def spread_y_first(values):
-    both = jnp.stack([values, swap(values, NEAR_Y)])
-    return jnp.stack([both, swap(both, NEAR_X)], axis=1).reshape(4, *values.shape)
+    return [partner(piece, step) for step in range(1, lax.axis_size("mp"))]
+
+
+def bit_step(held, level):
+    order = sorted(held)
+    other = partner(jnp.stack([held[i] for i in order]), level)
+    return held | {i | level: other[at] for at, i in enumerate(order)}
+
+
+def others_of(held):
+    return jnp.stack([held[i] for i in sorted(held)[1:]])
+
+
+def first_step(values):
+    middle = values.shape[1] // 2
+    first, second = values[:, :middle], values[:, middle:]
+    return [jnp.stack([first, swap(first, NEAR_X)]), jnp.stack([second, swap(second, NEAR_Y)])]
+
+
+def second_step(pairs):
+    first, second = pairs
+    return [first, swap(first, NEAR_Y), second, swap(second, NEAR_X)]
+
+
+def core_step(held):
+    return [*held, swap(jnp.stack(held), CORE)]
+
+
+def after(value, *others):
+    return lax.optimization_barrier((value, others))[0]
 
 
 def add(first, second):
     return (first.astype(f32) + second.astype(f32)).astype(bf16)
 
 
-def sum_along(parts):
-    ways = lax.axis_size("mp")
-    data_ways = lax.axis_size("dp")
-    total = parts[0].astype(f32)
-    for step in range(1, ways):
-        total = total + lax.ppermute(parts[step], "mp", turn(ways, -step)).astype(f32)
+def first_sum_step(sums):
+    half = sums.shape[2] // 2
+    first, second = sums[:, :, :half], sums[:, :, half:]
+    return [(first[0], swap(first[1], NEAR_Y)), (second[:, 0], swap(second[:, 1], NEAR_X))]
+
+
+def second_sum_step(halves):
+    first, second = (add(*half) for half in halves)
+    return [(first[0], swap(first[1], NEAR_X)), (second[0], swap(second[1], NEAR_Y))]
+
+
+def over_groups(total):
     level = PLANE
-    while level < data_ways:
+    while level < lax.axis_size("dp"):
         total = total + swap(total, level)
         level *= 2
     return total
+
+
+def sum_along(parts):
+    total = parts[0].astype(f32)
+    for step in range(1, len(parts)):
+        total = total + partner(parts[step], step).astype(f32)
+    return over_groups(total)
 
 
 def shards(
@@ -565,19 +631,29 @@
         [((PLANE, part, width), bf16), ((PLANE, piece_rows, width), bf16), ((PLANE, piece_rows, width), bf16)],
         [((heads * PLANE, 8, width), f32), ((PLANE, piece_rows, width), f32)], 5, "own_units",
     )
-    in_piece = jnp.concatenate([in_own[0], out_own[0]])
+    in_piece = jnp.concatenate([in_own[0], out_own[0], jnp.zeros((8, width), bf16)])
     back_piece = back_own[0]
-    qkv_along, in_piece, back_piece = lax.optimization_barrier((qkv_along, in_piece, back_piece))
-    bias_rest = jnp.stack([piece[3 * part :] for piece in qkv_along]).astype(f32)
+    in_piece, back_piece = after((in_piece, back_piece), qkv_along)
+    qkv_along = jnp.stack(qkv_along)
+    qkv_pairs = first_step(qkv_along)
+    in_held = {0: in_piece}
+    level = ways // 2
+    while level > 1:
+        in_held = bit_step(in_held, level)
+        level //= 2
+    qkv_held = second_step(after(qkv_pairs, in_held))
+    in_along = others_of(bit_step(in_held, 1))
+    qkv_parts = core_step(after(qkv_held, in_along))
+    back_held = bit_step({0: after(back_piece, in_along, qkv_held)}, ways // 2)
+    in_along = after(in_along, qkv_parts)
+    in_pairs = first_step(in_along)
+    bias_rest = after(qkv_along, qkv_parts)[:, 3 * part :].astype(f32)
     bias_in_rest = bias_rest[:, 0] + bias_rest[:, 1] + bias_rest[:, 2]
     bias_head_rest = bias_rest[:, 3] + bias_rest[:, 4] + bias_rest[:, 5]
     bias_in_all = jnp.concatenate([b_in[None], bias_in_rest])
     bias_heads = jnp.concatenate(
         [jnp.concatenate([b_query, b_value])[None], bias_head_rest[:, : 2 * inner]]
     )
-    qkv_near, qkv_far = spread_at_once(jnp.stack([piece[: 3 * part] for piece in qkv_along]))
-    in_along = jnp.stack(along(in_piece))
-    back_along = jnp.stack(along(back_piece))
 
     def in_order(parts):
         split = parts.reshape(*parts.shape[:-2], 2, 2, 2, parts.shape[-1])
@@ -602,24 +678,37 @@
     tiles = jnp.stack([tile_low, blocks, jnp.where(reach, blocks, 0)])
     bounds = (tiles, low[:, None], high[:, None])
 
-    qkv = (tokens_before, tokens, tokens_after, qkv_own, qkv_near, qkv_far, bias_query, bias_value)
+    tokens_before = after(tokens_before, in_along)
+    qkv = (tokens_before, tokens, tokens_after, qkv_own, *qkv_parts, bias_query, bias_value)
     queries, keys, values, qkv_all = local(
         project_kernel, place, qkv, [((count, width), bf16)] * 3 + [((3 * width, width), bf16)],
         [((count, width), bf16), ((PLANE, 3 * part, width), f32)], 10, "project",
     )
-    in_near = spread_x_first(in_along)
-    back_near = spread_y_first(back_along)
-    in_far = swap(in_near, CORE)
-    back_far = swap(back_near, CORE)
     own_queries = queries[halo : halo + own_rows]
-    context = [attend_forward(bounds, own_queries, keys, values, halo, i, 2) for i in range(2)]
+    back_held = after(back_held, queries)
+    level = ways // 4
+    while level:
+        back_held = bit_step(back_held, level)
+        level //= 2
+    back_along = others_of(back_held)
+    own_queries = after(own_queries, in_pairs)
+    context = [attend_forward(bounds, own_queries, keys, values, halo, 0, 2)]
+    in_held = second_step(in_pairs)
+    back_along = after(back_along, in_held, context[0])
+    back_pairs = first_step(back_along)
+    own_queries = after(own_queries, in_held, context[0])
+    in_parts = core_step(in_held)
+    context.append(attend_forward(bounds, own_queries, keys, values, halo, 1, 2))
+    in_own = after(in_own, back_pairs, context[1])
     in_all, out_all = local(
-        join_in_out_kernel, place, (in_own, out_own, in_near, in_far),
+        join_in_out_kernel, place, (in_own, out_own, *in_parts),
         [((ways * units, width), bf16), ((width, width), bf16)],
         [((PLANE, part, width), f32)], 5, "join_in_out",
     )
+    back_held = second_step(back_pairs)
+    back_parts = core_step(back_held)
     (back_all,) = local(
-        join_units_kernel, place, (back_own, back_near, back_far),
+        join_units_kernel, place, (back_own, *back_parts),
         [((ways * units, width), bf16)], [], 4, "join_back",
     )
     attended = mm(context[0], out_all[: width // 2]) + mm(context[1], out_all[width // 2 :])
@@ -627,7 +716,7 @@
     center_one, inverse_one = norm_parts(first_sum)
     unit_one = center_one * inverse_one
     hidden = unit_one * ln1_gain + ln1_shift
-    hidden_low = hidden.astype(bf16)
+    hidden_low = after(hidden.astype(bf16), back_held)
 
     active, slope = gelu_both(mm(hidden_low, in_all, NT) + bias_in)
     active, slope = lax.optimization_barrier((active.astype(bf16), slope.astype(bf16)))
@@ -695,7 +784,7 @@
     back_half = swap(back_sum[1], NEAR_Y)
     in_sent = to_core(grad_before, hidden_low)
     in_arrived = swap(in_sent, CORE)
-    pulled, in_sent = lax.optimization_barrier((grad_before, in_sent))
+    pulled = after(grad_before, in_sent, back_sum)
     grad_hidden = grad_second + mm(pulled, in_all)
     grad_first = norm_pull(grad_hidden, unit_one, inverse_one, ln1_gain)
     stats += [
@@ -705,12 +794,25 @@
     ]
     first_low = grad_first.astype(bf16)
     first_before, first_after = halo_rows(first_low, halo)
-    in_sum = chip_sum(grad_before, hidden_low, in_arrived)
+    out_keep, out_sent = local(
+        functools.partial(out_grads_kernel, ways), place, (*context, first_low),
+        [((4 * ways, part + 8, width), bf16)] * 2, [((8 * ways, part + 8, width), f32)], 3, "out_grads",
+    )
+    out_arrived = swap(out_sent, CORE)
+    in_sum = chip_sum(after(grad_before, out_sent), hidden_low, in_arrived)
+    out_sum = add(out_keep, out_arrived).reshape(2, 2, ways, part + 8, width)
+    in_sum = jnp.concatenate([in_sum, out_sum], axis=3)
     in_half = swap(in_sum[:, 1], NEAR_X)
     d_b_in = jnp.sum(grad_before, axis=0, dtype=f32).reshape(PLANE, ways, piece_rows)
 
     d_b_in = in_order(d_b_in.transpose(1, 0, 2)).reshape(ways, 1, units)
-    turned = jnp.roll(jnp.stack(stats).reshape(6, ways, inner), -mp_index, axis=1).transpose(1, 0, 2)
+    turned = jnp.stack(stats).reshape(6, ways, inner).transpose(1, 0, 2)
+    level = 1
+    while level < ways:
+        split = turned.reshape(-1, 2, level, *turned.shape[1:])
+        flipped = jnp.where((mp_index & level) != 0, jnp.flip(split, 1), split)
+        turned = flipped.reshape(turned.shape)
+        level *= 2
     turned = jnp.pad(turned.reshape(ways, -1), ((0, 0), (0, 2 * inner))).reshape(ways, 2, width)
     vectors = jnp.concatenate([d_b_in, turned, jnp.zeros((ways, 5, width), f32)], axis=1)
 
@@ -722,37 +824,46 @@
     def attend(grads, group):
         return attend_backward(bounds, queries, keys, values, grads, halo, group, groups)
 
-    grad_context, back_half, vectors = lax.optimization_barrier((grad_context, back_half, vectors))
+    grad_context = after(grad_context, in_sum, back_sum, vectors)
     parts.append(attend(grad_context, 0))
+    grad_context = after(grad_context, parts[0])
+    parts.append(attend(grad_context, 1))
+    back_half, in_half = after((back_half, in_half), parts[1])
     back_sum = add(back_sum[0], back_half)
+    in_sum = add(in_sum[:, 0], in_half)
     back_half = swap(back_sum[1], NEAR_X)
-    grad_context, in_half, _ = lax.optimization_barrier((grad_context, in_half, parts[0]))
-    parts.append(attend(grad_context, 1))
-    in_sum = add(in_sum[:, 0], in_half)
     in_half = swap(in_sum[1], NEAR_Y)
-    grad_context, back_half, in_half, _ = lax.optimization_barrier(
-        (grad_context, back_half, in_half, parts[1])
-    )
+    grad_context = after(grad_context, back_sum, in_sum, parts[1])
     parts.append(attend(grad_context, 2))
+    back_half, in_half = after((back_half, in_half), parts[2])
     early_sum = jnp.concatenate([add(back_sum[0], back_half), add(in_sum[0], in_half)], axis=1)
-    early_own = sum_along([early_sum[i] for i in range(ways)]).astype(bf16)
+    early_parts = [early_sum[i] for i in range(ways)]
+    early_odd = partner(jnp.stack(early_parts[1::2]), 1)
+    tokens_low = after(tokens, early_parts)
 
     grad_parts = [g[i] for i in range(3) for g in parts]
+    late_rows = 3 * part + 8
     late_keep, late_sent = local(
-        functools.partial(piece_grads_kernel, groups), place,
-        (*grad_parts, *context, tokens, first_low, vectors),
-        [((4 * ways, 4 * part + 8, width), bf16)] * 2,
-        [((8 * ways, 4 * part + 8, width), f32)], 10, "piece_grads",
-    )
-    late_sum = add(late_keep, swap(late_sent, CORE)).reshape(4, ways, 4 * part + 8, width)
-    arrived = [swap(late_sum[j], bit) for j, bit in ((1, NEAR_X), (2, NEAR_Y), (3, NEAR_X | NEAR_Y))]
-    late_sum = sum((a.astype(f32) for a in arrived), late_sum[0].astype(f32)).astype(bf16)
-    late_total = sum_along([late_sum[i] for i in range(ways)])
-    late_near, late_far = spread_at_once(late_total[: 4 * part].astype(bf16))
-    line = late_total[4 * part :]
-    back_near = spread_x_first(early_own[:piece_rows])
-    in_near = spread_y_first(early_own[piece_rows:])
-    early_far = swap(jnp.stack([back_near, in_near]), CORE)
+        functools.partial(piece_grads_kernel, groups), place, (*grad_parts, tokens_low, vectors),
+        [((4 * ways, late_rows, width), bf16)] * 2, [((8 * ways, late_rows, width), f32)], 8, "piece_grads",
+    )
+    late_sum = add(late_keep, swap(late_sent, CORE)).reshape(2, 2, ways, late_rows, width)
+    halves = first_sum_step(late_sum)
+    early_odd = after(early_odd, halves)
+    early_parts = [add(even, odd) for even, odd in zip(early_parts[::2], early_odd)]
+    halves = second_sum_step(halves)
+    late_parts = [half[i] for half in (add(*h) for h in halves) for i in range(ways // 2)]
+    level, early_own = 2, early_parts[0].astype(f32)
+    while level < ways:
+        early_own = early_own + after(partner(early_parts[level // 2], level), late_parts).astype(f32)
+        level *= 2
+    early_own = over_groups(early_own).astype(bf16)
+    early_held = second_step(first_step(after(early_own, late_parts)[None]))
+    late_total = sum_along(late_parts)
+    late_held = second_step(first_step(late_total.astype(bf16)[None]))
+    late_pieces = core_step(late_held)
+    early_pieces = core_step(early_held)
+    line = late_total[3 * part :]
     grad_queries, grad_keys, grad_values = (jnp.concatenate(p, axis=1) for p in zip(*parts))
     d_tokens = (
         grad_first
@@ -761,15 +872,14 @@
         + mm(grad_values, qkv_all[2 * width :])
     )
 
-    d_query, d_key, d_value, d_out = local(
-        finish_heads_kernel, place, (late_near, late_far),
-        [((inner, width), f32)] * 4,
-        [((PLANE, 4 * part, width), f32)], 5, "finish_heads",
-    )
-    d_back, d_in = local(
-        finish_units_kernel, place, (back_near, early_far[0], in_near, early_far[1]),
-        [((units, width), f32), ((width, units), f32)],
-        [((PLANE, piece_rows, width), f32), ((units, width), f32)], 6, "finish_units",
+    d_query, d_key, d_value = local(
+        finish_heads_kernel, place, late_pieces, [((inner, width), f32)] * 3,
+        [((PLANE, 3 * part, width), f32)], 4, "finish_heads",
+    )
+    d_back, d_in, d_out = local(
+        finish_units_kernel, place, early_pieces,
+        [((units, width), f32), ((width, units), f32), ((inner, width), f32)],
+        [((PLANE, 2 * piece_rows + part + 8, width), f32), ((units, width), f32)], 6, "finish_units",
     )
     norms = [line[1 + i // ways, i % ways * inner : (i % ways + 1) * inner] for i in range(8)]
     return (

time: 449 us -> 447 us (level)
  waiting for transfers between devices: 135 us -> 81.9 us
  local copies, waits for them, and re-layouts: 41.7 us -> 63 us
  other arithmetic: 31.5 us -> 47.6 us
  matrix products: 55 us -> 67.1 us
  Pallas kernels: 90.8 us -> 97.3 us
    ppermute x29 -> x37, waiting for transfers between devices: 75.5 us -> 34.8 us  [swap(): return lax.ppermute(values, 'dp', [(i, i ^ bit) for i in range(ways)])]
    ppermute x18 -> x15, waiting for transfers between devices: 50.7 us -> 38.7 us  [partner(): return lax.ppermute(values, 'mp', [(i, i ^ step) for i in range(ways)])]
    dot_general x16, matrix products: 50.4 us -> 61.7 us  [mm(): return lax.dot_general(a, b, dims, preferred_element_type=f32)]
    ppermute x2, starting transfers between devices: 18.8 us -> 8.61 us  [halo_rows(): lax.ppermute(values[-halo:], 'mp', [(i, i + 1) for i in range(ways - 1)])]
    ppermute x29 -> x37, starting transfers between devices: 32.9 us -> 42.2 us  [swap(): return lax.ppermute(values, 'dp', [(i, i ^ bit) for i in range(ways)])]
    another operation x21 -> x19, local copies, waits for them, and re-layouts: 6.18 us -> 14.3 us  [the longest x7 7.43 us: shards(): turned = jnp.stack(stats).reshape(6, ways, inner).transpose(1, 0, 2)]
    pallas_call x3, Pallas kernels: 43.4 us -> 48.6 us  [attend_backward(): pl.pallas_call(functools.partial(backward_kernel, halo), grid=(1,), out_s...]
    convert_element_type x5 -> x10, other arithmetic: 1.53 us -> 6.45 us  [add(): return (first.astype(f32) + second.astype(f32)).astype(bf16)]
  transfers between devices with their start and end apart: 54 -> 59, of which waited for: 22 -> 19; matrix products, arithmetic and copies ran while one was open for 17% -> 29% of each run, Pallas kernels for 14% -> 19%
where the time goes in v3:
time: 447 us; the launch traced here: 444 us
  Pallas kernels  97.3 us (22%)
  starting transfers between devices  85.3 us (19%)
  waiting for transfers between devices  81.9 us (18%)
  matrix products  67.1 us (15%)
  local copies, waits for them, and re-layouts  63 us (14%)
  other arithmetic  47.6 us (11%)
    dot_general x16, matrix products, mm(): return lax.dot_general(a, b, dims, preferred_element_type=f32)  61.7 us
    pallas_call x3, Pallas kernels, attend_backward(): pl.pallas_call(functools.partial(backward_kernel, halo), grid=(1,), out_s...  48.6 us
    ppermute x37, starting transfers between devices, swap(): return lax.ppermute(values, 'dp', [(i, i ^ bit) for i in range(ways)])  42.2 us
    ppermute x15, waiting for transfers between devices, partner(): return lax.ppermute(values, 'mp', [(i, i ^ step) for i in range(ways)])  38.7 us
    ppermute x37, waiting for transfers between devices, swap(): return lax.ppermute(values, 'dp', [(i, i ^ bit) for i in range(ways)])  34.8 us
    pallas_call x9, Pallas kernels, local(): pl.pallas_call(kernel, out_shape=tuple((jax.ShapeDtypeStruct(shape, dtype...  31.4 us
    ppermute x15, starting transfers between devices, partner(): return lax.ppermute(values, 'mp', [(i, i ^ step) for i in range(ways)])  29.5 us
    unnamed x179, local copies, waits for them, and re-layouts  18.2 us
  transfers between devices with their start and end apart: 59, of which 19 were waited for; matrix products, arithmetic and copies ran while one was open for 29% of the time, Pallas kernels for 19%

profile of v3, /device:TPU:1, one launch (start us, length us, event | category | flops | bytes accessed | tf_op | source)
XLA Modules:
  0.0 444.3 jit_solution(10370899252391804932)
XLA Ops:
  78.4 10.6 %project.1 = (bf16[1280,768]{1,0:T(8,128)(2,1)}, bf16[1280,768]{1,0:T(8,128)(2,1)}, bf16[1280,768]{1,0:T(8,128)(2,1)}, bf16[2304,768]{1,0:T(8,128)(2,1)}) custom-call(s32[1]{0:T(128)} %bitcast.3.place_ref, bf16[256,768]{1,0:T(8,128)(2,1)} %collective-permute-done.left_ref, bf16[768,768]{1,0:T(8,128)(2,1)S(1)} %copy-done, ...), custom_call_target="tpu_custom_call" | custom-call | flops 10000000000 | bytes 35000000 | tf_op jit(solution)/shard_map/project/pallas_call | solution.py:247
  100.9 7.6 %collective-permute-done.16.refs_1_ = bf16[2,3,64,768]{3,2,1,0:T(8,128)(2,1)} collective-permute-done((bf16[2,3,64,768]{3,2,1,0:T(8,128)(2,1)}, bf16[2,3,64,768]{3,2,1,0:T(8,128)(2,1)}, u32[]{:S(2)}, u32[]{:S(2)}) %collective-permute-start.16) | collective-permute-done | bytes 589856 | tf_op jit(solution)/shard_map/ppermute | solution.py:525
  116.3 8.9 %attend_forward.2.left_ref = bf16[768,384]{1,0:T(8,128)(2,1)S(1)} custom-call(s32[3,10]{1,0:T(4,128)S(1)} %pad_add_fusion.tiles_ref, s32[1280,1]{1,0:T(8,128)S(1)} %copy-done.7, s32[1280,1]{1,0:T(8,128)S(1)} %get-tuple-element.281.hi_ref, bf16[768,768]{1,0:T(8,128)(2,1)S(1)} %slice.335.q_ref, bf16[1280,768]{1,0:T(8,128)(2,1)S(1)} %copy-done.29, ...), custom_call_target="tpu_custom_call" | custom-call | flops 8999999488 | bytes 31500000 | tf_op jit(solution)/shard_map/attend_forward/pallas_call | solution.py:152
  128.5 5.7 %collective-permute-done.18 = bf16[3,48,768]{2,1,0:T(8,128)(2,1)S(1)} collective-permute-done((bf16[3,48,768]{2,1,0:T(8,128)(2,1)}, bf16[3,48,768]{2,1,0:T(8,128)(2,1)S(1)}, u32[]{:S(2)}, u32[]{:S(2)}) %collective-permute-start.18) | collective-permute-done | bytes 221216 | tf_op jit(solution)/shard_map/ppermute | solution.py:525
  139.5 8.4 %attend_forward.3.right_ref = bf16[768,384]{1,0:T(8,128)(2,1)S(1)} custom-call(s32[3,10]{1,0:T(4,128)S(1)} %pad_add_fusion.tiles_ref, s32[1280,1]{1,0:T(8,128)S(1)} %copy-done.8, s32[1280,1]{1,0:T(8,128)S(1)} %get-tuple-element.281.hi_ref, bf16[768,768]{1,0:T(8,128)(2,1)S(1)} %slice.335.q_ref, bf16[1280,768]{1,0:T(8,128)(2,1)S(1)} %copy-done.30, ...), custom_call_target="tpu_custom_call" | custom-call | flops 8999999488 | bytes 31500000 | tf_op jit(solution)/shard_map/attend_forward/pallas_call | solution.py:152
  150.5 4.9 %join_in_out.1 = (bf16[3072,768]{1,0:T(8,128)(2,1)}, bf16[768,768]{1,0:T(8,128)(2,1)S(1)}) custom-call(s32[1]{0:T(128)} %bitcast.3.place_ref, bf16[8,96,768]{2,1,0:T(8,128)(2,1)S(1)} %copy-done.18, bf16[8,24,768]{2,1,0:T(8,128)(2,1)S(1)} %copy-done.22, bf16[2,3,64,768]{3,2,1,0:T(8,128)(2,1)} %get-tuple-element.203.refs_0_, ...), custom_call_target="tpu_custom_call" | custom-call | flops 5000000000 | bytes 17500000 | tf_op jit(solution)/shard_map/join_in_out/pallas_call | solution.py:247
  158.7 8.7 %fusion.4 = (bf16[768,3072]{1,0:T(8,128)(2,1)}, bf16[768,3072]{1,0:T(8,128)(2,1)}) fusion(f32[3072]{0:T(1024)S(1)} %copy-done.65, bf16[768,768]{1,0:T(8,128)(2,1)S(1)} %fusion.14, bf16[3072,768]{1,0:T(8,128)(2,1)S(1)} %bitcast.295), kind=kOutput, calls=%fused_computation.5 | convolution fusion | flops 3652190208 | bytes 15347712 | tf_op jit(solution)/shard_map/dot_general | solution.py:30
  169.7 7.4 %fusion.119 = (f32[768]{0:T(1024)S(1)}, f32[768,768]{1,0:T(8,128)S(1)}) fusion(f32[768]{0:T(1024)S(1)} %copy-done.81, bf16[768,3072]{1,0:T(8,128)(2,1)} %get-tuple-element.128, bf16[3072,768]{1,0:T(8,128)(2,1)} %join_back.1, f32[768]{0:T(1024)S(1)} %copy-done.73, f32[768]{0:T(1024)S(1)} %copy-done.59, f32[768]{0:T(1024)S(1)} %add_rsqrt_fusion.1, ...), kind=kOutput, calls=%fused_computation.308 | convolution fusion | flops 3628006656 | bytes 14174208 | tf_op jit(solution)/shard_map/dot_general | solution.py:30
  194.4 4.5 %collective-permute-done.29 = bf16[4,32,768]{2,1,0:T(8,128)(2,1)S(1)} collective-permute-done((bf16[4,32,768]{2,1,0:T(8,128)(2,1)S(1)}, bf16[4,32,768]{2,1,0:T(8,128)(2,1)S(1)}, u32[]{:S(2)}, u32[]{:S(2)}) %collective-permute-start.29) | collective-permute-done | bytes 196640 | tf_op jit(solution)/shard_map/ppermute | solution.py:511
  200.6 4.9 %multiply_reduce_fusion.1 = (f32[768]{0:T(1024)}, f32[768]{0:T(1024)S(1)}, f32[768]{0:T(1024)S(1)}, f32[768]{0:T(1024)}, f32[768,768]{1,0:T(8,128)S(1)}) fusion(f32[768,768]{1,0:T(8,128)} %copy-done.37, f32[768]{0:T(1024)S(1)} %add_rsqrt_fusion, f32[768]{0:T(1024)S(1)} %broadcast_multiply_fusion.4, f32[768]{0:T(1024)S(1)} %copy-done.58, ...), kind=kOutput, calls=%fused_computation.25 | convolution fusion | flops 176391168 | bytes 5993568 | tf_op jit(solution)/shard_map/dot_general | solution.py:760
  214.7 8.2 %convert_reduce_fusion = (f32[3072]{0:T(1024)}, bf16[768,3072]{1,0:T(8,128)(2,1)S(1)}) fusion(bf16[768,3072]{1,0:T(8,128)(2,1)} %get-tuple-element.130, bf16[768,768]{1,0:T(8,128)(2,1)S(1)} %convert_element_type.255, bf16[3072,768]{1,0:T(8,128)(2,1)} %join_back.1), kind=kOutput, calls=%fused_computation.6 | convolution fusion | flops 3635672064 | bytes 15347712 | tf_op jit(solution)/shard_map/dot_general | solution.py:30
  238.1 6.0 %add_convert_fusion.1 = bf16[1536,768]{1,0:T(8,128)(2,1)} fusion(bf16[1536,768]{1,0:T(8,128)(2,1)} %collective-permute-done.30, bf16[768,768]{1,0:T(8,128)(2,1)S(1)} %convert_element_type.255, bf16[768,3072]{1,0:T(8,128)(2,1)} %get-tuple-element.128), kind=kOutput, calls=%fused_computation.11 | convolution fusion | flops 1815478272 | bytes 8257536 | tf_op jit(solution)/shard_map/dot_general | solution.py:30
  244.0 8.4 %multiply_reduce_fusion = (f32[768]{0:T(1024)}, f32[768]{0:T(1024)S(1)}, f32[768]{0:T(1024)S(1)}, f32[768]{0:T(1024)}, f32[768,768]{1,0:T(8,128)S(1)}) fusion(f32[768,768]{1,0:T(8,128)S(1)} %copy-done.36, f32[768]{0:T(1024)S(1)} %add_rsqrt_fusion.1, f32[768]{0:T(1024)S(1)} %broadcast_multiply_fusion.5, f32[768]{0:T(1024)S(1)} %copy-done.59, ...), kind=kOutput, calls=%fused_computation.24 | convolution fusion | flops 3629773824 | bytes 16536576 | tf_op jit(solution)/shard_map/dot_general | solution.py:30
  261.6 4.8 %collective-permute-start.31 = (bf16[256,768]{1,0:T(8,128)(2,1)}, bf16[256,768]{1,0:T(8,128)(2,1)}, u32[]{:S(2)}, u32[]{:S(2)}) collective-permute-start(bf16[256,768]{1,0:T(8,128)(2,1)} %get-tuple-element.198), channel_id=1, source_target_pairs={{0,1},{1,2},{2,3},{4,5},{5,6},{6,7},{8,9},{9,10},{10,11},{12,13},{... | collective-permute-start | bytes 1179656 | tf_op jit(solution)/shard_map/ppermute | solution.py:496
  274.5 6.2 %add_convert_fusion = bf16[1536,768]{1,0:T(8,128)(2,1)} fusion(bf16[1536,768]{1,0:T(8,128)(2,1)} %collective-permute-done.33, bf16[768,768]{1,0:T(8,128)(2,1)} %copy-done.47, bf16[768,3072]{1,0:T(8,128)(2,1)} %copy-done.83), kind=kOutput, calls=%fused_computation.10 | convolution fusion | flops 1815478272 | bytes 8257536 | tf_op jit(solution)/shard_map/dot_general | solution.py:30
  292.8 16.1 %attend_backward.3 = (bf16[768,256]{1,0:T(8,128)(2,1)S(1)}, bf16[768,256]{1,0:T(8,128)(2,1)S(1)}, bf16[768,256]{1,0:T(8,128)(2,1)S(1)}) custom-call(s32[3,10]{1,0:T(4,128)S(1)} %pad_add_fusion.tiles_ref, s32[1280,1]{1,0:T(8,128)S(1)} %copy-done.9, s32[1280,1]{1,0:T(8,128)S(1)} %copy-done.6, bf16[1280,768]{1,0:T(8,128)(2,1)S(1)} %copy-done.4, ...), custom_call_target="tpu_custom_call" | custom-call | flops 14000000000 | bytes 49000000 | tf_op jit(solution)/shard_map/attend_backward/pallas_call | solution.py:223
  308.9 16.1 %attend_backward.4 = (bf16[768,256]{1,0:T(8,128)(2,1)S(1)}, bf16[768,256]{1,0:T(8,128)(2,1)S(1)}, bf16[768,256]{1,0:T(8,128)(2,1)S(1)}) custom-call(s32[3,10]{1,0:T(4,128)S(1)} %pad_add_fusion.tiles_ref, s32[1280,1]{1,0:T(8,128)S(1)} %copy-done.9, s32[1280,1]{1,0:T(8,128)S(1)} %copy-done.6, bf16[1280,768]{1,0:T(8,128)(2,1)S(1)} %copy-done.4, ...), custom_call_target="tpu_custom_call" | custom-call | flops 14000000000 | bytes 49000000 | tf_op jit(solution)/shard_map/attend_backward/pallas_call | solution.py:223
  331.0 16.5 %attend_backward.5 = (bf16[768,256]{1,0:T(8,128)(2,1)S(1)}, bf16[768,256]{1,0:T(8,128)(2,1)S(1)}, bf16[768,256]{1,0:T(8,128)(2,1)S(1)}) custom-call(s32[3,10]{1,0:T(4,128)S(1)} %pad_add_fusion.tiles_ref, s32[1280,1]{1,0:T(8,128)S(1)} %copy-done.9, s32[1280,1]{1,0:T(8,128)S(1)} %copy-done.6, bf16[1280,768]{1,0:T(8,128)(2,1)S(1)} %copy-done.4, ...), custom_call_target="tpu_custom_call" | custom-call | flops 14000000000 | bytes 49000000 | tf_op jit(solution)/shard_map/attend_backward/pallas_call | solution.py:223
  347.9 5.9 %piece_grads.1 = (bf16[16,80,768]{2,1,0:T(8,128)(2,1)}, bf16[16,80,768]{2,1,0:T(8,128)(2,1)}) custom-call(s32[1]{0:T(128)} %bitcast.3.place_ref, bf16[768,256]{1,0:T(8,128)(2,1)S(1)} %get-tuple-element.136.refs_0_, bf16[768,256]{1,0:T(8,128)(2,1)S(1)} %get-tuple-element.140.refs_1_, bf16[768,256]{1,0:T(8,128)(2,1)S(1)} %get-tuple-element.146.refs_2_, ...), custom_call_target="tpu_custom_call" | custom-call | flops 8000000000 | bytes 28000000 | tf_op jit(solution)/shard_map/piece_grads/pallas_call | solution.py:247
  365.7 9.0 %collective-permute-done.40 = bf16[2,2,80,768]{3,2,1,0:T(8,128)(2,1)S(1)} collective-permute-done((bf16[2,2,80,768]{3,2,1,0:T(8,128)(2,1)S(1)}, bf16[2,2,80,768]{3,2,1,0:T(8,128)(2,1)S(1)}, u32[]{:S(2)}, u32[]{:S(2)}) %collective-permute-start.40) | collective-permute-done | bytes 491552 | tf_op jit(solution)/shard_map/ppermute | solution.py:525
  377.1 4.6 %collective-permute-done.52 = bf16[2,224,768]{2,1,0:T(8,128)(2,1)S(1)} collective-permute-done((bf16[2,224,768]{2,1,0:T(8,128)(2,1)S(1)}, bf16[2,224,768]{2,1,0:T(8,128)(2,1)S(1)}, u32[]{:S(2)}, u32[]{:S(2)}) %collective-permute-start.52) | collective-permute-done | bytes 688160 | tf_op jit(solution)/shard_map/ppermute | solution.py:491
  381.8 8.5 %collective-permute-start.53 = (bf16[224,768]{1,0:T(8,128)(2,1)S(1)}, bf16[224,768]{1,0:T(8,128)(2,1)S(1)}, u32[]{:S(2)}, u32[]{:S(2)}) collective-permute-start(bf16[224,768]{1,0:T(8,128)(2,1)S(1)} %fusion.49), channel_id=1, source_target_pairs={{0,2},{1,3},{2,0},{3,1},{4,6},{5,7},{6,4},{7,5},{8,10},{9,11},{10,... | collective-permute-start | bytes 1032200 | tf_op jit(solution)/shard_map/ppermute | solution.py:491
  394.2 17.3 %collective-permute-done.53 = bf16[224,768]{1,0:T(8,128)(2,1)S(1)} collective-permute-done((bf16[224,768]{1,0:T(8,128)(2,1)S(1)}, bf16[224,768]{1,0:T(8,128)(2,1)S(1)}, u32[]{:S(2)}, u32[]{:S(2)}) %collective-permute-start.53) | collective-permute-done | bytes 344096 | tf_op jit(solution)/shard_map/ppermute | solution.py:491
  422.4 4.6 %collective-permute-done.49 = bf16[1,40,768]{2,1,0:T(8,128)(2,1)S(1)} collective-permute-done((bf16[1,40,768]{2,1,0:T(8,128)(2,1)S(1)}, bf16[1,40,768]{2,1,0:T(8,128)(2,1)S(1)}, u32[]{:S(2)}, u32[]{:S(2)}) %collective-permute-start.49) | collective-permute-done | bytes 61472 | tf_op jit(solution)/shard_map/ppermute | solution.py:525
  (482 shorter events, 238.7 us)
Async XLA Ops:
  6.1 24.0 %collective-permute-start.3 = (bf16[80,768]{1,0:T(8,128)(2,1)}, bf16[80,768]{1,0:T(8,128)(2,1)}, u32[]{:S(2)}, u32[]{:S(2)}) collective-permute-start(bf16[80,768]{1,0:T(8,128)(2,1)} %fusion.68), channel_id=1, source_target_pairs={{0,3},{1,2},{2,1},{3,0},{4,7},{5,6},{6,5},{7,4},{8,11},{9,10},{10,... | collective-permute-start | bytes 368648 | tf_op jit(solution)/shard_map/ppermute | solution.py:491
  10.2 19.9 %collective-permute-start.2 = (bf16[80,768]{1,0:T(8,128)(2,1)}, bf16[80,768]{1,0:T(8,128)(2,1)}, u32[]{:S(2)}, u32[]{:S(2)}) collective-permute-start(bf16[80,768]{1,0:T(8,128)(2,1)} %fusion.68), channel_id=1, source_target_pairs={{0,2},{1,3},{2,0},{3,1},{4,6},{5,7},{6,4},{7,5},{8,10},{9,11},{10,... | collective-permute-start | bytes 368648 | tf_op jit(solution)/shard_map/ppermute | solution.py:491
  10.2 19.9 %collective-permute-start.1 = (bf16[80,768]{1,0:T(8,128)(2,1)}, bf16[80,768]{1,0:T(8,128)(2,1)}, u32[]{:S(2)}, u32[]{:S(2)}) collective-permute-start(bf16[80,768]{1,0:T(8,128)(2,1)} %fusion.68), channel_id=1, source_target_pairs={{0,1},{1,0},{2,3},{3,2},{4,5},{5,4},{6,7},{7,6},{8,9},{9,8},{10,11... | collective-permute-start | bytes 368648 | tf_op jit(solution)/shard_map/ppermute | solution.py:491
  11.4 59.0 %collective-permute-start = (bf16[256,768]{1,0:T(8,128)(2,1)}, bf16[256,768]{1,0:T(8,128)(2,1)}, u32[]{:S(2)}, u32[]{:S(2)}) collective-permute-start(bf16[256,768]{1,0:T(8,128)(2,1)} %get-tuple-element.201), channel_id=1, source_target_pairs={{0,1},{1,2},{2,3},{4,5},{5,6},{6,7},{8,9},{9,10},{10,11},{12,13},{... | collective-permute-start | bytes 1179656 | tf_op jit(solution)/shard_map/ppermute | solution.py:496
  15.3 61.9 %collective-permute-start.11 = (bf16[256,768]{1,0:T(8,128)(2,1)}, bf16[256,768]{1,0:T(8,128)(2,1)}, u32[]{:S(2)}, u32[]{:S(2)}) collective-permute-start(bf16[256,768]{1,0:T(8,128)(2,1)} %get-tuple-element.200), channel_id=1, source_target_pairs={{1,0},{2,1},{3,2},{5,4},{6,5},{7,6},{9,8},{10,9},{11,10},{13,12},{... | collective-permute-start | bytes 1179656 | tf_op jit(solution)/shard_map/ppermute | solution.py:497
  61.6 27.3 %collective-permute-start.14 = (bf16[1,96,768]{2,1,0:T(8,128)(2,1)}, bf16[1,96,768]{2,1,0:T(8,128)(2,1)}, u32[]{:S(2)}, u32[]{:S(2)}) collective-permute-start(bf16[1,96,768]{2,1,0:T(8,128)(2,1)} %bitcast.29), channel_id=1, source_target_pairs={{0,2},{1,3},{2,0},{3,1},{4,6},{5,7},{6,4},{7,5},{8,10},{9,11},{10,... | collective-permute-start | bytes 442376 | tf_op jit(solution)/shard_map/ppermute | solution.py:491
  73.9 18.5 %collective-permute-start.12 = (bf16[3,64,768]{2,1,0:T(8,128)(2,1)}, bf16[3,64,768]{2,1,0:T(8,128)(2,1)}, u32[]{:S(2)}, u32[]{:S(2)}) collective-permute-start(bf16[3,64,768]{2,1,0:T(8,128)(2,1)} %get-tuple-element.209), channel_id=1, source_target_pairs={{0,8},{4,12},{8,0},{12,4},{16,24},{20,28},{24,16},{28,20},{1,9},{5... | collective-permute-start | bytes 884744 | tf_op jit(solution)/shard_map/ppermute | solution.py:525
  76.0 18.8 %collective-permute-start.13 = (bf16[3,64,768]{2,1,0:T(8,128)(2,1)}, bf16[3,64,768]{2,1,0:T(8,128)(2,1)}, u32[]{:S(2)}, u32[]{:S(2)}) collective-permute-start(bf16[3,64,768]{2,1,0:T(8,128)(2,1)} %get-tuple-element.208), channel_id=1, source_target_pairs={{0,16},{4,20},{8,24},{12,28},{16,0},{20,4},{24,8},{28,12},{1,17},{... | collective-permute-start | bytes 884744 | tf_op jit(solution)/shard_map/ppermute | solution.py:525
  114.0 36.5 %collective-permute-start.20 = (bf16[4,2,3,64,768]{4,3,2,1,0:T(8,128)(2,1)}, bf16[4,2,3,64,768]{4,3,2,1,0:T(8,128)(2,1)}, u32[]{:S(2)}, u32[]{:S(2)}) collective-permute-start(bf16[4,2,3,64,768]{4,3,2,1,0:T(8,128)(2,1)} %pad_maximum_fusion.1), channel_id=1, source_target_pairs={{0,4},{4,0},{8,12},{12,8},{16,20},{20,16},{24,28},{28,24},{1,5},{5... | collective-permute-start | bytes 7077896 | tf_op jit(solution)/shard_map/ppermute | solution.py:525
  148.2 19.1 %collective-permute-start.23 = (bf16[4,2,3,48,768]{4,3,2,1,0:T(8,128)(2,1)S(1)}, bf16[4,2,3,48,768]{4,3,2,1,0:T(8,128)(2,1)S(1)}, u32[]{:S(2)}, u32[]{:S(2)}) collective-permute-start(bf16[4,2,3,48,768]{4,3,2,1,0:T(8,128)(2,1)S(1)} %pad_maximum_fusion.2), channel_id=1, source_target_pairs={{0,4},{4,0},{8,12},{12,8},{16,20},{20,16},{24,28},{28,24},{1,5},{5... | collective-permute-start | bytes 5308424 | tf_op jit(solution)/shard_map/ppermute | solution.py:525
  212.0 26.1 %collective-permute-start.30 = (bf16[1536,768]{1,0:T(8,128)(2,1)}, bf16[1536,768]{1,0:T(8,128)(2,1)}, u32[]{:S(2)}, u32[]{:S(2)}) collective-permute-start(bf16[1536,768]{1,0:T(8,128)(2,1)} %convolution_convert_fusion.1), channel_id=1, source_target_pairs={{0,4},{4,0},{8,12},{12,8},{16,20},{20,16},{24,28},{28,24},{1,5},{5... | collective-permute-start | bytes 7077896 | tf_op jit(solution)/shard_map/ppermute | solution.py:525
  226.5 48.0 %collective-permute-start.33 = (bf16[1536,768]{1,0:T(8,128)(2,1)}, bf16[1536,768]{1,0:T(8,128)(2,1)}, u32[]{:S(2)}, u32[]{:S(2)}) collective-permute-start(bf16[1536,768]{1,0:T(8,128)(2,1)} %convolution_convert_fusion), channel_id=1, source_target_pairs={{0,4},{4,0},{8,12},{12,8},{16,20},{20,16},{24,28},{28,24},{1,5},{5... | collective-permute-start | bytes 7077896 | tf_op jit(solution)/shard_map/ppermute | solution.py:525
  258.9 30.5 %collective-permute-start.34 = (bf16[16,32,768]{2,1,0:T(8,128)(2,1)}, bf16[16,32,768]{2,1,0:T(8,128)(2,1)}, u32[]{:S(2)}, u32[]{:S(2)}) collective-permute-start(bf16[16,32,768]{2,1,0:T(8,128)(2,1)} %get-tuple-element.132), channel_id=1, source_target_pairs={{0,4},{4,0},{8,12},{12,8},{16,20},{20,16},{24,28},{28,24},{1,5},{5... | collective-permute-start | bytes 2359304 | tf_op jit(solution)/shard_map/ppermute | solution.py:525
  260.3 26.0 %collective-permute-start.32 = (bf16[256,768]{1,0:T(8,128)(2,1)}, bf16[256,768]{1,0:T(8,128)(2,1)}, u32[]{:S(2)}, u32[]{:S(2)}) collective-permute-start(bf16[256,768]{1,0:T(8,128)(2,1)} %get-tuple-element.199), channel_id=1, source_target_pairs={{1,0},{2,1},{3,2},{5,4},{6,5},{7,6},{9,8},{10,9},{11,10},{13,12},{... | collective-permute-start | bytes 1179656 | tf_op jit(solution)/shard_map/ppermute | solution.py:497
  261.6 24.7 %collective-permute-start.31 = (bf16[256,768]{1,0:T(8,128)(2,1)}, bf16[256,768]{1,0:T(8,128)(2,1)}, u32[]{:S(2)}, u32[]{:S(2)}) collective-permute-start(bf16[256,768]{1,0:T(8,128)(2,1)} %get-tuple-element.198), channel_id=1, source_target_pairs={{0,1},{1,2},{2,3},{4,5},{5,6},{6,7},{8,9},{9,10},{10,11},{12,13},{... | collective-permute-start | bytes 1179656 | tf_op jit(solution)/shard_map/ppermute | solution.py:496
  271.6 53.4 %collective-permute-start.35 = (bf16[2,4,96,768]{3,2,1,0:T(8,128)(2,1)}, bf16[2,4,96,768]{3,2,1,0:T(8,128)(2,1)}, u32[]{:S(2)}, u32[]{:S(2)}) collective-permute-start(bf16[2,4,96,768]{3,2,1,0:T(8,128)(2,1)} %bitcast.61), channel_id=1, source_target_pairs={{0,16},{4,20},{8,24},{12,28},{16,0},{20,4},{24,8},{28,12},{1,17},{... | collective-permute-start | bytes 3538952 | tf_op jit(solution)/shard_map/ppermute | solution.py:525
  291.0 35.1 %collective-permute-start.36 = (bf16[2,4,128,768]{3,2,1,0:T(8,128)(2,1)S(1)}, bf16[2,4,128,768]{3,2,1,0:T(8,128)(2,1)S(1)}, u32[]{:S(2)}, u32[]{:S(2)}) collective-permute-start(bf16[2,4,128,768]{3,2,1,0:T(8,128)(2,1)S(1)} %slice_bitcast_fusion.1), channel_id=1, source_target_pairs={{0,8},{4,12},{8,0},{12,4},{16,24},{20,28},{24,16},{28,20},{1,9},{5... | collective-permute-start | bytes 4718600 | tf_op jit(solution)/shard_map/ppermute | solution.py:525
  329.1 18.4 %collective-permute-start.37 = (bf16[4,96,768]{2,1,0:T(8,128)(2,1)S(1)}, bf16[4,96,768]{2,1,0:T(8,128)(2,1)S(1)}, u32[]{:S(2)}, u32[]{:S(2)}) collective-permute-start(bf16[4,96,768]{2,1,0:T(8,128)(2,1)S(1)} %slice_bitcast_fusion.4), channel_id=1, source_target_pairs={{0,8},{4,12},{8,0},{12,4},{16,24},{20,28},{24,16},{28,20},{1,9},{5... | collective-permute-start | bytes 1769480 | tf_op jit(solution)/shard_map/ppermute | solution.py:525
  329.7 17.7 %collective-permute-start.38 = (bf16[4,128,768]{2,1,0:T(8,128)(2,1)S(1)}, bf16[4,128,768]{2,1,0:T(8,128)(2,1)S(1)}, u32[]{:S(2)}, u32[]{:S(2)}) collective-permute-start(bf16[4,128,768]{2,1,0:T(8,128)(2,1)S(1)} %slice_bitcast_fusion.3), channel_id=1, source_target_pairs={{0,16},{4,20},{8,24},{12,28},{16,0},{20,4},{24,8},{28,12},{1,17},{... | collective-permute-start | bytes 2359304 | tf_op jit(solution)/shard_map/ppermute | solution.py:525
  365.6 16.1 %collective-permute-start.52 = (bf16[2,224,768]{2,1,0:T(8,128)(2,1)S(1)}, bf16[2,224,768]{2,1,0:T(8,128)(2,1)S(1)}, u32[]{:S(2)}, u32[]{:S(2)}) collective-permute-start(bf16[2,224,768]{2,1,0:T(8,128)(2,1)S(1)} %fusion.48), channel_id=1, source_target_pairs={{0,1},{1,0},{2,3},{3,2},{4,5},{5,4},{6,7},{7,6},{8,9},{9,8},{10,11... | collective-permute-start | bytes 2064392 | tf_op jit(solution)/shard_map/ppermute | solution.py:491
  381.8 29.6 %collective-permute-start.53 = (bf16[224,768]{1,0:T(8,128)(2,1)S(1)}, bf16[224,768]{1,0:T(8,128)(2,1)S(1)}, u32[]{:S(2)}, u32[]{:S(2)}) collective-permute-start(bf16[224,768]{1,0:T(8,128)(2,1)S(1)} %fusion.49), channel_id=1, source_target_pairs={{0,2},{1,3},{2,0},{3,1},{4,6},{5,7},{6,4},{7,5},{8,10},{9,11},{10,... | collective-permute-start | bytes 1032200 | tf_op jit(solution)/shard_map/ppermute | solution.py:491
  390.4 22.7 %collective-permute-start.46 = (bf16[80,768]{1,0:T(8,128)(2,1)S(1)}, bf16[80,768]{1,0:T(8,128)(2,1)S(1)}, u32[]{:S(2)}, u32[]{:S(2)}) collective-permute-start(bf16[80,768]{1,0:T(8,128)(2,1)S(1)} %get-tuple-element.248), channel_id=1, source_target_pairs={{0,3},{1,2},{2,1},{3,0},{4,7},{5,6},{6,5},{7,4},{8,11},{9,10},{10,... | collective-permute-start | bytes 368648 | tf_op jit(solution)/shard_map/ppermute | solution.py:491
  390.5 26.2 %collective-permute-start.45 = (bf16[80,768]{1,0:T(8,128)(2,1)S(1)}, bf16[80,768]{1,0:T(8,128)(2,1)S(1)}, u32[]{:S(2)}, u32[]{:S(2)}) collective-permute-start(bf16[80,768]{1,0:T(8,128)(2,1)S(1)} %get-tuple-element.247), channel_id=1, source_target_pairs={{0,2},{1,3},{2,0},{3,1},{4,6},{5,7},{6,4},{7,5},{8,10},{9,11},{10,... | collective-permute-start | bytes 368648 | tf_op jit(solution)/shard_map/ppermute | solution.py:491
  392.0 24.6 %collective-permute-start.42 = (bf16[80,768]{1,0:T(8,128)(2,1)S(1)}, bf16[80,768]{1,0:T(8,128)(2,1)S(1)}, u32[]{:S(2)}, u32[]{:S(2)}) collective-permute-start(bf16[80,768]{1,0:T(8,128)(2,1)S(1)} %slice_bitcast_fusion.19), channel_id=1, source_target_pairs={{0,1},{1,0},{2,3},{3,2},{4,5},{5,4},{6,7},{7,6},{8,9},{9,8},{10,11... | collective-permute-start | bytes 368648 | tf_op jit(solution)/shard_map/ppermute | solution.py:491
  (123 other events, 899.0 us)

commit v4 on v3

--- a/solution.py
+++ b/solution.py
@@ -30,22 +30,59 @@
     return lax.dot_general(a, b, dims, preferred_element_type=f32)
 
 
-def segment_bounds(pass_len, start, count):
-    rows = pass_len.shape[0]
-    lens = [pass_len[:, j] for j in range(PAIRS)]
-    cuts = [jnp.full((rows,), j * QLEN, jnp.int32) for j in range(PAIRS + 1)]
-    for j in range(PAIRS):
-        cuts.append(cuts[-1] + lens[j])
-    cuts = jnp.stack(cuts, axis=1) + (jnp.arange(rows, dtype=jnp.int32) * ROW_LEN)[:, None]
-    cuts = cuts.reshape(-1)
-    place = start + jnp.arange(count, dtype=jnp.int32)
-    below = cuts[None, :] <= place[:, None]
-    low = jnp.max(jnp.where(below, cuts[None, :], start), axis=1)
-    high = jnp.min(jnp.where(below, rows * ROW_LEN, cuts[None, :]), axis=1)
-    outside = place >= rows * ROW_LEN
-    low = jnp.where(outside, rows * ROW_LEN, low)
-    high = jnp.where(outside, start + count, high)
-    return jnp.clip(low - start, 0, count), jnp.clip(high - start, 0, count)
+def bounds_kernel(halo, own, start_ref, pass_ref, tiles_ref, low_ref, high_ref):
+    start = start_ref[0]
+    count = low_ref.shape[0]
+    rows = pass_ref.shape[0]
+    last = rows * ROW_LEN
+    cuts = []
+    for row in range(rows):
+        cuts += [jnp.int32(row * ROW_LEN + j * QLEN) for j in range(PAIRS + 1)]
+        for j in range(PAIRS):
+            cuts.append(cuts[-1] + pass_ref[row, j])
+
+    def low_of(place):
+        low = jnp.full_like(place, start)
+        for cut in cuts:
+            low = jnp.where(cut <= place, cut, low)
+        return jnp.clip(jnp.where(place >= last, last, low) - start, 0, count)
+
+    def high_of(place):
+        high = jnp.full_like(place, last)
+        for cut in reversed(cuts):
+            high = jnp.where(cut > place, cut, high)
+        return jnp.clip(jnp.where(place >= last, start + count, high) - start, 0, count)
+
+    place = start + lax.broadcasted_iota(jnp.int32, (count, 1), 0)
+    low_ref[...] = low_of(place)
+    high_ref[...] = high_of(place)
+    for tile in range(count // TILE):
+        first = low_of(start + tile * TILE)
+        after_last = high_of(start + tile * TILE + TILE - 1)
+        low = first // ALIGN * ALIGN
+        blocks = (after_last - low + TILE - 1) // TILE
+        tiles_ref[0, tile] = low
+        tiles_ref[1, tile] = blocks
+        if tile * TILE < halo:
+            blocks = jnp.where(after_last > halo, blocks, 0)
+        if tile * TILE >= halo + own:
+            blocks = jnp.where(first < halo + own, blocks, 0)
+        tiles_ref[2, tile] = blocks
+
+
+def segment_bounds(pass_len, start, halo, own):
+    count = own + 2 * halo
+    smem = pl.BlockSpec(memory_space=pltpu.SMEM)
+    vmem = pl.BlockSpec(memory_space=pltpu.VMEM)
+    column = jax.ShapeDtypeStruct((count, 1), jnp.int32)
+    return pl.pallas_call(
+        functools.partial(bounds_kernel, halo, own),
+        out_shape=(jax.ShapeDtypeStruct((3, count // TILE), jnp.int32), column, column),
+        in_specs=[smem, smem],
+        out_specs=(smem, vmem, vmem),
+        compiler_params=pltpu.CompilerParams(vmem_limit_bytes=8 * 2**20),
+        name="bounds",
+    )(start.reshape(1), pass_len)
 
 
 def cls_places(pass_len):
@@ -134,7 +171,7 @@
 
 
 def lasting(micros):
-    return pl.CostEstimate(flops=int(micros * 1e9), bytes_accessed=int(micros * 3.5e6), transcendentals=0)
+    return pl.CostEstimate(flops=int(micros * 2e7), bytes_accessed=int(micros * 7e4), transcendentals=0)
 
 
 def lane_group(array, group, groups):
@@ -157,7 +194,7 @@
         + [lane_group(a, group, groups) for a in arrays],
         out_specs=pl.BlockSpec((rows, width // groups), lambda i: (0, 0)),
         scratch_shapes=[pltpu.VMEM((TILE, keys.shape[0]), f32)],
-        compiler_params=pltpu.CompilerParams(vmem_limit_bytes=32 * 2**20),
+        compiler_params=pltpu.CompilerParams(vmem_limit_bytes=14 * 2**20),
         cost_estimate=lasting(18 / groups),
         name="attend_forward",
     )(tiles, low, high, *arrays)
@@ -232,7 +269,7 @@
             pltpu.VMEM((count, lanes), f32),
             pltpu.VMEM((count, lanes), f32),
         ],
-        compiler_params=pltpu.CompilerParams(vmem_limit_bytes=32 * 2**20),
+        compiler_params=pltpu.CompilerParams(vmem_limit_bytes=20 * 2**20),
         cost_estimate=lasting(42 / groups),
         name="attend_backward",
     )(tiles, low, high, *arrays)
@@ -243,14 +280,14 @@
 PLANE = 8
 
 
-def local(kernel, place, arrays, outs, scratch, micros, name):
+def local(kernel, place, arrays, outs, scratch, micros, name, mib=20):
     return pl.pallas_call(
         kernel,
         out_shape=tuple(jax.ShapeDtypeStruct(shape, dtype) for shape, dtype in outs),
         in_specs=[SMEM] + [VMEM] * len(arrays),
         out_specs=(VMEM,) * len(outs),
         scratch_shapes=[pltpu.VMEM(shape, dtype) for shape, dtype in scratch],
-        compiler_params=pltpu.CompilerParams(vmem_limit_bytes=48 * 2**20),
+        compiler_params=pltpu.CompilerParams(vmem_limit_bytes=mib * 2**20),
         cost_estimate=lasting(micros),
         name=name,
     )(place, *arrays)
@@ -322,7 +359,7 @@
     place_ref, left_ref, tokens_ref, right_ref, own_ref, *refs
 ):
     halves, refs = by_eighth(refs[:5]), refs[5:]
-    bq_ref, bv_ref, q_ref, k_ref, v_ref, w_ref, x_ref, stage_ref = refs
+    bias_ref, q_ref, k_ref, v_ref, w_ref, x_ref, stage_ref = refs
     ways = halves[0][0].shape[0] + 1
     heads = own_ref.shape[1] // 24
     halo = left_ref.shape[0]
@@ -342,10 +379,10 @@
     def step(i, carry):
         rows = pl.ds(pl.multiple_of(i * 256, 256), 256)
         x = x_ref[rows, :]
-        q = mm(x, w_ref[:width], NT) + bq_ref[...]
+        q = mm(x, w_ref[:width], NT) + bias_ref[0:1]
         q_ref[rows, :] = (q * (1.0 / math.sqrt(HEAD))).astype(bf16)
         k_ref[rows, :] = mm(x, w_ref[pl.ds(width, width)], NT).astype(bf16)
-        v_ref[rows, :] = (mm(x, w_ref[pl.ds(2 * width, width)], NT) + bv_ref[...]).astype(bf16)
+        v_ref[rows, :] = (mm(x, w_ref[pl.ds(2 * width, width)], NT) + bias_ref[1:2]).astype(bf16)
         return carry
 
     lax.fori_loop(0, x_ref.shape[0] // 256, step, 0)
@@ -377,6 +414,70 @@
         for h in range(heads):
             block = head_block(stage_ref, h)
             out_ref[pl.ds((member * heads + h) * HEAD, HEAD), :] = block.astype(bf16)
+
+
+def split_digits(values):
+    digits = []
+    for _ in range(3):
+        digits.append(values.astype(bf16))
+        values = values - digits[-1].astype(f32)
+    return digits
+
+
+def biases_kernel(place_ref, along_ref, in_ref, q_ref, v_ref, heads_ref, units_ref, line_ref):
+    place = place_ref[0]
+    ways = along_ref.shape[0] + 1
+    inner = q_ref.shape[1]
+    rows = in_ref.shape[1] // PLANE
+    first = along_ref.shape[1] - 8
+    others = along_ref[:, first:, :].astype(f32)
+    digits = split_digits(jnp.concatenate([q_ref[...], v_ref[...]], axis=1))
+    digits = [digit.astype(f32) for digit in digits]
+    for member in range(ways - 1):
+        digits.append(others[member, 3:6, : 2 * inner])
+    digits = jnp.concatenate(digits, axis=0).astype(bf16)
+    lane = lax.broadcasted_iota(jnp.int32, (2 * inner, 2 * inner), 0)
+    to = lax.broadcasted_iota(jnp.int32, (2 * inner, 2 * inner), 1)
+    chosen = jnp.where((lane ^ (place << 3)) == to, 1.0, 0.0).astype(bf16)
+    moved = mm(digits, chosen)
+    sums = [moved[3 * m : 3 * m + 1] + moved[3 * m + 1 : 3 * m + 2] + moved[3 * m + 2 : 3 * m + 3] for m in range(ways)]
+    heads_ref[0:1] = jnp.concatenate([value[:, :inner] for value in sums], axis=1)
+    heads_ref[1:2] = jnp.concatenate([value[:, inner:] for value in sums], axis=1)
+    for member in range(ways):
+        if member == 0:
+            value = in_ref[...]
+        else:
+            three = others[member - 1]
+            value = three[0:1] + three[1:2] + three[2:3]
+        for p in range(PLANE):
+            line_ref[member * PLANE + p, 0:1, :rows] = value[:, p * rows : (p + 1) * rows]
+    held = [
+        line_ref[member * PLANE + (place ^ j), 0:1, :rows] for j in range(PLANE) for member in range(ways)
+    ]
+    units_ref[...] = jnp.concatenate(held, axis=1)
+
+
+def vectors_kernel(place_ref, *refs):
+    stat_refs, (units_ref, out_ref, line_ref) = refs[:6], refs[6:]
+    place, own = place_ref[0], place_ref[1]
+    ways, _, width = out_ref.shape
+    inner = width // ways
+    rows = units_ref.shape[1] // PLANE // ways
+    for j in range(PLANE):
+        for member in range(ways):
+            at = j * ways + member
+            line_ref[at, 0:1, :rows] = units_ref[:, at * rows : (at + 1) * rows]
+    stats = jnp.concatenate([ref[...] for ref in stat_refs], axis=0)
+    parts = [stats[:, i * inner : (i + 1) * inner] for i in range(ways)]
+    for member in range(ways):
+        held = [line_ref[(place ^ p) * ways + member, 0:1, :rows] for p in range(PLANE)]
+        mine = parts[0]
+        for i in range(1, ways):
+            mine = jnp.where((own ^ member) == i, parts[i], mine)
+        norms = jnp.concatenate([mine[i : i + 1] for i in range(6)], axis=1)
+        norms = jnp.concatenate([norms, jnp.zeros((1, 2 * inner), f32)], axis=1)
+        lines = [jnp.concatenate(held, axis=1), norms[:, :width], norms[:, width:]]
+        out_ref[member] = jnp.concatenate([*lines, jnp.zeros((5, width), f32)], axis=0)
 
 
 def put_heads(ways, heads, sum_ref, kind, first_head, block):
@@ -421,7 +522,7 @@
     to = lax.broadcasted_iota(jnp.int32, (width, width), 1)
     member = sum((lane >= i * inner).astype(jnp.int32) for i in range(1, ways))
     within = lane - member * inner
-    spot = (within & ~(HEAD - 8)) | ((((within >> 3) & 7) ^ place) << 3)
+    spot = within ^ (place << 3)
     row = lax.broadcasted_iota(jnp.int32, (8, width), 0)
     column = lax.broadcasted_iota(jnp.int32, (8, width), 1)
     of = sum((column >= i * inner).astype(jnp.int32) for i in range(1, ways))
@@ -608,7 +709,7 @@
     piece_rows = units // PLANE
     heads = inner // HEAD
     part = inner // PLANE
-    place = ((data_index & CORE) << 2 | (data_index % PLANE) >> 1).reshape(1)
+    place = jnp.stack([(data_index & CORE) << 2 | (data_index % PLANE) >> 1, mp_index])
     (qkv_own,) = local(
         own_heads_kernel, place, (w_query.T, w_key.T, w_value.T), [((PLANE, 3 * part, width), bf16)],
         [((3 * heads * PLANE, 8, width), f32)], 4, "own_heads",
@@ -641,48 +742,25 @@
     while level > 1:
         in_held = bit_step(in_held, level)
         level //= 2
-    qkv_held = second_step(after(qkv_pairs, in_held))
+    qkv_held = second_step(after(qkv_pairs, in_held, tokens_before, tokens_after))
     in_along = others_of(bit_step(in_held, 1))
     qkv_parts = core_step(after(qkv_held, in_along))
     back_held = bit_step({0: after(back_piece, in_along, qkv_held)}, ways // 2)
     in_along = after(in_along, qkv_parts)
     in_pairs = first_step(in_along)
-    bias_rest = after(qkv_along, qkv_parts)[:, 3 * part :].astype(f32)
-    bias_in_rest = bias_rest[:, 0] + bias_rest[:, 1] + bias_rest[:, 2]
-    bias_head_rest = bias_rest[:, 3] + bias_rest[:, 4] + bias_rest[:, 5]
-    bias_in_all = jnp.concatenate([b_in[None], bias_in_rest])
-    bias_heads = jnp.concatenate(
-        [jnp.concatenate([b_query, b_value])[None], bias_head_rest[:, : 2 * inner]]
-    )
-
-    def in_order(parts):
-        split = parts.reshape(*parts.shape[:-2], 2, 2, 2, parts.shape[-1])
-        for axis, bit in ((-4, CORE), (-3, NEAR_Y), (-2, NEAR_X)):
-            split = jnp.where((data_index & bit) != 0, jnp.flip(split, axis), split)
-        return split.reshape(parts.shape)
-
-    bias_heads = in_order(bias_heads.reshape(ways, 2 * heads, PLANE, 8)).reshape(ways, 2, inner)
-    bias_query = bias_heads[:, 0].reshape(1, width)
-    bias_value = bias_heads[:, 1].reshape(1, width)
-    bias_in = in_order(bias_in_all.reshape(ways, PLANE, piece_rows))
-    bias_in = bias_in.transpose(1, 0, 2).reshape(-1)
-
-    low, high = segment_bounds(pass_len, mp_index * own_rows - halo, count)
-    tile_low = low[::TILE] // ALIGN * ALIGN
-    tile_high = high[TILE - 1 :: TILE]
-    blocks = (tile_high - tile_low + TILE - 1) // TILE
-    tile = jnp.arange(count // TILE, dtype=jnp.int32)
-    before_own = tile < halo // TILE
-    after_own = tile >= (halo + own_rows) // TILE
-    reach = (~before_own | (tile_high > halo)) & (~after_own | (low[::TILE] < halo + own_rows))
-    tiles = jnp.stack([tile_low, blocks, jnp.where(reach, blocks, 0)])
-    bounds = (tiles, low[:, None], high[:, None])
+    bias_heads, bias_in = local(
+        biases_kernel, place,
+        (after(qkv_along, qkv_held), b_in[None], b_query[None], b_value[None]),
+        [((2, width), f32), ((1, ways * units), f32)], [((ways * PLANE, 8, 128), f32)], 2, "biases",
+    )
+
+    bounds = segment_bounds(pass_len, mp_index * own_rows - halo, halo, own_rows)
 
     tokens_before = after(tokens_before, in_along)
-    qkv = (tokens_before, tokens, tokens_after, qkv_own, *qkv_parts, bias_query, bias_value)
+    qkv = (tokens_before, tokens, tokens_after, qkv_own, *qkv_parts, bias_heads)
     queries, keys, values, qkv_all = local(
         project_kernel, place, qkv, [((count, width), bf16)] * 3 + [((3 * width, width), bf16)],
-        [((count, width), bf16), ((PLANE, 3 * part, width), f32)], 10, "project",
+        [((count, width), bf16), ((PLANE, 3 * part, width), f32)], 10, "project", 32,
     )
     own_queries = queries[halo : halo + own_rows]
     back_held = after(back_held, queries)
@@ -693,8 +771,8 @@
     back_along = others_of(back_held)
     own_queries = after(own_queries, in_pairs)
     context = [attend_forward(bounds, own_queries, keys, values, halo, 0, 2)]
-    in_held = second_step(in_pairs)
-    back_along = after(back_along, in_held, context[0])
+    in_held = after(second_step(in_pairs), context[0])
+    back_along = after(back_along, in_held)
     back_pairs = first_step(back_along)
     own_queries = after(own_queries, in_held, context[0])
     in_parts = core_step(in_held)
@@ -763,9 +841,9 @@
 
     grad_second = norm_pull(grad_mixed, unit_two, inverse_two, ln2_gain)
     stats = [
-        jnp.sum(grad_mixed * unit_two, axis=0),
-        jnp.sum(grad_mixed, axis=0),
-        jnp.sum(grad_second, axis=0),
+        jnp.sum(grad_mixed * unit_two, axis=0, keepdims=True),
+        jnp.sum(grad_mixed, axis=0, keepdims=True),
+        jnp.sum(grad_second, axis=0, keepdims=True),
     ]
     second_low = grad_second.astype(bf16)
 
@@ -784,13 +862,15 @@
     back_half = swap(back_sum[1], NEAR_Y)
     in_sent = to_core(grad_before, hidden_low)
     in_arrived = swap(in_sent, CORE)
-    pulled = after(grad_before, in_sent, back_sum)
+    in_sum = chip_sum(grad_before, hidden_low, in_arrived)
+    in_half = swap(in_sum[:, 1], NEAR_X)
+    pulled = after(grad_before, back_sum, in_sum)
     grad_hidden = grad_second + mm(pulled, in_all)
     grad_first = norm_pull(grad_hidden, unit_one, inverse_one, ln1_gain)
     stats += [
-        jnp.sum(grad_hidden * unit_one, axis=0),
-        jnp.sum(grad_hidden, axis=0),
-        jnp.sum(grad_first, axis=0),
+        jnp.sum(grad_hidden * unit_one, axis=0, keepdims=True),
+        jnp.sum(grad_hidden, axis=0, keepdims=True),
+        jnp.sum(grad_first, axis=0, keepdims=True),
     ]
     first_low = grad_first.astype(bf16)
     first_before, first_after = halo_rows(first_low, halo)
@@ -798,23 +878,14 @@
         functools.partial(out_grads_kernel, ways), place, (*context, first_low),
         [((4 * ways, part + 8, width), bf16)] * 2, [((8 * ways, part + 8, width), f32)], 3, "out_grads",
     )
-    out_arrived = swap(out_sent, CORE)
-    in_sum = chip_sum(after(grad_before, out_sent), hidden_low, in_arrived)
-    out_sum = add(out_keep, out_arrived).reshape(2, 2, ways, part + 8, width)
-    in_sum = jnp.concatenate([in_sum, out_sum], axis=3)
-    in_half = swap(in_sum[:, 1], NEAR_X)
-    d_b_in = jnp.sum(grad_before, axis=0, dtype=f32).reshape(PLANE, ways, piece_rows)
-
-    d_b_in = in_order(d_b_in.transpose(1, 0, 2)).reshape(ways, 1, units)
-    turned = jnp.stack(stats).reshape(6, ways, inner).transpose(1, 0, 2)
-    level = 1
-    while level < ways:
-        split = turned.reshape(-1, 2, level, *turned.shape[1:])
-        flipped = jnp.where((mp_index & level) != 0, jnp.flip(split, 1), split)
-        turned = flipped.reshape(turned.shape)
-        level *= 2
-    turned = jnp.pad(turned.reshape(ways, -1), ((0, 0), (0, 2 * inner))).reshape(ways, 2, width)
-    vectors = jnp.concatenate([d_b_in, turned, jnp.zeros((ways, 5, width), f32)], axis=1)
+    out_sum = add(out_keep, swap(out_sent, CORE)).reshape(2, 2, ways, part + 8, width)
+    out_half = swap(out_sum[1], NEAR_Y)
+
+    d_b_in = jnp.sum(grad_before, axis=0, dtype=f32, keepdims=True)
+    (vectors,) = local(
+        vectors_kernel, place, (*stats, d_b_in), [((ways, 8, width), f32)],
+        [((ways * PLANE, 8, 128), f32)], 2, "vectors",
+    )
 
     first_window = jnp.concatenate([first_before, first_low, first_after])
     grad_context = mm(first_window, out_all, NT).astype(bf16)
@@ -824,45 +895,48 @@
     def attend(grads, group):
         return attend_backward(bounds, queries, keys, values, grads, halo, group, groups)
 
-    grad_context = after(grad_context, in_sum, back_sum, vectors)
+    grad_context = after(grad_context, in_sum, back_sum, out_sum, vectors)
     parts.append(attend(grad_context, 0))
-    grad_context = after(grad_context, parts[0])
-    parts.append(attend(grad_context, 1))
-    back_half, in_half = after((back_half, in_half), parts[1])
+    back_half, in_half, out_half = after((back_half, in_half, out_half), parts[0])
     back_sum = add(back_sum[0], back_half)
     in_sum = add(in_sum[:, 0], in_half)
+    out_sum = add(out_sum[0], out_half)
     back_half = swap(back_sum[1], NEAR_X)
     in_half = swap(in_sum[1], NEAR_Y)
-    grad_context = after(grad_context, back_sum, in_sum, parts[1])
+    out_half = swap(out_sum[1], NEAR_X)
+    grad_context = after(grad_context, back_sum, in_sum, out_sum, parts[0])
+    parts.append(attend(grad_context, 1))
+    halves = [(back_sum[0], back_half), (in_sum[0], in_half), (out_sum[0], out_half)]
+    halves = after(halves, parts[1])
+    early_sum = jnp.concatenate([add(*half) for half in halves], axis=1)
+    early_parts = [early_sum[i] for i in range(ways)]
+    early_odd = jnp.stack(early_parts[1::2])
+    grad_context, early_odd = lax.optimization_barrier((grad_context, early_odd))
+    early_odd = partner(early_odd, 1)
     parts.append(attend(grad_context, 2))
-    back_half, in_half = after((back_half, in_half), parts[2])
-    early_sum = jnp.concatenate([add(back_sum[0], back_half), add(in_sum[0], in_half)], axis=1)
-    early_parts = [early_sum[i] for i in range(ways)]
-    early_odd = partner(jnp.stack(early_parts[1::2]), 1)
+    early_odd = after(early_odd, parts[2])
+    early_parts = [add(even, odd) for even, odd in zip(early_parts[::2], early_odd)]
     tokens_low = after(tokens, early_parts)
 
     grad_parts = [g[i] for i in range(3) for g in parts]
     late_rows = 3 * part + 8
     late_keep, late_sent = local(
         functools.partial(piece_grads_kernel, groups), place, (*grad_parts, tokens_low, vectors),
-        [((4 * ways, late_rows, width), bf16)] * 2, [((8 * ways, late_rows, width), f32)], 8, "piece_grads",
+        [((4 * ways, late_rows, width), bf16)] * 2, [((8 * ways, late_rows, width), f32)], 8, "piece_grads", 36,
     )
     late_sum = add(late_keep, swap(late_sent, CORE)).reshape(2, 2, ways, late_rows, width)
+    level, early_own = 2, early_parts[0].astype(f32)
+    while level < ways:
+        early_own = early_own + after(partner(early_parts[level // 2], level), late_keep).astype(f32)
+        level *= 2
+    early_held = first_step(over_groups(early_own).astype(bf16)[None])
     halves = first_sum_step(late_sum)
-    early_odd = after(early_odd, halves)
-    early_parts = [add(even, odd) for even, odd in zip(early_parts[::2], early_odd)]
+    early_held = second_step(after(early_held, late_sum))
     halves = second_sum_step(halves)
     late_parts = [half[i] for half in (add(*h) for h in halves) for i in range(ways // 2)]
-    level, early_own = 2, early_parts[0].astype(f32)
-    while level < ways:
-        early_own = early_own + after(partner(early_parts[level // 2], level), late_parts).astype(f32)
-        level *= 2
-    early_own = over_groups(early_own).astype(bf16)
-    early_held = second_step(first_step(after(early_own, late_parts)[None]))
+    early_pieces = core_step(after(early_held, late_parts))
     late_total = sum_along(late_parts)
-    late_held = second_step(first_step(late_total.astype(bf16)[None]))
-    late_pieces = core_step(late_held)
-    early_pieces = core_step(early_held)
+    late_pieces = core_step(second_step(first_step(late_total.astype(bf16)[None])))
     line = late_total[3 * part :]
     grad_queries, grad_keys, grad_values = (jnp.concatenate(p, axis=1) for p in zip(*parts))
     d_tokens = (

time: 447 us -> 407 us (0.911)
  waiting for transfers between devices: 81.9 us -> 124 us
  local copies, waits for them, and re-layouts: 63 us -> 34.8 us
  other arithmetic: 47.6 us -> 21 us
  matrix products: 67.1 us -> 51.1 us
  starting transfers between devices: 85.3 us -> 71.5 us
    ppermute x37 -> x39, waiting for transfers between devices: 34.8 us -> 57.6 us  [swap(): return lax.ppermute(values, 'dp', [(i, i ^ bit) for i in range(ways)])]
    ppermute x15, starting transfers between devices: 29.5 us -> 12.9 us  [partner(): return lax.ppermute(values, 'mp', [(i, i ^ step) for i in range(ways)])]
    dot_general x16, matrix products: 61.7 us -> 45.4 us  [mm(): return lax.dot_general(a, b, dims, preferred_element_type=f32)]
    another operation x19 -> x6, local copies, waits for them, and re-layouts: 15.2 us -> 0.01 us  [the longest x7 7.43 us: shards(): turned = jnp.stack(stats).reshape(6, ways, inner).transpose(1, 0, 2)]
    ppermute x15, waiting for transfers between devices: 38.7 us -> 50.2 us  [partner(): return lax.ppermute(values, 'mp', [(i, i ^ step) for i in range(ways)])]
    unnamed x179 -> x156, local copies, waits for them, and re-layouts: 18.2 us -> 23.8 us
    another operation x13 -> x9, other arithmetic: 11.6 us -> 6.08 us  [core_step(): return [*held, swap(jnp.stack(held), CORE)]]
    pallas_call x9 -> x11, Pallas kernels: 31.4 us -> 26 us  [local(): pl.pallas_call(kernel, out_shape=tuple((jax.ShapeDtypeStruct(shape, dtype...]
  transfers between devices with their start and end apart: 59 -> 61, of which waited for: 19 -> 29; matrix products, arithmetic and copies ran while one was open for 29% -> 9% of each run, Pallas kernels for 19% -> 21%
where the time goes in v4:
time: 407 us; the launch traced here: 401 us
  waiting for transfers between devices  124 us (30%)
  Pallas kernels  96 us (24%)
  starting transfers between devices  71.5 us (18%)
  matrix products  51.1 us (13%)
  local copies, waits for them, and re-layouts  34.8 us (9%)
  other arithmetic  21 us (5%)
    ppermute x39, waiting for transfers between devices, swap(): return lax.ppermute(values, 'dp', [(i, i ^ bit) for i in range(ways)])  57.6 us
    ppermute x15, waiting for transfers between devices, partner(): return lax.ppermute(values, 'mp', [(i, i ^ step) for i in range(ways)])  50.2 us
    pallas_call x3, Pallas kernels, attend_backward(): pl.pallas_call(functools.partial(backward_kernel, halo), grid=(1,), out_s...  48.6 us
    ppermute x39, starting transfers between devices, swap(): return lax.ppermute(values, 'dp', [(i, i ^ bit) for i in range(ways)])  45.7 us
    dot_general x16, matrix products, mm(): return lax.dot_general(a, b, dims, preferred_element_type=f32)  45.4 us
    pallas_call x11, Pallas kernels, local(): pl.pallas_call(kernel, out_shape=tuple((jax.ShapeDtypeStruct(shape, dtype...  26 us
    unnamed x156, local copies, waits for them, and re-layouts  23.8 us
    pallas_call x2, Pallas kernels, attend_forward(): pl.pallas_call(functools.partial(forward_kernel, halo), grid=(1,), out_sh...  17.2 us
  transfers between devices with their start and end apart: 61, of which 29 were waited for; matrix products, arithmetic and copies ran while one was open for 9% of the time, Pallas kernels for 21%

profile of v4, /device:TPU:1, one launch (start us, length us, event | category | flops | bytes accessed | tf_op | source)
XLA Modules:
  0.0 400.8 jit_solution(9537665455095735567)
XLA Ops:
  8.9 4.2 %collective-permute-start.3 = (bf16[80,768]{1,0:T(8,128)(2,1)S(1)}, bf16[80,768]{1,0:T(8,128)(2,1)S(1)}, u32[]{:S(2)}, u32[]{:S(2)}) collective-permute-start(bf16[80,768]{1,0:T(8,128)(2,1)S(1)} %fusion.55), channel_id=1, source_target_pairs={{0,3},{1,2},{2,1},{3,0},{4,7},{5,6},{6,5},{7,4},{8,11},{9,10},{10,... | collective-permute-start | bytes 368648 | tf_op jit(solution)/shard_map/ppermute | solution.py:592
  14.9 4.0 %collective-permute-start = (bf16[256,768]{1,0:T(8,128)(2,1)S(1)}, bf16[256,768]{1,0:T(8,128)(2,1)S(1)}, u32[]{:S(2)}, u32[]{:S(2)}) collective-permute-start(bf16[256,768]{1,0:T(8,128)(2,1)S(1)} %get-tuple-element.237), channel_id=1, source_target_pairs={{0,1},{1,2},{2,3},{4,5},{5,6},{6,7},{8,9},{9,10},{10,11},{12,13},{... | collective-permute-start | bytes 1179656 | tf_op jit(solution)/shard_map/ppermute | solution.py:597
  24.7 15.3 %collective-permute-done.4 = bf16[1,128,768]{2,1,0:T(8,128)(2,1)S(1)} collective-permute-done((bf16[1,128,768]{2,1,0:T(8,128)(2,1)S(1)}, bf16[1,128,768]{2,1,0:T(8,128)(2,1)S(1)}, u32[]{:S(2)}, u32[]{:S(2)}) %collective-permute-start.4) | collective-permute-done | bytes 196640 | tf_op jit(solution)/shard_map/ppermute | solution.py:592
  63.4 6.8 %collective-permute-done.12 = bf16[3,64,768]{2,1,0:T(8,128)(2,1)S(1)} collective-permute-done((bf16[3,64,768]{2,1,0:T(8,128)(2,1)S(1)}, bf16[3,64,768]{2,1,0:T(8,128)(2,1)S(1)}, u32[]{:S(2)}, u32[]{:S(2)}) %collective-permute-start.12) | collective-permute-done | bytes 294944 | tf_op jit(solution)/shard_map/ppermute | solution.py:626
  73.3 4.2 %bounds.1 = (s32[3,10]{1,0:T(4,128)S(1)}, s32[1280,1]{1,0:T(8,128)S(1)}, s32[1280,1]{1,0:T(8,128)S(1)}) custom-call(s32[1]{0:T(128)} %bitcast.start_ref, s32[3,4]{1,0:T(4,128)S(1)} %copy-done.49), custom_call_target="tpu_custom_call" | custom-call | tf_op jit(solution)/shard_map/bounds/pallas_call | solution.py:78
  90.3 6.7 %project.1 = (bf16[1280,768]{1,0:T(8,128)(2,1)S(1)}, bf16[1280,768]{1,0:T(8,128)(2,1)S(1)}, bf16[1280,768]{1,0:T(8,128)(2,1)S(1)}, bf16[2304,768]{1,0:T(8,128)(2,1)S(1)}) custom-call(s32[2]{0:T(128)S(1)} %pad_add_fusion.place_ref, bf16[256,768]{1,0:T(8,128)(2,1)S(1)} %copy-done.42, bf16[768,768]{1,0:T(8,128)(2,1)S(1)} %copy-done.6, ...), custom_call_target="tpu_custom_call" | custom-call | flops 200000000 | bytes 700000 | tf_op jit(solution)/shard_map/project/pallas_call | solution.py:284
  97.2 8.4 %attend_forward.2.left_ref = bf16[768,384]{1,0:T(8,128)(2,1)S(1)} custom-call(s32[3,10]{1,0:T(4,128)S(1)} %get-tuple-element.116.tiles_ref, s32[1280,1]{1,0:T(8,128)S(1)} %get-tuple-element.117.lo_ref, s32[1280,1]{1,0:T(8,128)S(1)} %get-tuple-element.118.hi_ref, bf16[768,768]{1,0:T(8,128)(2,1)S(1)} %slice.293.q_ref, ...), custom_call_target="tpu_custom_call" | custom-call | flops 180000000 | bytes 630000 | tf_op jit(solution)/shard_map/attend_forward/pallas_call | solution.py:189
  112.9 8.5 %collective-permute-done.15 = bf16[2,96,768]{2,1,0:T(8,128)(2,1)S(1)} collective-permute-done((bf16[2,96,768]{2,1,0:T(8,128)(2,1)S(1)}, bf16[2,96,768]{2,1,0:T(8,128)(2,1)S(1)}, u32[]{:S(2)}, u32[]{:S(2)}) %collective-permute-start.15) | collective-permute-done | bytes 294944 | tf_op jit(solution)/shard_map/ppermute | solution.py:592
  124.4 4.5 %collective-permute-done.19 = bf16[3,48,768]{2,1,0:T(8,128)(2,1)} collective-permute-done((bf16[3,48,768]{2,1,0:T(8,128)(2,1)}, bf16[3,48,768]{2,1,0:T(8,128)(2,1)}, u32[]{:S(2)}, u32[]{:S(2)}) %collective-permute-start.19) | collective-permute-done | bytes 221216 | tf_op jit(solution)/shard_map/ppermute | solution.py:626
  134.3 8.8 %attend_forward.3.right_ref = bf16[768,384]{1,0:T(8,128)(2,1)S(1)} custom-call(s32[3,10]{1,0:T(4,128)S(1)} %get-tuple-element.116.tiles_ref, s32[1280,1]{1,0:T(8,128)S(1)} %get-tuple-element.117.lo_ref, s32[1280,1]{1,0:T(8,128)S(1)} %get-tuple-element.118.hi_ref, bf16[768,768]{1,0:T(8,128)(2,1)S(1)} %copy-done.10, ...), custom_call_target="tpu_custom_call" | custom-call | flops 180000000 | bytes 630000 | tf_op jit(solution)/shard_map/attend_forward/pallas_call | solution.py:189
  153.2 9.1 %fusion.4 = (bf16[768,3072]{1,0:T(8,128)(2,1)}, bf16[768,3072]{1,0:T(8,128)(2,1)S(1)}) fusion(f32[3072]{0:T(1024)S(1)} %bitcast.246, bf16[768,768]{1,0:T(8,128)(2,1)S(1)} %fusion.14, bf16[3072,768]{1,0:T(8,128)(2,1)S(1)} %get-tuple-element.154), kind=kOutput, calls=%fused_computation.5 | convolution fusion | flops 3652190208 | bytes 15347712 | tf_op jit(solution)/shard_map/dot_general | solution.py:30
  164.4 4.1 %fusion.98 = (f32[768]{0:T(1024)S(1)}, f32[768,768]{1,0:T(8,128)S(1)}) fusion(f32[768]{0:T(1024)S(1)} %copy-done.68, bf16[768,3072]{1,0:T(8,128)(2,1)S(1)} %get-tuple-element.156, bf16[3072,768]{1,0:T(8,128)(2,1)S(1)} %join_back.1, f32[768]{0:T(1024)S(1)} %copy-done.65, f32[768]{0:T(1024)S(1)} %copy-done.62, f32[768]{0:T(1024)S(1)} %add_rsqrt_fusion.1, ...), kind=kOutput, calls=%fused_computation.241 | convolution fusion | flops 3628006656 | bytes 14174208 | tf_op jit(solution)/shard_map/dot_general | solution.py:30
  187.1 4.9 %collective-permute-done.29 = bf16[4,32,768]{2,1,0:T(8,128)(2,1)} collective-permute-done((bf16[4,32,768]{2,1,0:T(8,128)(2,1)S(1)}, bf16[4,32,768]{2,1,0:T(8,128)(2,1)}, u32[]{:S(2)}, u32[]{:S(2)}) %collective-permute-start.29) | collective-permute-done | bytes 196640 | tf_op jit(solution)/shard_map/ppermute | solution.py:612
  199.9 4.3 %multiply_reduce_fusion.1 = (f32[768]{0:T(1024)S(1)}, f32[768]{0:T(1024)S(1)}, f32[768]{0:T(1024)S(1)}, f32[768]{0:T(1024)S(1)}, f32[768,768]{1,0:T(8,128)S(1)}) fusion(f32[768,768]{1,0:T(8,128)} %copy-done.55, f32[768]{0:T(1024)S(1)} %add_rsqrt_fusion, f32[768]{0:T(1024)S(1)} %broadcast_multiply_fusion.4, f32[768]{0:T(1024)S(1)} %copy-done.61, ...), kind=kOutput, calls=%fused_computation.25 | convolution fusion | flops 176391168 | bytes 5993568 | tf_op jit(solution)/shard_map/dot_general | solution.py:838
  207.5 7.7 %convert_reduce_fusion = (f32[3072]{0:T(1024)S(1)}, bf16[768,3072]{1,0:T(8,128)(2,1)}) fusion(bf16[768,3072]{1,0:T(8,128)(2,1)} %get-tuple-element.158, bf16[768,768]{1,0:T(8,128)(2,1)S(1)} %convert_element_type.274, bf16[3072,768]{1,0:T(8,128)(2,1)S(1)} %bitcast.221), kind=kOutput, calls=%fused_computation.6 | convolution fusion | flops 3635672064 | bytes 15347712 | tf_op jit(solution)/shard_map/dot_general | solution.py:30
  221.3 4.1 %collective-permute-done.31 = bf16[1536,768]{1,0:T(8,128)(2,1)S(1)} collective-permute-done((bf16[1536,768]{1,0:T(8,128)(2,1)S(1)}, bf16[1536,768]{1,0:T(8,128)(2,1)S(1)}, u32[]{:S(2)}, u32[]{:S(2)}) %collective-permute-start.31) | collective-permute-done | bytes 2359328 | tf_op jit(solution)/shard_map/ppermute | solution.py:626
  231.0 4.5 %multiply_reduce_fusion = (f32[768]{0:T(1024)S(1)}, f32[768]{0:T(1024)S(1)}, f32[768]{0:T(1024)S(1)}, f32[768]{0:T(1024)S(1)}, f32[768,768]{1,0:T(8,128)S(1)}) fusion(f32[768,768]{1,0:T(8,128)S(1)} %copy-done.54, f32[768]{0:T(1024)S(1)} %add_rsqrt_fusion.1, f32[768]{0:T(1024)S(1)} %broadcast_multiply_fusion.5, f32[768]{0:T(1024)S(1)} %copy-done.62, ...), kind=kOutput, calls=%fused_computation.24 | convolution fusion | flops 3629773824 | bytes 16536576 | tf_op jit(solution)/shard_map/dot_general | solution.py:30
  257.1 16.0 %attend_backward.3 = (bf16[768,256]{1,0:T(8,128)(2,1)S(1)}, bf16[768,256]{1,0:T(8,128)(2,1)S(1)}, bf16[768,256]{1,0:T(8,128)(2,1)S(1)}) custom-call(s32[3,10]{1,0:T(4,128)S(1)} %get-tuple-element.116.tiles_ref, s32[1280,1]{1,0:T(8,128)S(1)} %get-tuple-element.117.lo_ref, s32[1280,1]{1,0:T(8,128)S(1)} %get-tuple-element.118.hi_ref, ...), custom_call_target="tpu_custom_call" | custom-call | flops 280000000 | bytes 980000 | tf_op jit(solution)/shard_map/attend_backward/pallas_call | solution.py:260
  280.1 16.3 %attend_backward.4 = (bf16[768,256]{1,0:T(8,128)(2,1)S(1)}, bf16[768,256]{1,0:T(8,128)(2,1)S(1)}, bf16[768,256]{1,0:T(8,128)(2,1)S(1)}) custom-call(s32[3,10]{1,0:T(4,128)S(1)} %get-tuple-element.116.tiles_ref, s32[1280,1]{1,0:T(8,128)S(1)} %get-tuple-element.117.lo_ref, s32[1280,1]{1,0:T(8,128)S(1)} %get-tuple-element.118.hi_ref, ...), custom_call_target="tpu_custom_call" | custom-call | flops 280000000 | bytes 980000 | tf_op jit(solution)/shard_map/attend_backward/pallas_call | solution.py:260
  297.0 16.3 %attend_backward.5 = (bf16[768,256]{1,0:T(8,128)(2,1)S(1)}, bf16[768,256]{1,0:T(8,128)(2,1)S(1)}, bf16[768,256]{1,0:T(8,128)(2,1)S(1)}) custom-call(s32[3,10]{1,0:T(4,128)S(1)} %get-tuple-element.116.tiles_ref, s32[1280,1]{1,0:T(8,128)S(1)} %get-tuple-element.117.lo_ref, s32[1280,1]{1,0:T(8,128)S(1)} %get-tuple-element.118.hi_ref, ...), custom_call_target="tpu_custom_call" | custom-call | flops 280000000 | bytes 980000 | tf_op jit(solution)/shard_map/attend_backward/pallas_call | solution.py:260
  314.6 4.4 %piece_grads.1 = (bf16[16,80,768]{2,1,0:T(8,128)(2,1)S(1)}, bf16[16,80,768]{2,1,0:T(8,128)(2,1)S(1)}) custom-call(s32[2]{0:T(128)S(1)} %pad_add_fusion.place_ref, bf16[768,256]{1,0:T(8,128)(2,1)S(1)} %get-tuple-element.161.refs_0_, bf16[768,256]{1,0:T(8,128)(2,1)S(1)} %get-tuple-element.170.refs_1_, bf16[768,256]{1,0:T(8,128)(2,1)S(1)} %get-tuple-element.180.refs_2_, ...), custom_call_target="tpu_custom_call" | custom-call | flops 160000000 | bytes 560000 | tf_op jit(solution)/shard_map/piece_grads/pallas_call | solution.py:284
  322.3 16.8 %collective-permute-done.55 = bf16[224,768]{1,0:T(8,128)(2,1)S(1)} collective-permute-done((bf16[224,768]{1,0:T(8,128)(2,1)S(1)}, bf16[224,768]{1,0:T(8,128)(2,1)S(1)}, u32[]{:S(2)}, u32[]{:S(2)}) %collective-permute-start.55) | collective-permute-done | bytes 344096 | tf_op jit(solution)/shard_map/ppermute | solution.py:592
  343.7 12.0 %collective-permute-done.57 = bf16[1,112,768]{2,1,0:T(8,128)(2,1)S(1)} collective-permute-done((bf16[1,112,768]{2,1,0:T(8,128)(2,1)S(1)}, bf16[1,112,768]{2,1,0:T(8,128)(2,1)S(1)}, u32[]{:S(2)}, u32[]{:S(2)}) %collective-permute-start.57) | collective-permute-done | bytes 172064 | tf_op jit(solution)/shard_map/ppermute | solution.py:626
  363.9 7.8 %collective-permute-done.44 = bf16[2,80,768]{2,1,0:T(8,128)(2,1)S(1)} collective-permute-done((bf16[2,80,768]{2,1,0:T(8,128)(2,1)S(1)}, bf16[2,80,768]{2,1,0:T(8,128)(2,1)S(1)}, u32[]{:S(2)}, u32[]{:S(2)}) %collective-permute-start.44) | collective-permute-done | bytes 245792 | tf_op jit(solution)/shard_map/ppermute | solution.py:626
  (421 shorter events, 198.4 us)
Async XLA Ops:
  13.6 31.4 %collective-permute-start.8 = (bf16[256,768]{1,0:T(8,128)(2,1)S(1)}, bf16[256,768]{1,0:T(8,128)(2,1)S(1)}, u32[]{:S(2)}, u32[]{:S(2)}) collective-permute-start(bf16[256,768]{1,0:T(8,128)(2,1)S(1)} %get-tuple-element.236), channel_id=1, source_target_pairs={{1,0},{2,1},{3,2},{5,4},{6,5},{7,6},{9,8},{10,9},{11,10},{13,12},{... | collective-permute-start | bytes 1179656 | tf_op jit(solution)/shard_map/ppermute | solution.py:598
  14.9 30.2 %collective-permute-start = (bf16[256,768]{1,0:T(8,128)(2,1)S(1)}, bf16[256,768]{1,0:T(8,128)(2,1)S(1)}, u32[]{:S(2)}, u32[]{:S(2)}) collective-permute-start(bf16[256,768]{1,0:T(8,128)(2,1)S(1)} %get-tuple-element.237), channel_id=1, source_target_pairs={{0,1},{1,2},{2,3},{4,5},{5,6},{6,7},{8,9},{9,10},{10,11},{12,13},{... | collective-permute-start | bytes 1179656 | tf_op jit(solution)/shard_map/ppermute | solution.py:597
  23.1 16.8 %collective-permute-start.4 = (bf16[1,128,768]{2,1,0:T(8,128)(2,1)S(1)}, bf16[1,128,768]{2,1,0:T(8,128)(2,1)S(1)}, u32[]{:S(2)}, u32[]{:S(2)}) collective-permute-start(bf16[1,128,768]{2,1,0:T(8,128)(2,1)S(1)} %bitcast.256), channel_id=1, source_target_pairs={{0,2},{1,3},{2,0},{3,1},{4,6},{5,7},{6,4},{7,5},{8,10},{9,11},{10,... | collective-permute-start | bytes 589832 | tf_op jit(solution)/shard_map/ppermute | solution.py:592
  23.4 18.0 %collective-permute-start.7 = (bf16[3,40,768]{2,1,0:T(8,128)(2,1)S(1)}, bf16[3,40,768]{2,1,0:T(8,128)(2,1)S(1)}, u32[]{:S(2)}, u32[]{:S(2)}) collective-permute-start(bf16[3,40,768]{2,1,0:T(8,128)(2,1)S(1)} %get-tuple-element.260), channel_id=1, source_target_pairs={{0,16},{4,20},{8,24},{12,28},{16,0},{20,4},{24,8},{28,12},{1,17},{... | collective-permute-start | bytes 552968 | tf_op jit(solution)/shard_map/ppermute | solution.py:626
  71.0 35.5 %collective-permute-start.16 = (bf16[2,3,64,768]{3,2,1,0:T(8,128)(2,1)}, bf16[2,3,64,768]{3,2,1,0:T(8,128)(2,1)}, u32[]{:S(2)}, u32[]{:S(2)}) collective-permute-start(bf16[2,3,64,768]{3,2,1,0:T(8,128)(2,1)} %pad_maximum_fusion.7.refs_0_), channel_id=1, source_target_pairs={{0,16},{4,20},{8,24},{12,28},{16,0},{20,4},{24,8},{28,12},{1,17},{... | collective-permute-start | bytes 1769480 | tf_op jit(solution)/shard_map/ppermute | solution.py:626
  72.1 34.4 %collective-permute-start.17 = (bf16[2,3,64,768]{3,2,1,0:T(8,128)(2,1)}, bf16[2,3,64,768]{3,2,1,0:T(8,128)(2,1)}, u32[]{:S(2)}, u32[]{:S(2)}) collective-permute-start(bf16[2,3,64,768]{3,2,1,0:T(8,128)(2,1)} %pad_maximum_fusion.8.refs_2_), channel_id=1, source_target_pairs={{0,8},{4,12},{8,0},{12,4},{16,24},{20,28},{24,16},{28,20},{1,9},{5... | collective-permute-start | bytes 1769480 | tf_op jit(solution)/shard_map/ppermute | solution.py:626
  77.5 34.2 %collective-permute-start.14 = (bf16[1,96,768]{2,1,0:T(8,128)(2,1)}, bf16[1,96,768]{2,1,0:T(8,128)(2,1)S(1)}, u32[]{:S(2)}, u32[]{:S(2)}) collective-permute-start(bf16[1,96,768]{2,1,0:T(8,128)(2,1)} %bitcast.28), channel_id=1, source_target_pairs={{0,2},{1,3},{2,0},{3,1},{4,6},{5,7},{6,4},{7,5},{8,10},{9,11},{10,... | collective-permute-start | bytes 442376 | tf_op jit(solution)/shard_map/ppermute | solution.py:592
  109.8 35.6 %collective-permute-start.20 = (bf16[4,2,3,64,768]{4,3,2,1,0:T(8,128)(2,1)}, bf16[4,2,3,64,768]{4,3,2,1,0:T(8,128)(2,1)}, u32[]{:S(2)}, u32[]{:S(2)}) collective-permute-start(bf16[4,2,3,64,768]{4,3,2,1,0:T(8,128)(2,1)} %pad_maximum_fusion), channel_id=1, source_target_pairs={{0,4},{4,0},{8,12},{12,8},{16,20},{20,16},{24,28},{28,24},{1,5},{5... | collective-permute-start | bytes 7077896 | tf_op jit(solution)/shard_map/ppermute | solution.py:626
  143.4 19.0 %collective-permute-start.23 = (bf16[4,2,3,48,768]{4,3,2,1,0:T(8,128)(2,1)S(1)}, bf16[4,2,3,48,768]{4,3,2,1,0:T(8,128)(2,1)S(1)}, u32[]{:S(2)}, u32[]{:S(2)}) collective-permute-start(bf16[4,2,3,48,768]{4,3,2,1,0:T(8,128)(2,1)S(1)} %pad_maximum_fusion.1), channel_id=1, source_target_pairs={{0,4},{4,0},{8,12},{12,8},{16,20},{20,16},{24,28},{28,24},{1,5},{5... | collective-permute-start | bytes 5308424 | tf_op jit(solution)/shard_map/ppermute | solution.py:626
  239.9 33.3 %collective-permute-start.35 = (bf16[2,4,96,768]{3,2,1,0:T(8,128)(2,1)S(1)}, bf16[2,4,96,768]{3,2,1,0:T(8,128)(2,1)S(1)}, u32[]{:S(2)}, u32[]{:S(2)}) collective-permute-start(bf16[2,4,96,768]{3,2,1,0:T(8,128)(2,1)S(1)} %slice_bitcast_fusion.1), channel_id=1, source_target_pairs={{0,8},{4,12},{8,0},{12,4},{16,24},{20,28},{24,16},{28,20},{1,9},{5... | collective-permute-start | bytes 3538952 | tf_op jit(solution)/shard_map/ppermute | solution.py:626
  241.4 31.8 %collective-permute-start.34 = (bf16[2,4,96,768]{3,2,1,0:T(8,128)(2,1)S(1)}, bf16[2,4,96,768]{3,2,1,0:T(8,128)(2,1)S(1)}, u32[]{:S(2)}, u32[]{:S(2)}) collective-permute-start(bf16[2,4,96,768]{3,2,1,0:T(8,128)(2,1)S(1)} %bitcast.255), channel_id=1, source_target_pairs={{0,16},{4,20},{8,24},{12,28},{16,0},{20,4},{24,8},{28,12},{1,17},{... | collective-permute-start | bytes 3538952 | tf_op jit(solution)/shard_map/ppermute | solution.py:626
  246.3 30.7 %collective-permute-start.37 = (bf16[2,4,32,768]{3,2,1,0:T(8,128)(2,1)S(1)}, bf16[2,4,32,768]{3,2,1,0:T(8,128)(2,1)S(1)}, u32[]{:S(2)}, u32[]{:S(2)}) collective-permute-start(bf16[2,4,32,768]{3,2,1,0:T(8,128)(2,1)S(1)} %bitcast.258), channel_id=1, source_target_pairs={{0,16},{4,20},{8,24},{12,28},{16,0},{20,4},{24,8},{28,12},{1,17},{... | collective-permute-start | bytes 1179656 | tf_op jit(solution)/shard_map/ppermute | solution.py:626
  277.7 18.6 %collective-permute-start.38 = (bf16[4,96,768]{2,1,0:T(8,128)(2,1)S(1)}, bf16[4,96,768]{2,1,0:T(8,128)(2,1)S(1)}, u32[]{:S(2)}, u32[]{:S(2)}) collective-permute-start(bf16[4,96,768]{2,1,0:T(8,128)(2,1)S(1)} %get-tuple-element.232), channel_id=1, source_target_pairs={{0,8},{4,12},{8,0},{12,4},{16,24},{20,28},{24,16},{28,20},{1,9},{5... | collective-permute-start | bytes 1769480 | tf_op jit(solution)/shard_map/ppermute | solution.py:626
  278.0 18.3 %collective-permute-start.39 = (bf16[4,96,768]{2,1,0:T(8,128)(2,1)S(1)}, bf16[4,96,768]{2,1,0:T(8,128)(2,1)S(1)}, u32[]{:S(2)}, u32[]{:S(2)}) collective-permute-start(bf16[4,96,768]{2,1,0:T(8,128)(2,1)S(1)} %get-tuple-element.230), channel_id=1, source_target_pairs={{0,16},{4,20},{8,24},{12,28},{16,0},{20,4},{24,8},{28,12},{1,17},{... | collective-permute-start | bytes 1769480 | tf_op jit(solution)/shard_map/ppermute | solution.py:626
  278.7 17.7 %collective-permute-start.40 = (bf16[4,32,768]{2,1,0:T(8,128)(2,1)S(1)}, bf16[4,32,768]{2,1,0:T(8,128)(2,1)S(1)}, u32[]{:S(2)}, u32[]{:S(2)}) collective-permute-start(bf16[4,32,768]{2,1,0:T(8,128)(2,1)S(1)} %get-tuple-element.252), channel_id=1, source_target_pairs={{0,8},{4,12},{8,0},{12,4},{16,24},{20,28},{24,16},{28,20},{1,9},{5... | collective-permute-start | bytes 589832 | tf_op jit(solution)/shard_map/ppermute | solution.py:626
  296.9 16.4 %collective-permute-start.41 = (bf16[2,224,768]{2,1,0:T(8,128)(2,1)S(1)}, bf16[2,224,768]{2,1,0:T(8,128)(2,1)S(1)}, u32[]{:S(2)}, u32[]{:S(2)}) collective-permute-start(bf16[2,224,768]{2,1,0:T(8,128)(2,1)S(1)} %pad_maximum_fusion.5), channel_id=1, source_target_pairs={{0,1},{1,0},{2,3},{3,2},{4,5},{5,4},{6,7},{7,6},{8,9},{9,8},{10,11... | collective-permute-start | bytes 2064392 | tf_op jit(solution)/shard_map/ppermute | solution.py:592
  319.0 20.2 %collective-permute-start.42 = (bf16[16,80,768]{2,1,0:T(8,128)(2,1)S(1)}, bf16[16,80,768]{2,1,0:T(8,128)(2,1)S(1)}, u32[]{:S(2)}, u32[]{:S(2)}) collective-permute-start(bf16[16,80,768]{2,1,0:T(8,128)(2,1)S(1)} %get-tuple-element.188), channel_id=1, source_target_pairs={{0,4},{4,0},{8,12},{12,8},{16,20},{20,16},{24,28},{28,24},{1,5},{5... | collective-permute-start | bytes 5898248 | tf_op jit(solution)/shard_map/ppermute | solution.py:626
  321.2 17.9 %collective-permute-start.55 = (bf16[224,768]{1,0:T(8,128)(2,1)S(1)}, bf16[224,768]{1,0:T(8,128)(2,1)S(1)}, u32[]{:S(2)}, u32[]{:S(2)}) collective-permute-start(bf16[224,768]{1,0:T(8,128)(2,1)S(1)} %get-tuple-element.224), channel_id=1, source_target_pairs={{0,2},{1,3},{2,0},{3,1},{4,6},{5,7},{6,4},{7,5},{8,10},{9,11},{10,... | collective-permute-start | bytes 1032200 | tf_op jit(solution)/shard_map/ppermute | solution.py:592
  339.9 15.9 %collective-permute-start.43 = (bf16[2,2,80,768]{3,2,1,0:T(8,128)(2,1)S(1)}, bf16[2,2,80,768]{3,2,1,0:T(8,128)(2,1)S(1)}, u32[]{:S(2)}, u32[]{:S(2)}) collective-permute-start(bf16[2,2,80,768]{3,2,1,0:T(8,128)(2,1)S(1)} %slice_bitcast_fusion.8), channel_id=1, source_target_pairs={{0,16},{4,20},{8,24},{12,28},{16,0},{20,4},{24,8},{28,12},{1,17},{... | collective-permute-start | bytes 1474568 | tf_op jit(solution)/shard_map/ppermute | solution.py:626
  341.5 14.3 %collective-permute-start.46 = (bf16[2,2,80,768]{3,2,1,0:T(8,128)(2,1)S(1)}, bf16[2,2,80,768]{3,2,1,0:T(8,128)(2,1)S(1)}, u32[]{:S(2)}, u32[]{:S(2)}) collective-permute-start(bf16[2,2,80,768]{3,2,1,0:T(8,128)(2,1)S(1)} %slice_bitcast_fusion.6), channel_id=1, source_target_pairs={{0,8},{4,12},{8,0},{12,4},{16,24},{20,28},{24,16},{28,20},{1,9},{5... | collective-permute-start | bytes 1474568 | tf_op jit(solution)/shard_map/ppermute | solution.py:626
  343.7 13.8 %collective-permute-start.56 = (bf16[1,112,768]{2,1,0:T(8,128)(2,1)S(1)}, bf16[1,112,768]{2,1,0:T(8,128)(2,1)S(1)}, u32[]{:S(2)}, u32[]{:S(2)}) collective-permute-start(bf16[1,112,768]{2,1,0:T(8,128)(2,1)S(1)} %get-tuple-element.265), channel_id=1, source_target_pairs={{0,8},{4,12},{8,0},{12,4},{16,24},{20,28},{24,16},{28,20},{1,9},{5... | collective-permute-start | bytes 516104 | tf_op jit(solution)/shard_map/ppermute | solution.py:626
  357.5 15.4 %collective-permute-start.58 = (bf16[2,1,112,768]{3,2,1,0:T(8,128)(2,1)S(1)}, bf16[2,1,112,768]{3,2,1,0:T(8,128)(2,1)S(1)}, u32[]{:S(2)}, u32[]{:S(2)}) collective-permute-start(bf16[2,1,112,768]{3,2,1,0:T(8,128)(2,1)S(1)} %pad_maximum_fusion.17.refs_0_), channel_id=1, source_target_pairs={{0,16},{4,20},{8,24},{12,28},{16,0},{20,4},{24,8},{28,12},{1,17},{... | collective-permute-start | bytes 1032200 | tf_op jit(solution)/shard_map/ppermute | solution.py:626
  357.7 15.3 %collective-permute-start.59 = (bf16[2,1,112,768]{3,2,0,1:T(8,128)(2,1)S(1)}, bf16[2,1,112,768]{3,2,0,1:T(8,128)(2,1)S(1)}, u32[]{:S(2)}, u32[]{:S(2)}) collective-permute-start(bf16[2,1,112,768]{3,2,0,1:T(8,128)(2,1)S(1)} %pad_maximum_fusion.18), channel_id=1, source_target_pairs={{0,8},{4,12},{8,0},{12,4},{16,24},{20,28},{24,16},{28,20},{1,9},{5... | collective-permute-start | bytes 1032200 | tf_op jit(solution)/shard_map/ppermute | solution.py:626
  377.6 19.1 %collective-permute-start.60 = (bf16[4,2,1,112,768]{4,3,2,1,0:T(8,128)(2,1)S(1)}, bf16[4,2,1,112,768]{4,3,2,1,0:T(8,128)(2,1)S(1)}, u32[]{:S(2)}, u32[]{:S(2)}) collective-permute-start(bf16[4,2,1,112,768]{4,3,2,1,0:T(8,128)(2,1)S(1)} %pad_maximum_fusion.4), channel_id=1, source_target_pairs={{0,4},{4,0},{8,12},{12,8},{16,20},{20,16},{24,28},{28,24},{1,5},{5... | collective-permute-start | bytes 4128776 | tf_op jit(solution)/shard_map/ppermute | solution.py:626
  (115 other events, 830.3 us)
